TPU v7x, 256 devices: a whole 4x4x8 slice. The times are simulated.
256 devices in a mesh: mesh: 16 (over x, y_lo, core), snap: 16 (over z, y_hi).
Axes of the slice: x: 4, y: 4 (y_hi: 2, y_lo: 2; y = y_hi * 2 + y_lo), z: 8, core: 2. Of those that a mesh axis runs over, the one named last changes fastest.
Arguments:
- snapshots: float32 [1024, 98304], P('snap', 'mesh'), may hold values from -40 to 40, as said below
- connectivity: int32 [3, 196608], P(None, 'mesh'), may hold values from 0 to 6143, as said below
- element_mass: float32 [196608], P('mesh'), may hold values from 0.3 to 3
- lower_shared: int32 [8192], P('mesh'), may hold values from 0 to 6143, as said below
- upper_shared: int32 [8192], P('mesh'), may hold values from 0 to 6143, as said below
Outputs:
- mass_weighted: float32 [1024, 98304], P('snap', 'mesh')
- gram: float32 [1024, 1024], P('snap', 'mesh')
Inputs may be any that keep to these rules, and one draw needn't show every extreme that they name: `connectivity`: entries are local slot indices of the element's partition; the three corners of an element differ, and every slot is a corner of some element. `lower_shared`: entry p * 512 + k is a local slot of partition p; a partition's lower and upper lists are disjoint and hold no repeats; slot lower_shared[p, k] of partition p is the same node as slot upper_shared[p - 1, k] of partition p - 1, and snapshots agree there. The lower list of partition 0 has no partner. `upper_shared`: entry p * 512 + k is a local slot of partition p, disjoint from its lower list; the upper list of the last partition has no partner. `snapshots`: values at the two slots of a shared node are equal.
All inputs are finite; a program needn't handle non-finite values.
Results may differ from a plain program's by a relative error of at most 0.0001.
Values sent between devices are 32-bit elements; how exact they have to be, the bound alone decides.
No kernel may reach another device: no remote copies, remote signals or barrier semaphores. Data moves between devices by JAX's collectives and lax.ppermute only.
A program may use at most 128 MiB of HBM per device.

v0:
```python
import jax
import jax.numpy as jnp
from jax import lax
from jax.sharding import PartitionSpec as P


def passed_along(value, axis, steps):
    count = lax.axis_size(axis)
    leading, last = (max(0, -steps), min(count, count - steps))
    return lax.ppermute(value, axis, [(source, source + steps) for source in range(leading, last)])


def partial_apply(snapshots, corners, masses):
    values = snapshots[:, corners]
    summed = jnp.sum(values, axis=1, keepdims=True)
    contrib = masses / 12.0 * (values + summed)
    blank = jnp.zeros_like(snapshots)
    return blank.at[:, corners.reshape(-1)].add(contrib.reshape(snapshots.shape[0], -1))


def inner_rows(left_rows, right_rows):
    return lax.dot_general(
        left_rows,
        right_rows,
        (((1,), (1,)), ((), ())),
        precision=lax.Precision.HIGHEST,
        preferred_element_type=jnp.float32,
    )


def on_device(snapshots, connectivity, element_mass, lower_shared, upper_shared):
    position = lax.axis_index("mesh")
    part_count = lax.axis_size("mesh")
    partials = partial_apply(snapshots, connectivity, element_mass)
    from_below = passed_along(partials[:, upper_shared], "mesh", 1)
    from_above = passed_along(partials[:, lower_shared], "mesh", -1)
    weighted = partials.at[:, lower_shared].add(from_below).at[:, upper_shared].add(from_above)
    flag = jnp.where(position > 0, 0.0, 1.0).astype(jnp.float32)
    owned_mask = jnp.ones((snapshots.shape[1],), jnp.float32).at[lower_shared].set(flag)
    owned_rows = weighted * owned_mask[None, :]
    gram_tile = inner_rows(snapshots, lax.all_gather(owned_rows, "snap", axis=0, tiled=True))
    columns = gram_tile.shape[1] // part_count
    summed_rows = lax.psum(gram_tile, "mesh")
    gram_share = lax.dynamic_slice_in_dim(summed_rows, position * columns, columns, 1)
    gram = gram_share / float(part_count * snapshots.shape[1])
    return (weighted, gram)


def solution(mesh):
    placed = (P("snap", "mesh"), P(None, "mesh"), P("mesh"), P("mesh"), P("mesh"))
    return jax.shard_map(
        on_device,
        mesh=mesh,
        in_specs=placed,
        out_specs=(P("snap", "mesh"), P("snap", "mesh")),
        check_vma=False,
    )
```

profile of v0, /device:TPU:1, one launch (start us, length us, event | category | flops | bytes accessed | tf_op | source)
XLA Modules:
  0.0 861.3 jit_solution(5876554764011859223)
XLA Ops:
  7.2 0.0 all-gather.2.cloned.1.call-start
  7.2 2.1 copy.12
  9.4 0.7 compare_select_fusion.1
  10.1 1.7 reshape.46
  11.8 0.9 broadcast_clamp_fusion
  12.7 121.6 %gather_fusion = f32[36864,64]{1,0:T(8,128)} fusion(f32[64,6144]{0,1:T(8,128)S(1)} %copy.12, s32[36864]{0:T(1024)S(1)} %broadcast_clamp_fusion), kind=kCustom, calls=%fused_computation | custom fusion | bytes 19021824 | tf_op jit(solution)/shard_map/gather | solution.py:14
  134.3 13.4 %reduce_sum.9 = f32[64,12288]{0,1:T(8,128)} reduce(f32[64,3,12288]{0,2,1:T(8,128)} %bitcast.25, f32[]{:T(128)} %constant.10.clone.1), dimensions={1}, to_apply=%region_0.0 | reduce | flops 1572864 | bytes 12582916 | tf_op jit(solution)/shard_map/reduce_sum | solution.py:15
  147.8 16.1 %broadcast_add_fusion = f32[64,3,12288]{0,2,1:T(8,128)} fusion(f32[64,3,12288]{0,2,1:T(8,128)} %bitcast.26, f32[64,12288]{0,1:T(8,128)} %reduce_sum.9), kind=kLoop, calls=%fused_computation.10 | loop fusion | flops 2359296 | bytes 22020096 | tf_op jit(solution)/shard_map/add | solution.py:16
  163.9 0.1 mul.25
  164.1 0.2 copy.15
  164.2 0.2 compare_select_fusion
  164.4 0.0 copy-done.3
  164.4 13.4 %bitcast_multiply_fusion = f32[64,36864]{0,1:T(8,128)} fusion(f32[64,3,12288]{0,2,1:T(8,128)} %broadcast_add_fusion, f32[36864]{0:T(1024)S(1)} %mul.25), kind=kLoop, calls=%fused_computation.9 | loop fusion | flops 2359296 | bytes 19021824 | tf_op jit(solution)/shard_map/mul | solution.py:16
  177.8 178.9 %scatter_custom_fusion = f32[64,6144]{0,1:T(8,128)S(1)} fusion(s32[36864]{0:T(1024)S(1)} %bitcast.29, f32[64,36864]{0,1:T(8,128)} %bitcast_multiply_fusion, f32[]{:T(128)} %constant.10.clone.1), kind=kCustom, calls=%fused_computation.7 | custom fusion | flops 2359296 | bytes 11010052 | tf_op jit(solution)/shard_map/scatter-add | solution.py:18
  356.7 1.6 gather_fusion.1
  358.4 4.6 collective-permute-start
  363.0 1.6 gather_fusion.2
  364.6 1.9 collective-permute-start.1
  366.6 2.5 scatter_custom_fusion.3
  369.1 0.0 collective-permute-done
  369.1 4.5 scatter_custom_fusion.1
  373.5 0.0 collective-permute-done.1
  373.5 5.0 scatter_custom_fusion.2
  378.6 2.0 copy.14
  380.6 2.9 broadcast_multiply_fusion
  383.5 0.0 all-gather.2.cloned.1.call-update
  383.5 0.0 all-reduce.2.cloned.1.call-start
  383.5 322.5 %all-gather.2.cloned.1.call-done = f32[1024,6144]{1,0:T(8,128)} async-done(((f32[64,6144]{1,0:T(8,128)}), f32[1024,6144]{1,0:T(8,128)}) %all-gather.2.cloned.1.call-update) | async-done | bytes 25165840 | tf_op jit(solution)/shard_map/all_gather | solution.py:41
  706.1 28.2 %convolution_bitcast_fusion = f32[64,1024]{1,0:T(8,128)} fusion(f32[1024,6144]{1,0:T(8,128)} %all-gather.2.cloned.1.call-done, f32[64,6144]{1,0:T(8,128)S(1)} %copy-done), kind=kOutput, calls=%fused_computation.12 | convolution fusion | flops 4831838208 | bytes 27000832 | tf_op jit(solution)/shard_map/dot_general | solution.py:22
  734.2 0.0 all-reduce.2.cloned.1.call-update
  734.3 118.7 %all-reduce.2.cloned.1.call-done = f32[64,1024]{1,0:T(8,128)} async-done(((f32[64,1024]{1,0:T(8,128)}), f32[64,1024]{1,0:T(8,128)}) %all-reduce.2.cloned.1.call-update) | async-done | bytes 262160 | tf_op jit(solution)/shard_map/psum | solution.py:43
  853.0 1.4 dynamic-slice_multiply_fusion
  (16 shorter events, 0.1 us)
Async XLA Ops:
  7.2 2.2 copy-start.1
  7.2 698.9 %all-gather.2.cloned.1.call-start = ((), (), s32[]{:S(2)}) async-start(), calls=%async_computation | async-start | bytes 26738688 | tf_op jit(solution)/shard_map/all_gather | solution.py:41
  147.8 16.1 %copy-start.2 = (f32[12288]{0:T(1024)S(1)}, f32[12288]{0:T(1024)}, u32[]{:S(2)}) copy-start(f32[12288]{0:T(1024)} %param.7) | copy-start | bytes 147460
  147.8 16.6 %copy-start.3 = (s32[512]{0:T(512)S(1)}, s32[512]{0:T(512)}, u32[]{:S(2)}) copy-start(s32[512]{0:T(512)} %param.9) | copy-start | bytes 6148
  177.8 185.1 %copy-start.4 = (s32[512]{0:T(512)S(1)}, s32[512]{0:T(512)}, u32[]{:S(2)}) copy-start(s32[512]{0:T(512)} %param.8) | copy-start | bytes 6148
  358.4 10.7 %collective-permute-start = (f32[64,512]{0,1:T(8,128)}, f32[64,512]{0,1:T(8,128)S(1)}, u32[]{:S(2)}, u32[]{:S(2)}) collective-permute-start(f32[64,512]{0,1:T(8,128)} %bitcast.30), channel_id=1, source_target_pairs={{0,16},{16,32},{32,48},{48,64},{64,80},{80,96},{96,112},{112,128},... | collective-permute-start | bytes 393224 | tf_op jit(solution)/shard_map/ppermute | solution.py:10
  364.6 8.9 %collective-permute-start.1 = (f32[64,512]{0,1:T(8,128)}, f32[64,512]{0,1:T(8,128)}, u32[]{:S(2)}, u32[]{:S(2)}) collective-permute-start(f32[64,512]{0,1:T(8,128)} %bitcast.31), channel_id=1, source_target_pairs={{16,0},{32,16},{48,32},{64,48},{80,64},{96,80},{112,96},{128,112},... | collective-permute-start | bytes 393224 | tf_op jit(solution)/shard_map/ppermute | solution.py:10
  380.6 325.5 %copy-start = (f32[64,6144]{1,0:T(8,128)S(1)}, f32[64,6144]{1,0:T(8,128)}, u32[]{:S(2)}) copy-start(f32[64,6144]{1,0:T(8,128)} %param.5) | copy-start | bytes 4718596
  383.5 469.5 %all-reduce.2.cloned.1.call-start = ((), (), s32[]{:S(2)}) async-start(), calls=%async_computation.1 | async-start | bytes 524288 | tf_op jit(solution)/shard_map/psum | solution.py:43
Sparse Core Ops, SparseCore 0:
  383.6 322.3 all-gather.1
  734.4 118.5 all-reduce.1
where the time goes:
time: 862 us; the launch traced here: 861 us
  waiting for transfers between devices  441 us (51%)
  other arithmetic  237 us (27%)
  local copies, waits for them, and re-layouts  134 us (16%)
  matrix products  28.2 us (3%)
  between operations  14.2 us (2%)
    all_gather x1, waiting for transfers between devices, on_device(): lax.all_gather(owned_rows, 'snap', axis=0, tiled=True)  323 us
    scatter-add x1, other arithmetic, partial_apply(): blank.at[:, corners.reshape(-1)]  179 us
    gather x1, local copies, waits for them, and re-layouts, partial_apply(): values = snapshots[:, corners]  122 us
    psum x1, waiting for transfers between devices, on_device(): summed_rows = lax.psum(gram_tile, 'mesh')  119 us
    dot_general x1, matrix products, inner_rows(): lax.dot_general(left_rows, right_rows, (((1,), (1,)), ((), ())), precisio...  28.2 us
  transfers between devices with their start and end apart: 4, of which 2 were waited for; matrix products, arithmetic and copies ran while one was open for 1% of the time, Pallas kernels for 0%

commit v1 on v0

v1 whole, which is shorter than its diff:
```python
import functools

import jax
import jax.numpy as jnp
from jax import lax
from jax.experimental import pallas as pl
from jax.experimental.pallas import tpu as pltpu
from jax.sharding import PartitionSpec as P

LANES = 128
MIB = 2 ** 20


def ring_hop(value, steps, cross=False, closing=False):
    parts, blocks = lax.axis_size("mesh"), lax.axis_size("snap")
    rings = blocks // 2
    pairs = []
    for part in range(parts):
        way = 1 if part % 2 == 0 else -1
        for block in range(blocks):
            z, h = block // 2, block % 2
            target = (z + way * steps) % rings
            if closing and (target < rings // 2) != (part % 2 == 0):
                continue
            pairs.append((part * blocks + block, part * blocks + 2 * target + (h ^ 1 if cross else h)))
    return lax.ppermute(value, ("mesh", "snap"), pairs)


def passed_along(value, axis, steps):
    count = lax.axis_size(axis)
    leading, last = (max(0, -steps), min(count, count - steps))
    return lax.ppermute(value, axis, [(source, source + steps) for source in range(leading, last)])


def partner(value):
    return lax.ppermute(value, "snap", [(i, i ^ 1) for i in range(lax.axis_size("snap"))])


def mirrored(value, cross):
    count = lax.axis_size("snap")
    flip = 1 if cross else 0
    return lax.ppermute(value, ("mesh", "snap"),
                        [(s * count + (m ^ flip), m * count + s) for m in range(count) for s in range(count)])


def apply_kernel(first, start, count, banks, *refs):
    if first:
        (a_hbm, b_hbm, c_hbm, m_hbm, x_ref, rows_out, a_s, b_s, c_s, m_s, sems, xt, *ys) = refs
        sources = (a_hbm, b_hbm, c_hbm, m_hbm)
    else:
        (a_hbm, b_hbm, c_hbm, m_hbm, low_s, up_s, x_ref, rows_in, y_out, rows_out, low_out, up_out,
         a_s, b_s, c_s, m_s, sems, xt, *ys) = refs
        sources = (a_hbm, b_hbm, c_hbm, m_hbm)
    snaps, nodes = x_ref.shape
    copies = []
    for j, (source, target) in enumerate(zip(sources, (a_s, b_s, c_s, m_s))):
        copy = pltpu.make_async_copy(source.at[pl.ds(start, count)], target, sems.at[j])
        copy.start()
        copies.append(copy)

    def prepare(i, carry):
        at = pl.multiple_of(i * LANES, LANES)
        xt[pl.ds(at, LANES), 0:snaps] = x_ref[:, pl.ds(at, LANES)].T
        for y in ys:
            y[pl.ds(at, LANES), :] = jnp.zeros((LANES, LANES), jnp.float32)
        return carry

    lax.fori_loop(0, nodes // LANES, prepare, 0)
    for copy in copies:
        copy.wait()

    def elements(group, carry):
        base = group * banks
        corners = [(a_s[base + k], b_s[base + k], c_s[base + k]) for k in range(banks)]
        updated = []
        for k in range(banks):
            values = [xt[pl.ds(n, 1), :] for n in corners[k]]
            held = [ys[k][pl.ds(n, 1), :] for n in corners[k]]
            total = values[0] + values[1] + values[2]
            mass = m_s[base + k]
            updated.append([h + mass * (v + total) for h, v in zip(held, values)])
        for k in range(banks):
            for n, new in zip(corners[k], updated[k]):
                ys[k][pl.ds(n, 1), :] = new
        return carry

    lax.fori_loop(0, count // banks, elements, 0)

    def finish(i, carry):
        at = pl.multiple_of(i * LANES, LANES)
        total = ys[0][pl.ds(at, LANES), :]
        for y in ys[1:]:
            total = total + y[pl.ds(at, LANES), :]
        if first:
            rows_out[pl.ds(at, LANES), :] = total
        else:
            total = (total + rows_in[pl.ds(at, LANES), :]) * (1.0 / 12.0)
            rows_out[pl.ds(at, LANES), :] = total
            y_out[:, pl.ds(at, LANES)] = total.T[0:snaps, :]
        return carry

    lax.fori_loop(0, nodes // LANES, finish, 0)
    if first:
        return
    for list_s, out in ((low_s, low_out), (up_s, up_out)):
        def gather(i, carry, list_s=list_s):
            at = pl.multiple_of(i * 8, 8)
            for k in range(8):
                xt[pl.ds(at + k, 1), :] = rows_out[pl.ds(list_s[at + k], 1), :]
            return carry

        shared = out.shape[1]
        lax.fori_loop(0, shared // 8, gather, 0)
        for block in range(shared // LANES):
            at = block * LANES
            out[:, at:at + LANES] = xt[at:at + LANES, :].T[0:snaps, :]


def assemble_kernel(low_s, up_s, rows_ref, below_ref, above_ref, out_ref, rows, taken):
    snaps, shared = below_ref.shape
    nodes = rows_ref.shape[0]

    def copy(i, carry):
        at = pl.multiple_of(i * LANES, LANES)
        rows[pl.ds(at, LANES), :] = rows_ref[pl.ds(at, LANES), :]
        return carry

    lax.fori_loop(0, nodes // LANES, copy, 0)
    for list_s, received in ((low_s, below_ref), (up_s, above_ref)):
        for block in range(shared // LANES):
            at = block * LANES
            taken[at:at + LANES, 0:snaps] = received[:, at:at + LANES].T

        def add(i, carry, list_s=list_s):
            at = pl.multiple_of(i * 8, 8)
            nodes_of = [list_s[at + k] for k in range(8)]
            new = [rows[pl.ds(n, 1), :] + taken[pl.ds(at + k, 1), :] for k, n in enumerate(nodes_of)]
            for n, value in zip(nodes_of, new):
                rows[pl.ds(n, 1), :] = value
            return carry

        lax.fori_loop(0, shared // 8, add, 0)

    def write(i, carry):
        at = pl.multiple_of(i * LANES, LANES)
        out_ref[:, pl.ds(at, LANES)] = rows[pl.ds(at, LANES), :].T[0:snaps, :]
        return carry

    lax.fori_loop(0, nodes // LANES, write, 0)


ANYWHERE = pl.BlockSpec(memory_space=pl.ANY)
IN_VMEM = pl.BlockSpec(memory_space=pltpu.VMEM)
IN_SMEM = pl.BlockSpec(memory_space=pltpu.SMEM)


def cost(micros):
    return pl.CostEstimate(flops=int(micros * 1e9), bytes_accessed=int(micros * 3e6), transcendentals=0)


def apply_call(first, start, count, banks, operands, snaps, nodes, shared):
    rows = jax.ShapeDtypeStruct((nodes, LANES), jnp.float32)
    side = jax.ShapeDtypeStruct((snaps, shared), jnp.float32)
    whole = jax.ShapeDtypeStruct((snaps, nodes), jnp.float32)
    return pl.pallas_call(
        functools.partial(apply_kernel, first, start, count, banks),
        out_shape=[rows] if first else [whole, rows, side, side],
        in_specs=[ANYWHERE] * 4 + ([IN_VMEM] if first else [IN_SMEM] * 2 + [IN_VMEM] * 2),
        out_specs=[IN_VMEM] if first else [IN_VMEM] * 4,
        scratch_shapes=[pltpu.SMEM((count,), jnp.int32)] * 3
        + [pltpu.SMEM((count,), jnp.float32), pltpu.SemaphoreType.DMA((4,))]
        + [pltpu.VMEM((nodes, LANES), jnp.float32)] * (banks + 1),
        compiler_params=pltpu.CompilerParams(vmem_limit_bytes=56 * MIB),
        cost_estimate=cost(30),
    )(*operands)


def split3(left, right):
    dims = (((1,), (1,)), ((), ()))
    dot = functools.partial(lax.dot_general, dimension_numbers=dims, preferred_element_type=jnp.float32)
    (l_hi, l_lo), (r_hi, r_lo) = left, right
    return dot(l_hi, r_hi) + (dot(l_hi, r_lo) + dot(l_lo, r_hi))


def halves_of(value):
    high = value.astype(jnp.bfloat16)
    return high, (value - high.astype(jnp.float32)).astype(jnp.bfloat16)


def gram_kernel(place, ya_ref, yb_ref, *refs):
    *blocks, out_ref = refs
    snaps = ya_ref.shape[0]
    rings = out_ref.shape[0] // 2
    z, h, way = place[0], place[1], place[2]

    @pl.when(pl.program_id(0) == 0)
    def _():
        out_ref[...] = jnp.zeros_like(out_ref)

    y = halves_of(jnp.concatenate([ya_ref[...], yb_ref[...]], axis=0))
    for distance, (a, b) in enumerate(zip(blocks[0::2], blocks[1::2])):
        value = split3(halves_of(jnp.concatenate([a[...], b[...]], axis=0)), y)
        if distance == 0:
            value = 0.5 * value
        at = lax.rem(z - way * distance + rings, rings)
        out_ref[2 * at + h] += value[0:snaps]
        out_ref[2 * at + (1 - h)] += value[snaps:2 * snaps]


def gram_call(place, ya, yb, blocks, rings):
    snaps, nodes = ya.shape
    chunk = nodes // 4
    piece = pl.BlockSpec((snaps, chunk), lambda i: (0, i))
    return pl.pallas_call(
        gram_kernel,
        grid=(nodes // chunk,),
        out_shape=jax.ShapeDtypeStruct((2 * rings, snaps, 2 * snaps), jnp.float32),
        in_specs=[IN_SMEM] + [piece] * (2 + len(blocks)),
        out_specs=pl.BlockSpec((2 * rings, snaps, 2 * snaps), lambda i: (0, 0, 0)),
        compiler_params=pltpu.CompilerParams(vmem_limit_bytes=40 * MIB),
        cost_estimate=cost(8),
    )(place, ya, yb, *blocks)


def on_device(snapshots, connectivity, element_mass, lower_shared, upper_shared):
    snaps, nodes = snapshots.shape
    elements = element_mass.shape[0]
    shared = lower_shared.shape[0]
    position = lax.axis_index("mesh")
    block = lax.axis_index("snap")
    rings = lax.axis_size("snap") // 2
    z, h = block // 2, block % 2
    half = nodes // 2

    own = lax.dynamic_slice_in_dim(snapshots, h * half, half, 1)
    given = lax.dynamic_slice_in_dim(snapshots, (1 - h) * half, half, 1)
    a1 = ring_hop(own, 1)
    b1 = ring_hop(given, 1, cross=True)
    a2 = ring_hop(own, 2)

    columns = tuple(connectivity[k] for k in range(3)) + (element_mass,)
    (rows,) = apply_call(True, 0, elements // 2, 8, columns + (snapshots,), snaps, nodes, shared)

    rows, b1, a2 = lax.optimization_barrier((rows, b1, a2))
    b2 = ring_hop(b1, 1)
    a3 = ring_hop(a2, 1)
    b3 = ring_hop(b1, 2)
    b0 = partner(given)

    partial, rows, low, high = apply_call(
        False, elements // 2, elements // 2, 8, columns + (lower_shared, upper_shared, snapshots, rows),
        snaps, nodes, shared)

    partial, a3, b3 = lax.optimization_barrier((partial, a3, b3))
    y_own = lax.dynamic_slice_in_dim(partial, h * half, half, 1)
    y_given = lax.dynamic_slice_in_dim(partial, (1 - h) * half, half, 1)
    y_theirs = partner(y_given)
    a4 = ring_hop(a3, 1, closing=True)
    b4 = ring_hop(b3, 1, closing=True)

    from_below = passed_along(high, "mesh", 1)
    from_above = passed_along(low, "mesh", -1)
    weighted = pl.pallas_call(
        assemble_kernel,
        out_shape=jax.ShapeDtypeStruct((snaps, nodes), jnp.float32),
        in_specs=[IN_SMEM] * 2 + [IN_VMEM] * 3,
        out_specs=IN_VMEM,
        scratch_shapes=[pltpu.VMEM((nodes, LANES), jnp.float32), pltpu.VMEM((shared, LANES), jnp.float32)],
        compiler_params=pltpu.CompilerParams(vmem_limit_bytes=20 * MIB),
        cost_estimate=cost(6),
    )(lower_shared, upper_shared, rows, from_below, from_above)
    weighted, y_theirs = lax.optimization_barrier((weighted, y_theirs))

    place = jnp.stack([z, h, jnp.where(position % 2 == 0, 1, -1)]).astype(jnp.int32)
    tiles = gram_call(place, y_own, y_theirs, [own, b0, a1, b1, a2, b2, a3, b3, a4, b4], rings)
    tile = jnp.sum(lax.all_to_all(tiles, "mesh", 0, 0, tiled=True), axis=0)
    mine, others = tile[:, :snaps], tile[:, snaps:]
    total = (mine + partner(others)).T + (mirrored(mine, False) + mirrored(others, True))
    return weighted, total * (1.0 / float(lax.axis_size("mesh") * nodes))


def solution(mesh):
    placed = (P("snap", "mesh"), P(None, "mesh"), P("mesh"), P("mesh"), P("mesh"))
    return jax.shard_map(
        on_device,
        mesh=mesh,
        in_specs=placed,
        out_specs=(P("snap", "mesh"), P("snap", "mesh")),
        check_vma=False,
    )
```

time: 862 us -> 184 us (0.21)
  the two profiles are of different devices: /device:TPU:1 before, /device:TPU:20 now
where the time goes in v1:
time: 184 us
  Pallas kernels  90 us (49%)
  starting transfers between devices  40.2 us (22%)
  waiting for transfers between devices  29.7 us (16%)
  blocking collectives  14.8 us (8%)
  local copies, waits for them, and re-layouts  7.7 us (4%)
    pallas_call x2, Pallas kernels, apply_call(): pl.pallas_call(functools.partial(apply_kernel, first, start, count, banks...  76 us
    ppermute x8, starting transfers between devices, ring_hop(): return lax.ppermute(value, ('mesh', 'snap'), pairs)  16.9 us
    all_to_all x1, blocking collectives, on_device(): tile = jnp.sum(lax.all_to_all(tiles, 'mesh', 0, 0, tiled=True), axis=0)  14.8 us
    ppermute x2, starting transfers between devices, mirrored(): lax.ppermute(value, ('mesh', 'snap'), [(s * count + (m ^ flip), m * count...  11.7 us
    ppermute x8, waiting for transfers between devices, ring_hop(): return lax.ppermute(value, ('mesh', 'snap'), pairs)  10.4 us
    ppermute x3, waiting for transfers between devices, partner(): lax.ppermute(value, 'snap', [(i, i ^ 1) for i in range(lax.axis_size('sna...  9.32 us
    ppermute x2, waiting for transfers between devices, mirrored(): lax.ppermute(value, ('mesh', 'snap'), [(s * count + (m ^ flip), m * count...  9.28 us
    pallas_call x1, Pallas kernels, on_device(): pl.pallas_call(assemble_kernel, out_shape=jax.ShapeDtypeStruct((snaps, no...  8.04 us
  transfers between devices with their start and end apart: 15, of which 6 were waited for; matrix products, arithmetic and copies ran while one was open for 0% of the time, Pallas kernels for 46%

profile of v1, /device:TPU:20, one launch (start us, length us, event | category | flops | bytes accessed | tf_op | source)
XLA Modules:
  0.0 184.0 jit_solution(6497574676338331834)
XLA Ops:
  0.7 2.4 %constant_dynamic-slice_fusion.2 = (f32[64,3072]{1,0:T(8,128)S(1)}, f32[64,3072]{1,0:T(8,128)}) fusion(f32[64,6144]{1,0:T(8,128)} %refs_6_.1, s32[]{:T(128)S(6)} %select_n.29, s32[]{:T(128)S(6)} %select_n.28), kind=kLoop, calls=%fused_computation.4 | loop fusion | bytes 3145736 | tf_op jit(solution)/shard_map/dynamic_slice | solution.py:235
  3.1 1.7 collective-permute-start
  4.8 3.3 %collective-permute-start.1 = (f32[64,3072]{1,0:T(8,128)S(1)}, f32[64,3072]{1,0:T(8,128)S(1)}, u32[]{:S(2)}, u32[]{:S(2)}) collective-permute-start(f32[64,3072]{1,0:T(8,128)S(1)} %get-tuple-element.28.refs_0_), channel_id=1, source_target_pairs={{0,4},{1,5},{2,6},{3,7},{4,8},{5,9},{6,10},{7,11},{8,12},{9,13},{1... | collective-permute-start | bytes 2359304 | tf_op jit(solution)/shard_map/ppermute | solution.py:26
  8.1 0.8 fusion
  8.8 34.9 %shard_map.68.refs_7_ = f32[6144,128]{1,0:T(8,128)} custom-call(s32[12288]{0:T(1024)} %bitcast.10, s32[12288]{0:T(1024)} %bitcast.12, s32[12288]{0:T(1024)} %bitcast.8, f32[12288]{0:T(1024)} %refs_3_.3, f32[64,6144]{1,0:T(8,128)} %refs_6_.1), custom_call_target="tpu_custom_call" | custom-call | flops 30000001024 | bytes 90000000 | tf_op jit(solution)/shard_map/pallas_call | solution.py:165
  43.8 3.2 %collective-permute-start.4 = (f32[64,3072]{1,0:T(8,128)S(1)}, f32[64,3072]{1,0:T(8,128)}, u32[]{:S(2)}, u32[]{:S(2)}) collective-permute-start(f32[64,3072]{1,0:T(8,128)S(1)} %collective-permute-done.1.refs_4_), channel_id=1, source_target_pairs={{0,2},{1,3},{2,4},{3,5},{4,6},{5,7},{6,8},{7,9},{8,10},{9,11},{10,... | collective-permute-start | bytes 2359304 | tf_op jit(solution)/shard_map/ppermute | solution.py:26
  47.0 1.5 collective-permute-start.5
  48.5 41.0 %shard_map.69 = (f32[64,6144]{1,0:T(8,128)}, f32[6144,128]{1,0:T(8,128)}, f32[64,512]{1,0:T(8,128)}, f32[64,512]{1,0:T(8,128)}) custom-call(s32[12288]{0:T(1024)} %bitcast.11, s32[12288]{0:T(1024)} %bitcast.13, s32[12288]{0:T(1024)} %bitcast.9, f32[12288]{0:T(1024)} %refs_3_.3, s32[512]{0:T(512)} %low_s.1, s32[512]{0:T(512)} %up_s.1, f32[64,6144]{1,0:T(8,128)} %refs_6_.1, ...), custom_call_target="tpu_custom_call" | custom-call | flops 30000001024 | bytes 90000000 | tf_op jit(solution)/shard_map/pallas_call | solution.py:165
  89.6 1.6 constant_dynamic-slice_fusion
  91.1 3.3 %collective-permute-start.6 = (f32[64,3072]{1,0:T(8,128)S(1)}, f32[64,3072]{1,0:T(8,128)S(1)}, u32[]{:S(2)}, u32[]{:S(2)}) collective-permute-start(f32[64,3072]{1,0:T(8,128)S(1)} %get-tuple-element.27), channel_id=1, source_target_pairs={{0,1},{1,0},{2,3},{3,2},{4,5},{5,4},{6,7},{7,6},{8,9},{9,8},{10,11... | collective-permute-start | bytes 2359304 | tf_op jit(solution)/shard_map/ppermute | solution.py:36
  94.4 1.9 %collective-permute-start.2 = (f32[64,512]{1,0:T(8,128)S(1)}, f32[64,512]{1,0:T(8,128)S(1)}, u32[]{:S(2)}, u32[]{:S(2)}) collective-permute-start(f32[64,512]{1,0:T(8,128)S(1)} %copy-done.7), channel_id=1, source_target_pairs={{0,16},{16,32},{32,48},{48,64},{64,80},{80,96},{96,112},{112,128},... | collective-permute-start | bytes 393224 | tf_op jit(solution)/shard_map/ppermute | solution.py:32
  96.3 4.5 %collective-permute-start.3 = (f32[64,512]{1,0:T(8,128)S(1)}, f32[64,512]{1,0:T(8,128)S(1)}, u32[]{:S(2)}, u32[]{:S(2)}) collective-permute-start(f32[64,512]{1,0:T(8,128)S(1)} %copy-done.6), channel_id=1, source_target_pairs={{16,0},{32,16},{48,32},{64,48},{80,64},{96,80},{112,96},{128,112},... | collective-permute-start | bytes 393224 | tf_op jit(solution)/shard_map/ppermute | solution.py:32
  100.9 0.4 collective-permute-start.7
  101.3 1.0 collective-permute-start.8
  102.3 0.4 collective-permute-start.9
  102.7 0.7 collective-permute-done.3.above_ref
  103.4 2.9 %collective-permute-start.10 = (f32[64,3072]{1,0:T(8,128)}, f32[64,3072]{1,0:T(8,128)}, u32[]{:S(2)}, u32[]{:S(2)}) collective-permute-start(f32[64,3072]{1,0:T(8,128)} %collective-permute-done.4.refs_6_), channel_id=1, source_target_pairs={{0,2},{1,3},{2,4},{3,5},{4,6},{5,7},{14,0},{15,1},{16,30},{17,31},... | collective-permute-start | bytes 2359304 | tf_op jit(solution)/shard_map/ppermute | solution.py:26
  106.3 8.3 %collective-permute-done.6.yb_ref = f32[64,3072]{1,0:T(8,128)S(1)} collective-permute-done((f32[64,3072]{1,0:T(8,128)S(1)}, f32[64,3072]{1,0:T(8,128)S(1)}, u32[]{:S(2)}, u32[]{:S(2)}) %collective-permute-start.6) | collective-permute-done | bytes 786464 | tf_op jit(solution)/shard_map/ppermute | solution.py:36
  114.6 0.9 copy-done
  115.5 2.9 %collective-permute-start.11 = (f32[64,3072]{1,0:T(8,128)}, f32[64,3072]{1,0:T(8,128)}, u32[]{:S(2)}, u32[]{:S(2)}) collective-permute-start(f32[64,3072]{1,0:T(8,128)} %collective-permute-done.5.refs_7_), channel_id=1, source_target_pairs={{0,2},{1,3},{2,4},{3,5},{4,6},{5,7},{14,0},{15,1},{16,30},{17,31},... | collective-permute-start | bytes 2359304 | tf_op jit(solution)/shard_map/ppermute | solution.py:26
  118.5 1.9 %copy-done.4 = f32[6144,128]{1,0:T(8,128)S(1)} copy-done((f32[6144,128]{1,0:T(8,128)S(1)}, f32[6144,128]{1,0:T(8,128)}, u32[]{:S(2)}) %copy-start.4) | copy-done | bytes 3145752
  120.4 8.0 %shard_map.70 = f32[64,6144]{1,0:T(8,128)} custom-call(s32[512]{0:T(512)S(1)} %copy-done.2, s32[512]{0:T(512)S(1)} %copy-done.3, f32[6144,128]{1,0:T(8,128)S(1)} %copy-done.4, f32[64,512]{1,0:T(8,128)S(1)} %collective-permute-done.2.below_ref, f32[64,512]{1,0:T(8,128)S(1)} %collective-permute-done.3.above_ref), custom_call_target="tpu_custom_call" | custom-call | flops 6000000000 | bytes 18000000 | tf_op jit(solution)/shard_map/pallas_call | solution.py:263
  128.4 1.0 collective-permute-done.7.refs_1_
  129.5 2.0 %collective-permute-done.10.refs_8_ = f32[64,3072]{1,0:T(8,128)} collective-permute-done((f32[64,3072]{1,0:T(8,128)}, f32[64,3072]{1,0:T(8,128)}, u32[]{:S(2)}, u32[]{:S(2)}) %collective-permute-start.10) | collective-permute-done | bytes 786464 | tf_op jit(solution)/shard_map/ppermute | solution.py:26
  131.5 8.4 %collective-permute-done.11.refs_9_ = f32[64,3072]{1,0:T(8,128)} collective-permute-done((f32[64,3072]{1,0:T(8,128)}, f32[64,3072]{1,0:T(8,128)}, u32[]{:S(2)}, u32[]{:S(2)}) %collective-permute-start.11) | collective-permute-done | bytes 786464 | tf_op jit(solution)/shard_map/ppermute | solution.py:26
  139.9 6.0 %shard_map.71 = f32[16,64,128]{2,1,0:T(8,128)S(1)} custom-call(s32[3]{0:T(128)S(1)} %pad_add_fusion.place, f32[64,3072]{1,0:T(8,128)S(1)} %get-tuple-element.26.ya_ref, f32[64,3072]{1,0:T(8,128)S(1)} %copy-done.1, f32[64,3072]{1,0:T(8,128)S(1)} %get-tuple-element.28.refs_0_, f32[64,3072]{1,0:T(8,128)} %collective-permute-done.7.refs_1_, ...), custom_call_target="tpu_custom_call" | custom-call | flops 8000000000 | bytes 24000000 | tf_op jit(solution)/shard_map/pallas_call | solution.py:214
  145.9 14.8 %all_to_all.5 = f32[16,64,128]{2,1,0:T(8,128)S(1)} all-to-all(f32[16,64,128]{2,1,0:T(8,128)S(1)} %shard_map.71), channel_id=1, replica_groups=mesh['mesh'=16,'snap'=16] {'mesh'}, dimensions={0} | all-to-all | bytes 1048576 | tf_op jit(solution)/shard_map/all_to_all | solution.py:276
  160.8 1.4 collective-permute-start.12
  162.3 7.1 %collective-permute-start.14 = (f32[64,64]{1,0:T(8,128)S(1)}, f32[64,64]{1,0:T(8,128)S(1)}, u32[]{:S(2)}, u32[]{:S(2)}) collective-permute-start(f32[64,64]{1,0:T(8,128)S(1)} %slice.21), channel_id=1, source_target_pairs={{1,0},{17,1},{33,2},{49,3},{65,4},{81,5},{97,6},{113,7},{129,8},{1... | collective-permute-start | bytes 49160 | tf_op jit(solution)/shard_map/ppermute | solution.py:42
  169.4 4.6 %collective-permute-start.13 = (f32[64,64]{1,0:T(8,128)S(1)}, f32[64,64]{1,0:T(8,128)S(1)}, u32[]{:S(2)}, u32[]{:S(2)}) collective-permute-start(f32[64,64]{1,0:T(8,128)S(1)} %get-tuple-element.33), channel_id=1, source_target_pairs={{0,0},{16,1},{32,2},{48,3},{64,4},{80,5},{96,6},{112,7},{128,8},{1... | collective-permute-start | bytes 49160 | tf_op jit(solution)/shard_map/ppermute | solution.py:42
  174.1 9.3 %collective-permute-done.13 = f32[64,64]{1,0:T(8,128)S(1)} collective-permute-done((f32[64,64]{1,0:T(8,128)S(1)}, f32[64,64]{1,0:T(8,128)S(1)}, u32[]{:S(2)}, u32[]{:S(2)}) %collective-permute-start.13) | collective-permute-done | bytes 16416 | tf_op jit(solution)/shard_map/ppermute | solution.py:42
  183.4 0.6 add_multiply_fusion
  (28 shorter events, 0.3 us)
Async XLA Ops:
  0.7 7.4 %copy-start.5 = (s32[3,12288]{1,0:T(4,128)S(1)}, s32[3,12288]{1,0:T(4,128)}, u32[]{:S(2)}) copy-start(s32[3,12288]{1,0:T(4,128)} %param.6) | copy-start | bytes 442372
  3.1 40.7 %collective-permute-start = (f32[64,3072]{1,0:T(8,128)}, f32[64,3072]{1,0:T(8,128)S(1)}, u32[]{:S(2)}, u32[]{:S(2)}) collective-permute-start(f32[64,3072]{1,0:T(8,128)} %get-tuple-element.29), channel_id=1, source_target_pairs={{0,3},{1,2},{2,5},{3,4},{4,7},{5,6},{6,9},{7,8},{8,11},{9,10},{10,... | collective-permute-start | bytes 2359304 | tf_op jit(solution)/shard_map/ppermute | solution.py:26
  4.8 39.0 %collective-permute-start.1 = (f32[64,3072]{1,0:T(8,128)S(1)}, f32[64,3072]{1,0:T(8,128)S(1)}, u32[]{:S(2)}, u32[]{:S(2)}) collective-permute-start(f32[64,3072]{1,0:T(8,128)S(1)} %get-tuple-element.28.refs_0_), channel_id=1, source_target_pairs={{0,4},{1,5},{2,6},{3,7},{4,8},{5,9},{6,10},{7,11},{8,12},{9,13},{1... | collective-permute-start | bytes 2359304 | tf_op jit(solution)/shard_map/ppermute | solution.py:26
  43.8 45.7 %collective-permute-start.4 = (f32[64,3072]{1,0:T(8,128)S(1)}, f32[64,3072]{1,0:T(8,128)}, u32[]{:S(2)}, u32[]{:S(2)}) collective-permute-start(f32[64,3072]{1,0:T(8,128)S(1)} %collective-permute-done.1.refs_4_), channel_id=1, source_target_pairs={{0,2},{1,3},{2,4},{3,5},{4,6},{5,7},{6,8},{7,9},{8,10},{9,11},{10,... | collective-permute-start | bytes 2359304 | tf_op jit(solution)/shard_map/ppermute | solution.py:26
  47.0 42.5 %collective-permute-start.5 = (f32[64,3072]{1,0:T(8,128)S(1)}, f32[64,3072]{1,0:T(8,128)}, u32[]{:S(2)}, u32[]{:S(2)}) collective-permute-start(f32[64,3072]{1,0:T(8,128)S(1)} %collective-permute-done.refs_3_), channel_id=1, source_target_pairs={{0,4},{1,5},{2,6},{3,7},{4,8},{5,9},{6,10},{7,11},{8,12},{9,13},{1... | collective-permute-start | bytes 2359304 | tf_op jit(solution)/shard_map/ppermute | solution.py:26
  89.5 4.9 %copy-start.7 = (f32[64,512]{1,0:T(8,128)S(1)}, f32[64,512]{1,0:T(8,128)}, u32[]{:S(2)}) copy-start(f32[64,512]{1,0:T(8,128)} %get-tuple-element.16) | copy-start | bytes 393220
  89.5 6.8 %copy-start.6 = (f32[64,512]{1,0:T(8,128)S(1)}, f32[64,512]{1,0:T(8,128)}, u32[]{:S(2)}) copy-start(f32[64,512]{1,0:T(8,128)} %get-tuple-element.17) | copy-start | bytes 393220
  89.5 29.0 %copy-start.2 = (s32[512]{0:T(512)S(1)}, s32[512]{0:T(512)}, u32[]{:S(2)}) copy-start(s32[512]{0:T(512)} %low_s.1) | copy-start | bytes 6148
  89.5 29.0 %copy-start.3 = (s32[512]{0:T(512)S(1)}, s32[512]{0:T(512)}, u32[]{:S(2)}) copy-start(s32[512]{0:T(512)} %up_s.1) | copy-start | bytes 6148
  91.1 23.5 %collective-permute-start.6 = (f32[64,3072]{1,0:T(8,128)S(1)}, f32[64,3072]{1,0:T(8,128)S(1)}, u32[]{:S(2)}, u32[]{:S(2)}) collective-permute-start(f32[64,3072]{1,0:T(8,128)S(1)} %get-tuple-element.27), channel_id=1, source_target_pairs={{0,1},{1,0},{2,3},{3,2},{4,5},{5,4},{6,7},{7,6},{8,9},{9,8},{10,11... | collective-permute-start | bytes 2359304 | tf_op jit(solution)/shard_map/ppermute | solution.py:36
  94.4 7.9 %collective-permute-start.2 = (f32[64,512]{1,0:T(8,128)S(1)}, f32[64,512]{1,0:T(8,128)S(1)}, u32[]{:S(2)}, u32[]{:S(2)}) collective-permute-start(f32[64,512]{1,0:T(8,128)S(1)} %copy-done.7), channel_id=1, source_target_pairs={{0,16},{16,32},{32,48},{48,64},{64,80},{80,96},{96,112},{112,128},... | collective-permute-start | bytes 393224 | tf_op jit(solution)/shard_map/ppermute | solution.py:32
  96.3 7.1 %collective-permute-start.3 = (f32[64,512]{1,0:T(8,128)S(1)}, f32[64,512]{1,0:T(8,128)S(1)}, u32[]{:S(2)}, u32[]{:S(2)}) collective-permute-start(f32[64,512]{1,0:T(8,128)S(1)} %copy-done.6), channel_id=1, source_target_pairs={{16,0},{32,16},{48,32},{64,48},{80,64},{96,80},{112,96},{128,112},... | collective-permute-start | bytes 393224 | tf_op jit(solution)/shard_map/ppermute | solution.py:32
  100.9 28.6 %collective-permute-start.7 = (f32[64,3072]{1,0:T(8,128)}, f32[64,3072]{1,0:T(8,128)}, u32[]{:S(2)}, u32[]{:S(2)}) collective-permute-start(f32[64,3072]{1,0:T(8,128)} %get-tuple-element.29), channel_id=1, source_target_pairs={{0,1},{1,0},{2,3},{3,2},{4,5},{5,4},{6,7},{7,6},{8,9},{9,8},{10,11... | collective-permute-start | bytes 2359304 | tf_op jit(solution)/shard_map/ppermute | solution.py:36
  101.3 28.2 %collective-permute-start.8 = (f32[64,3072]{1,0:T(8,128)S(1)}, f32[64,3072]{1,0:T(8,128)}, u32[]{:S(2)}, u32[]{:S(2)}) collective-permute-start(f32[64,3072]{1,0:T(8,128)S(1)} %get-tuple-element.28.refs_0_), channel_id=1, source_target_pairs={{0,2},{1,3},{2,4},{3,5},{4,6},{5,7},{6,8},{7,9},{8,10},{9,11},{10,... | collective-permute-start | bytes 2359304 | tf_op jit(solution)/shard_map/ppermute | solution.py:26
  102.3 27.2 %collective-permute-start.9 = (f32[64,3072]{1,0:T(8,128)S(1)}, f32[64,3072]{1,0:T(8,128)}, u32[]{:S(2)}, u32[]{:S(2)}) collective-permute-start(f32[64,3072]{1,0:T(8,128)S(1)} %collective-permute-done.refs_3_), channel_id=1, source_target_pairs={{0,2},{1,3},{2,4},{3,5},{4,6},{5,7},{6,8},{7,9},{8,10},{9,11},{10,... | collective-permute-start | bytes 2359304 | tf_op jit(solution)/shard_map/ppermute | solution.py:26
  103.4 28.1 %collective-permute-start.10 = (f32[64,3072]{1,0:T(8,128)}, f32[64,3072]{1,0:T(8,128)}, u32[]{:S(2)}, u32[]{:S(2)}) collective-permute-start(f32[64,3072]{1,0:T(8,128)} %collective-permute-done.4.refs_6_), channel_id=1, source_target_pairs={{0,2},{1,3},{2,4},{3,5},{4,6},{5,7},{14,0},{15,1},{16,30},{17,31},... | collective-permute-start | bytes 2359304 | tf_op jit(solution)/shard_map/ppermute | solution.py:26
  114.6 0.9 copy-start
  115.5 24.4 %collective-permute-start.11 = (f32[64,3072]{1,0:T(8,128)}, f32[64,3072]{1,0:T(8,128)}, u32[]{:S(2)}, u32[]{:S(2)}) collective-permute-start(f32[64,3072]{1,0:T(8,128)} %collective-permute-done.5.refs_7_), channel_id=1, source_target_pairs={{0,2},{1,3},{2,4},{3,5},{4,6},{5,7},{14,0},{15,1},{16,30},{17,31},... | collective-permute-start | bytes 2359304 | tf_op jit(solution)/shard_map/ppermute | solution.py:26
  118.5 1.9 %copy-start.4 = (f32[6144,128]{1,0:T(8,128)S(1)}, f32[6144,128]{1,0:T(8,128)}, u32[]{:S(2)}) copy-start(f32[6144,128]{1,0:T(8,128)} %get-tuple-element.15.rows_ref) | copy-start | bytes 9437188
  120.4 19.5 %copy-start.1 = (f32[64,3072]{1,0:T(8,128)S(1)}, f32[64,3072]{1,0:T(8,128)}, u32[]{:S(2)}) copy-start(f32[64,3072]{1,0:T(8,128)} %copy-done) | copy-start | bytes 2359300
  160.8 8.6 %collective-permute-start.12 = (f32[64,64]{1,0:T(8,128)S(1)}, f32[64,64]{1,0:T(8,128)S(1)}, u32[]{:S(2)}, u32[]{:S(2)}) collective-permute-start(f32[64,64]{1,0:T(8,128)S(1)} %slice.21), channel_id=1, source_target_pairs={{0,1},{1,0},{2,3},{3,2},{4,5},{5,4},{6,7},{7,6},{8,9},{9,8},{10,11... | collective-permute-start | bytes 49160 | tf_op jit(solution)/shard_map/ppermute | solution.py:36
  162.3 11.8 %collective-permute-start.14 = (f32[64,64]{1,0:T(8,128)S(1)}, f32[64,64]{1,0:T(8,128)S(1)}, u32[]{:S(2)}, u32[]{:S(2)}) collective-permute-start(f32[64,64]{1,0:T(8,128)S(1)} %slice.21), channel_id=1, source_target_pairs={{1,0},{17,1},{33,2},{49,3},{65,4},{81,5},{97,6},{113,7},{129,8},{1... | collective-permute-start | bytes 49160 | tf_op jit(solution)/shard_map/ppermute | solution.py:42
  169.4 13.9 %collective-permute-start.13 = (f32[64,64]{1,0:T(8,128)S(1)}, f32[64,64]{1,0:T(8,128)S(1)}, u32[]{:S(2)}, u32[]{:S(2)}) collective-permute-start(f32[64,64]{1,0:T(8,128)S(1)} %get-tuple-element.33), channel_id=1, source_target_pairs={{0,0},{16,1},{32,2},{48,3},{64,4},{80,5},{96,6},{112,7},{128,8},{1... | collective-permute-start | bytes 49160 | tf_op jit(solution)/shard_map/ppermute | solution.py:42

commit v2 on v1

v2 whole, which is shorter than its diff:
```python
import functools

import jax
import jax.numpy as jnp
from jax import lax
from jax.experimental import pallas as pl
from jax.experimental.pallas import tpu as pltpu
from jax.sharding import PartitionSpec as P

LANES = 128
MIB = 2 ** 20


def ring_hop(value, steps, cross=False, closing=False):
    parts, blocks = lax.axis_size("mesh"), lax.axis_size("snap")
    rings = blocks // 2
    pairs = []
    for part in range(parts):
        way = 1 if part % 2 == 0 else -1
        for block in range(blocks):
            z, h = block // 2, block % 2
            target = (z + way * steps) % rings
            if closing and (target < rings // 2) != (part % 2 == 0):
                continue
            pairs.append((part * blocks + block, part * blocks + 2 * target + (h ^ 1 if cross else h)))
    return lax.ppermute(value, ("mesh", "snap"), pairs)


def passed_along(value, axis, steps):
    count = lax.axis_size(axis)
    leading, last = (max(0, -steps), min(count, count - steps))
    return lax.ppermute(value, axis, [(source, source + steps) for source in range(leading, last)])


def partner(value):
    return lax.ppermute(value, "snap", [(i, i ^ 1) for i in range(lax.axis_size("snap"))])


def mirrored(value):
    count = lax.axis_size("snap")
    return lax.ppermute(value, ("mesh", "snap"),
                        [(s * count + m, m * count + s) for m in range(count) for s in range(count)])


def apply_kernel(first, last, start, count, arrays, parts, *refs):
    refs = list(refs)
    a_hbm, b_hbm, c_hbm, m_hbm, x_ref = refs[:5]
    del refs[:5]
    rows_in = None if first else refs.pop(0)
    low_s, up_s = (refs.pop(0), refs.pop(0)) if last else (None, None)
    rows_out = refs.pop(0)
    y_out, low_out, up_out = (refs.pop(0), refs.pop(0), refs.pop(0)) if last else (None, None, None)
    a_s, b_s, c_s, m_s, sems, *zs = refs
    snaps, nodes = x_ref.shape
    tiles = LANES // 8
    width = 1 + parts
    copies = []
    for j, (source, target) in enumerate(zip((a_hbm, b_hbm, c_hbm, m_hbm), (a_s, b_s, c_s, m_s))):
        copy = pltpu.make_async_copy(source.at[pl.ds(start, count)], target, sems.at[j])
        copy.start()
        copies.append(copy)

    def tile_of(block, i, part):
        return pl.ds(pl.multiple_of(block * (LANES * width) + (i * width + part) * 8, 8), 8)

    def prepare(block, carry):
        x = x_ref[:, pl.ds(pl.multiple_of(block * LANES, LANES), LANES)]
        rows = jnp.concatenate([x, x], axis=0).T
        blank = jnp.zeros((8, LANES), jnp.float32)
        for z in zs:
            for i in range(tiles):
                z[tile_of(block, i, 0), :] = rows[i * 8:(i + 1) * 8]
                for part in range(parts):
                    z[tile_of(block, i, 1 + part), :] = blank
        return carry

    lax.fori_loop(0, nodes // LANES, prepare, 0)
    for copy in copies:
        copy.wait()

    def elements(group, carry):
        for j, z in enumerate(zs):
            corners, updated = [], []
            for k in range(2 * parts):
                e = group * (arrays * 2 * parts) + (j * 2 * parts + k)
                corners.append((a_s[e], b_s[e], c_s[e]))
                mass = m_s[e]
                values = [z[pl.ds(n, 1), :] for n in corners[k]]
                held = [z[pl.ds(n + 8 * (1 + k // 2), 1), :] for n in corners[k]]
                total = values[0] + values[1] + values[2]
                updated.append([h + mass * (v + total) for h, v in zip(held, values)])
            for k in range(2 * parts):
                at = snaps * (k % 2)
                for n, new in zip(corners[k], updated[k]):
                    z[pl.ds(n + 8 * (1 + k // 2), 1), at:at + snaps] = new[:, at:at + snaps]
        return carry

    lax.fori_loop(0, count // (arrays * 2 * parts), elements, 0)

    def finish(block, carry):
        totals = []
        for i in range(tiles):
            total = None
            for z in zs:
                for part in range(parts):
                    value = z[tile_of(block, i, 1 + part), :]
                    total = value if total is None else total + value
            totals.append(total)
        total = jnp.concatenate(totals, axis=0)
        at = pl.multiple_of(block * LANES, LANES)
        if not first:
            total = total + rows_in[pl.ds(at, LANES), :]
        if last:
            total = total * (1.0 / 12.0)
            columns = total.T
            y_out[:, pl.ds(at, LANES)] = columns[0:snaps, :] + columns[snaps:2 * snaps, :]
        rows_out[pl.ds(at, LANES), :] = total
        return carry

    lax.fori_loop(0, nodes // LANES, finish, 0)
    if not last:
        return
    for list_s, out in ((low_s, low_out), (up_s, up_out)):
        def gather(i, carry, list_s=list_s):
            at = pl.multiple_of(i * 16, 16)
            for k in range(16):
                zs[0][pl.ds(at + k, 1), :] = rows_out[pl.ds(list_s[at + k], 1), :]
            return carry

        shared = out.shape[1]
        lax.fori_loop(0, shared // 16, gather, 0)
        for block in range(shared // LANES):
            at = block * LANES
            columns = zs[0][at:at + LANES, :].T
            out[:, at:at + LANES] = columns[0:snaps, :] + columns[snaps:2 * snaps, :]


def assemble_kernel(low_s, up_s, rows_ref, below_ref, above_ref, out_ref, rows, taken):
    snaps, shared = below_ref.shape
    nodes = rows_ref.shape[0]

    def copy(i, carry):
        at = pl.multiple_of(i * LANES, LANES)
        rows[pl.ds(at, LANES), :] = rows_ref[pl.ds(at, LANES), :]
        return carry

    lax.fori_loop(0, nodes // LANES, copy, 0)
    for list_s, received in ((low_s, below_ref), (up_s, above_ref)):
        for block in range(shared // LANES):
            at = block * LANES
            value = received[:, at:at + LANES]
            taken[at:at + LANES, :] = jnp.concatenate([value, jnp.zeros_like(value)], axis=0).T

        def add(i, carry, list_s=list_s):
            at = pl.multiple_of(i * 8, 8)
            nodes_of = [list_s[at + k] for k in range(8)]
            new = [rows[pl.ds(n, 1), :] + taken[pl.ds(at + k, 1), :] for k, n in enumerate(nodes_of)]
            for n, value in zip(nodes_of, new):
                rows[pl.ds(n, 1), :] = value
            return carry

        lax.fori_loop(0, shared // 8, add, 0)

    def write(i, carry):
        at = pl.multiple_of(i * LANES, LANES)
        columns = rows[pl.ds(at, LANES), :].T
        out_ref[:, pl.ds(at, LANES)] = columns[0:snaps, :] + columns[snaps:2 * snaps, :]
        return carry

    lax.fori_loop(0, nodes // LANES, write, 0)


ANYWHERE = pl.BlockSpec(memory_space=pl.ANY)
IN_VMEM = pl.BlockSpec(memory_space=pltpu.VMEM)
IN_SMEM = pl.BlockSpec(memory_space=pltpu.SMEM)


def cost(micros):
    return pl.CostEstimate(flops=int(micros * 1e9), bytes_accessed=int(micros * 3e6), transcendentals=0)


ARRAYS, PARTS = 4, 2


def apply_call(index, calls, columns, snapshots, rows, lists):
    first, last = index == 0, index == calls - 1
    snaps, nodes = snapshots.shape
    count = columns[0].shape[0] // calls
    shared = lists[0].shape[0]
    row_shape = jax.ShapeDtypeStruct((nodes, LANES), jnp.float32)
    side = jax.ShapeDtypeStruct((snaps, shared), jnp.float32)
    whole = jax.ShapeDtypeStruct((snaps, nodes), jnp.float32)
    operands = columns + (snapshots,) + (() if first else (rows,)) + (lists if last else ())
    return pl.pallas_call(
        functools.partial(apply_kernel, first, last, index * count, count, ARRAYS, PARTS),
        out_shape=[row_shape] + ([whole, side, side] if last else []),
        in_specs=[ANYWHERE] * 4 + [IN_VMEM] + ([] if first else [IN_VMEM]) + ([IN_SMEM] * 2 if last else []),
        out_specs=[IN_VMEM] + ([IN_VMEM] * 3 if last else []),
        scratch_shapes=[pltpu.SMEM((count,), jnp.int32)] * 3
        + [pltpu.SMEM((count,), jnp.float32), pltpu.SemaphoreType.DMA((4,))]
        + [pltpu.VMEM((nodes * (1 + PARTS), LANES), jnp.float32)] * ARRAYS,
        compiler_params=pltpu.CompilerParams(vmem_limit_bytes=56 * MIB),
        cost_estimate=cost(20),
    )(*operands)


def split3(left, right):
    dims = (((1,), (1,)), ((), ()))
    dot = functools.partial(lax.dot_general, dimension_numbers=dims, preferred_element_type=jnp.float32)
    (l_hi, l_lo), (r_hi, r_lo) = left, right
    return dot(l_hi, r_hi) + (dot(l_hi, r_lo) + dot(l_lo, r_hi))


def halves_of(value):
    high = value.astype(jnp.bfloat16)
    return high, (value - high.astype(jnp.float32)).astype(jnp.bfloat16)


def gram_kernel(place, ya_ref, yb_ref, a0_ref, b0_ref, *refs):
    *streams, out_ref, sums = refs
    snaps = ya_ref.shape[0]
    rings = out_ref.shape[0] // 4
    low = snaps // 2
    z, h, way = place[0], place[1], place[2]
    step = pl.program_id(0)

    @pl.when(step == 0)
    def _():
        sums[...] = jnp.zeros_like(sums)

    y = halves_of(jnp.concatenate([ya_ref[...], yb_ref[...]], axis=0))
    sums[0] += split3(halves_of(jnp.concatenate([a0_ref[...], b0_ref[...]], axis=0)), y)
    for distance, stream in enumerate(streams, 1):
        sums[distance] += split3(halves_of(stream[...]), y)

    @pl.when(step == pl.num_programs(0) - 1)
    def _():
        out_ref[...] = jnp.zeros_like(out_ref)
        for distance in range(1 + len(streams)):
            value = sums[distance]
            if distance == 0:
                value = 0.5 * value
            at = lax.rem(z - way * distance + rings, rings)
            for side in range(2):
                row = 2 * at + (h if side == 0 else 1 - h)
                upper, lower = value[side * snaps:side * snaps + low], value[side * snaps + low:(side + 1) * snaps]
                out_ref[2 * row + h] = jnp.concatenate([upper[:, :snaps], lower[:, :snaps]], axis=1)
                out_ref[2 * row + (1 - h)] = jnp.concatenate([upper[:, snaps:], lower[:, snaps:]], axis=1)


def gram_call(place, ya, yb, a0, b0, streams, rings):
    snaps, nodes = ya.shape
    chunk = nodes // 4
    single = pl.BlockSpec((snaps, chunk), lambda i: (0, i))
    double = pl.BlockSpec((2 * snaps, chunk), lambda i: (0, i))
    tiles = (4 * rings, snaps // 2, 2 * snaps)
    return pl.pallas_call(
        gram_kernel,
        grid=(nodes // chunk,),
        out_shape=jax.ShapeDtypeStruct(tiles, jnp.float32),
        in_specs=[IN_SMEM] + [single] * 4 + [double] * len(streams),
        out_specs=pl.BlockSpec(tiles, lambda i: (0, 0, 0)),
        scratch_shapes=[pltpu.VMEM((1 + len(streams), 2 * snaps, 2 * snaps), jnp.float32)],
        compiler_params=pltpu.CompilerParams(vmem_limit_bytes=40 * MIB),
        cost_estimate=cost(8),
    )(place, ya, yb, a0, b0, *streams)


def on_device(snapshots, connectivity, element_mass, lower_shared, upper_shared):
    snaps, nodes = snapshots.shape
    parts = lax.axis_size("mesh")
    blocks = lax.axis_size("snap")
    position = lax.axis_index("mesh")
    block = lax.axis_index("snap")
    rings = blocks // 2
    z, h = block // 2, block % 2
    half = nodes // 2
    tied = lax.optimization_barrier

    own = lax.dynamic_slice_in_dim(snapshots, h * half, half, 1)
    given = lax.dynamic_slice_in_dim(snapshots, (1 - h) * half, half, 1)
    a1 = ring_hop(own, 1)
    b1 = ring_hop(given, 1, cross=True)

    spread = (connectivity >> 3) * (8 * (1 + PARTS)) + (connectivity & 7)
    columns = tuple(spread[k] for k in range(3)) + (element_mass,)
    lists = (lower_shared, upper_shared)
    (rows,) = apply_call(0, 3, columns, snapshots, None, lists)

    rows, a1, b1 = tied((rows, a1, b1))
    pair1 = jnp.concatenate([a1, b1], axis=0)
    pair2 = ring_hop(pair1, 1)
    (rows,) = apply_call(1, 3, columns, snapshots, rows, lists)

    rows, pair2 = tied((rows, pair2))
    pair3 = ring_hop(pair2, 1)
    b0 = partner(given)
    rows, partial, low, high = apply_call(2, 3, columns, snapshots, rows, lists)

    partial, pair3, b0 = tied((partial, pair3, b0))
    y_own = lax.dynamic_slice_in_dim(partial, h * half, half, 1)
    y_theirs = partner(lax.dynamic_slice_in_dim(partial, (1 - h) * half, half, 1))
    pair4 = ring_hop(pair3, 1, closing=True)

    from_below = passed_along(high, "mesh", 1)
    from_above = passed_along(low, "mesh", -1)
    shared = lower_shared.shape[0]
    weighted = pl.pallas_call(
        assemble_kernel,
        out_shape=jax.ShapeDtypeStruct((snaps, nodes), jnp.float32),
        in_specs=[IN_SMEM] * 2 + [IN_VMEM] * 3,
        out_specs=IN_VMEM,
        scratch_shapes=[pltpu.VMEM((nodes, LANES), jnp.float32), pltpu.VMEM((shared, LANES), jnp.float32)],
        compiler_params=pltpu.CompilerParams(vmem_limit_bytes=20 * MIB),
        cost_estimate=cost(8),
    )(lower_shared, upper_shared, rows, from_below, from_above)
    weighted, y_theirs, pair4 = tied((weighted, y_theirs, pair4))

    place = jnp.stack([z, h, jnp.where(position % 2 == 0, 1, -1)]).astype(jnp.int32)
    tiles = gram_call(place, y_own, y_theirs, own, b0, [pair1, pair2, pair3, pair4], rings)
    planes = [[m * blocks + 2 * r + c for m in range(parts) for c in range(2)] for r in range(rings)]
    tile = jnp.sum(lax.all_to_all(tiles, ("mesh", "snap"), 0, 0, axis_index_groups=planes, tiled=True), axis=0)
    other = mirrored(tile)

    def unfolded(value):
        return jnp.concatenate([value[:, :snaps], value[:, snaps:]], axis=0)

    return weighted, (unfolded(tile).T + unfolded(other)) * (1.0 / float(parts * nodes))


def solution(mesh):
    placed = (P("snap", "mesh"), P(None, "mesh"), P("mesh"), P("mesh"), P("mesh"))
    return jax.shard_map(
        on_device,
        mesh=mesh,
        in_specs=placed,
        out_specs=(P("snap", "mesh"), P("snap", "mesh")),
        check_vma=False,
    )
```

time: 184 us -> 159 us (0.86)
  the two profiles are of different devices: /device:TPU:20 before, /device:TPU:5 now
where the time goes in v2:
time: 159 us
  Pallas kernels  88 us (55%)
  starting transfers between devices  30 us (19%)
  waiting for transfers between devices  17.5 us (11%)
  blocking collectives  17.4 us (11%)
  local copies, waits for them, and re-layouts  4.16 us (3%)
    pallas_call x3, Pallas kernels, apply_call(): pl.pallas_call(functools.partial(apply_kernel, first, last, index * count...  73.4 us
    all_to_all x1, blocking collectives, on_device(): lax.all_to_all(tiles, ('mesh', 'snap'), 0, 0, axis_index_groups=planes, t...  17.4 us
    ppermute x5, starting transfers between devices, ring_hop(): return lax.ppermute(value, ('mesh', 'snap'), pairs)  16.2 us
    pallas_call x1, Pallas kernels, on_device(): pl.pallas_call(assemble_kernel, out_shape=jax.ShapeDtypeStruct((snaps, no...  8.9 us
    ppermute x2, waiting for transfers between devices, partner(): lax.ppermute(value, 'snap', [(i, i ^ 1) for i in range(lax.axis_size('sna...  8.69 us
    ppermute x1, waiting for transfers between devices, mirrored(): lax.ppermute(value, ('mesh', 'snap'), [(s * count + m, m * count + s) for...  7.33 us
    ppermute x1, starting transfers between devices, mirrored(): lax.ppermute(value, ('mesh', 'snap'), [(s * count + m, m * count + s) for...  6.34 us
    pallas_call x1, Pallas kernels, gram_call(): pl.pallas_call(gram_kernel, grid=(nodes // chunk,), out_shape=jax.ShapeDt...  5.7 us
  transfers between devices with their start and end apart: 10, of which 3 were waited for; matrix products, arithmetic and copies ran while one was open for 2% of the time, Pallas kernels for 52%

profile of v2, /device:TPU:5, one launch (start us, length us, event | category | flops | bytes accessed | tf_op | source)
XLA Modules:
  0.0 158.7 jit_solution(16652803152039448210)
XLA Ops:
  0.7 1.6 constant_dynamic-slice_fusion.2
  2.2 8.3 %collective-permute-start.1 = (f32[64,3072]{1,0:T(8,128)S(1)}, f32[64,3072]{1,0:T(8,128)S(1)}, u32[]{:S(2)}, u32[]{:S(2)}) collective-permute-start(f32[64,3072]{1,0:T(8,128)S(1)} %get-tuple-element.34), channel_id=1, source_target_pairs={{0,3},{1,2},{2,5},{3,4},{4,7},{5,6},{6,9},{7,8},{8,11},{9,10},{10,... | collective-permute-start | bytes 2359304 | tf_op jit(solution)/shard_map/ppermute | solution.py:26
  10.5 0.1 collective-permute-start.6
  10.6 0.7 collective-permute-start
  11.3 0.1 and_add_fusion
  11.4 0.8 fusion.1
  12.1 21.9 %shard_map.68.refs_5_ = f32[6144,128]{1,0:T(8,128)} custom-call(s32[12288]{0:T(1024)} %bitcast.14, s32[12288]{0:T(1024)} %bitcast.11, s32[12288]{0:T(1024)} %bitcast.8, f32[12288]{0:T(1024)} %refs_3_.5, f32[64,6144]{1,0:T(8,128)} %refs_4_.5), custom_call_target="tpu_custom_call" | custom-call | flops 20000000000 | bytes 60000000 | tf_op jit(solution)/shard_map/pallas_call | solution.py:194
  34.0 0.1 constant_dynamic-update-slice_fusion.1
  34.1 0.1 constant_dynamic-update-slice_fusion.refs_0_
  34.1 1.7 %collective-permute-start.2 = (f32[128,3072]{1,0:T(8,128)S(1)}, f32[128,3072]{1,0:T(8,128)S(1)}, u32[]{:S(2)}, u32[]{:S(2)}) collective-permute-start(f32[128,3072]{1,0:T(8,128)S(1)} %constant_dynamic-update-slice_fusion.refs_0_), channel_id=1, source_target_pairs={{0,2},{1,3},{2,4},{3,5},{4,6},{5,7},{6,8},{7,9},{8,10},{9,11},{10,... | collective-permute-start | bytes 4718600 | tf_op jit(solution)/shard_map/ppermute | solution.py:26
  35.9 23.0 %shard_map.69.refs_5_ = f32[6144,128]{1,0:T(8,128)} custom-call(s32[12288]{0:T(1024)} %bitcast.15, s32[12288]{0:T(1024)} %bitcast.12, s32[12288]{0:T(1024)} %bitcast.9, f32[12288]{0:T(1024)} %refs_3_.5, f32[64,6144]{1,0:T(8,128)} %refs_4_.5, f32[6144,128]{1,0:T(8,128)} %shard_map.68.refs_5_), custom_call_target="tpu_custom_call" | custom-call | flops 20000000000 | bytes 60000000 | tf_op jit(solution)/shard_map/pallas_call | solution.py:194
  58.9 1.6 %collective-permute-start.5 = (f32[128,3072]{1,0:T(8,128)S(1)}, f32[128,3072]{1,0:T(8,128)}, u32[]{:S(2)}, u32[]{:S(2)}) collective-permute-start(f32[128,3072]{1,0:T(8,128)S(1)} %collective-permute-done.2.refs_1_), channel_id=1, source_target_pairs={{0,2},{1,3},{2,4},{3,5},{4,6},{5,7},{6,8},{7,9},{8,10},{9,11},{10,... | collective-permute-start | bytes 4718600 | tf_op jit(solution)/shard_map/ppermute | solution.py:26
  60.5 28.5 %shard_map.70 = (f32[6144,128]{1,0:T(8,128)}, f32[64,6144]{1,0:T(8,128)}, f32[64,512]{1,0:T(8,128)}, f32[64,512]{1,0:T(8,128)}) custom-call(s32[12288]{0:T(1024)} %bitcast.16, s32[12288]{0:T(1024)} %bitcast.13, s32[12288]{0:T(1024)} %bitcast.10, f32[12288]{0:T(1024)} %refs_3_.5, f32[64,6144]{1,0:T(8,128)} %refs_4_.5, f32[6144,128]{1,0:T(8,128)} %shard_map.69.refs_5_, ...), custom_call_target="tpu_custom_call" | custom-call | flops 20000000000 | bytes 60000000 | tf_op jit(solution)/shard_map/pallas_call | solution.py:194
  89.1 3.8 %collective-permute-start.8 = (f32[128,3072]{1,0:T(8,128)}, f32[128,3072]{1,0:T(8,128)}, u32[]{:S(2)}, u32[]{:S(2)}) collective-permute-start(f32[128,3072]{1,0:T(8,128)} %collective-permute-done.5.refs_2_), channel_id=1, source_target_pairs={{0,2},{1,3},{2,4},{3,5},{4,6},{5,7},{14,0},{15,1},{16,30},{17,31},... | collective-permute-start | bytes 4718600 | tf_op jit(solution)/shard_map/ppermute | solution.py:26
  92.9 3.4 %collective-permute-start.3 = (f32[64,512]{1,0:T(8,128)}, f32[64,512]{1,0:T(8,128)S(1)}, u32[]{:S(2)}, u32[]{:S(2)}) collective-permute-start(f32[64,512]{1,0:T(8,128)} %get-tuple-element.22), channel_id=1, source_target_pairs={{0,16},{16,32},{32,48},{48,64},{64,80},{80,96},{96,112},{112,128},... | collective-permute-start | bytes 393224 | tf_op jit(solution)/shard_map/ppermute | solution.py:32
  96.3 0.0 copy-start.2
  96.3 0.0 copy-start.3
  96.3 2.2 %collective-permute-start.4 = (f32[64,512]{1,0:T(8,128)}, f32[64,512]{1,0:T(8,128)S(1)}, u32[]{:S(2)}, u32[]{:S(2)}) collective-permute-start(f32[64,512]{1,0:T(8,128)} %get-tuple-element.23), channel_id=1, source_target_pairs={{16,0},{32,16},{48,32},{64,48},{80,64},{96,80},{112,96},{128,112},... | collective-permute-start | bytes 393224 | tf_op jit(solution)/shard_map/ppermute | solution.py:32
  98.5 1.5 constant_dynamic-slice_fusion
  100.0 1.9 %collective-permute-start.7 = (f32[64,3072]{1,0:T(8,128)S(1)}, f32[64,3072]{1,0:T(8,128)S(1)}, u32[]{:S(2)}, u32[]{:S(2)}) collective-permute-start(f32[64,3072]{1,0:T(8,128)S(1)} %get-tuple-element.33), channel_id=1, source_target_pairs={{0,1},{1,0},{2,3},{3,2},{4,5},{5,4},{6,7},{7,6},{8,9},{9,8},{10,11... | collective-permute-start | bytes 2359304 | tf_op jit(solution)/shard_map/ppermute | solution.py:36
  101.9 0.1 pad_add_fusion.place
  102.0 1.5 collective-permute-done.4.above_ref
  103.5 8.9 %shard_map.71 = f32[64,6144]{1,0:T(8,128)} custom-call(s32[512]{0:T(512)S(1)} %copy-done.2, s32[512]{0:T(512)S(1)} %copy-done.3, f32[6144,128]{1,0:T(8,128)S(1)} %copy-done.4, f32[64,512]{1,0:T(8,128)S(1)} %collective-permute-done.3.below_ref, f32[64,512]{1,0:T(8,128)S(1)} %collective-permute-done.4.above_ref), custom_call_target="tpu_custom_call" | custom-call | flops 8000000000 | bytes 24000000 | tf_op jit(solution)/shard_map/pallas_call | solution.py:308
  112.4 8.7 %collective-permute-done.7.yb_ref = f32[64,3072]{1,0:T(8,128)S(1)} collective-permute-done((f32[64,3072]{1,0:T(8,128)S(1)}, f32[64,3072]{1,0:T(8,128)S(1)}, u32[]{:S(2)}, u32[]{:S(2)}) %collective-permute-start.7) | collective-permute-done | bytes 786464 | tf_op jit(solution)/shard_map/ppermute | solution.py:36
  121.1 5.7 %shard_map.72 = f32[32,32,128]{2,1,0:T(8,128)S(1)} custom-call(s32[3]{0:T(128)S(1)} %pad_add_fusion.place, f32[64,3072]{1,0:T(8,128)S(1)} %get-tuple-element.32.ya_ref, f32[64,3072]{1,0:T(8,128)S(1)} %collective-permute-done.7.yb_ref, f32[64,3072]{1,0:T(8,128)S(1)} %get-tuple-element.35.a0_ref, f32[64,3072]{1,0:T(8,128)S(1)} %collective-permute-done.6.b0_ref, ...), custom_call_target="tpu_custom_call" | custom-call | flops 8000000000 | bytes 24000000 | tf_op jit(solution)/shard_map/pallas_call | solution.py:257
  126.8 17.4 %all_to_all.5 = f32[32,32,128]{2,1,0:T(8,128)S(1)} all-to-all(f32[32,32,128]{2,1,0:T(8,128)S(1)} %shard_map.72), channel_id=1, replica_groups={{0,1,16,17,32,33,48,49,64,65,80,81,96,97,112,113,128,129,144,145,160,16..., dimensions={0} | all-to-all | bytes 1048576 | tf_op jit(solution)/shard_map/all_to_all | solution.py:322
  144.2 0.1 fusion.3
  144.3 6.3 %collective-permute-start.9 = (f32[32,128]{1,0:T(8,128)S(1)}, f32[32,128]{1,0:T(8,128)S(1)}, u32[]{:S(2)}, u32[]{:S(2)}) collective-permute-start(f32[32,128]{1,0:T(8,128)S(1)} %reduce_sum.9), channel_id=1, source_target_pairs={{0,0},{16,1},{32,2},{48,3},{64,4},{80,5},{96,6},{112,7},{128,8},{1... | collective-permute-start | bytes 49160 | tf_op jit(solution)/shard_map/ppermute | solution.py:41
  150.6 0.1 copy.7
  150.7 7.3 %collective-permute-done.9 = f32[32,128]{1,0:T(8,128)S(1)} collective-permute-done((f32[32,128]{1,0:T(8,128)S(1)}, f32[32,128]{1,0:T(8,128)S(1)}, u32[]{:S(2)}, u32[]{:S(2)}) %collective-permute-start.9) | collective-permute-done | bytes 16416 | tf_op jit(solution)/shard_map/ppermute | solution.py:41
  158.0 0.1 fusion.2
  158.1 0.6 fusion
  (19 shorter events, 0.1 us)
Async XLA Ops:
  0.7 10.6 %copy-start.5 = (s32[3,12288]{1,0:T(4,128)S(1)}, s32[3,12288]{1,0:T(4,128)}, u32[]{:S(2)}) copy-start(s32[3,12288]{1,0:T(4,128)} %param.6) | copy-start | bytes 442372
  2.2 31.8 %collective-permute-start.1 = (f32[64,3072]{1,0:T(8,128)S(1)}, f32[64,3072]{1,0:T(8,128)S(1)}, u32[]{:S(2)}, u32[]{:S(2)}) collective-permute-start(f32[64,3072]{1,0:T(8,128)S(1)} %get-tuple-element.34), channel_id=1, source_target_pairs={{0,3},{1,2},{2,5},{3,4},{4,7},{5,6},{6,9},{7,8},{8,11},{9,10},{10,... | collective-permute-start | bytes 2359304 | tf_op jit(solution)/shard_map/ppermute | solution.py:26
  10.5 78.6 %collective-permute-start.6 = (f32[64,3072]{1,0:T(8,128)S(1)}, f32[64,3072]{1,0:T(8,128)S(1)}, u32[]{:S(2)}, u32[]{:S(2)}) collective-permute-start(f32[64,3072]{1,0:T(8,128)S(1)} %get-tuple-element.34), channel_id=1, source_target_pairs={{0,1},{1,0},{2,3},{3,2},{4,5},{5,4},{6,7},{7,6},{8,9},{9,8},{10,11... | collective-permute-start | bytes 2359304 | tf_op jit(solution)/shard_map/ppermute | solution.py:36
  10.6 23.4 %collective-permute-start = (f32[64,3072]{1,0:T(8,128)S(1)}, f32[64,3072]{1,0:T(8,128)S(1)}, u32[]{:S(2)}, u32[]{:S(2)}) collective-permute-start(f32[64,3072]{1,0:T(8,128)S(1)} %get-tuple-element.35.a0_ref), channel_id=1, source_target_pairs={{0,2},{1,3},{2,4},{3,5},{4,6},{5,7},{6,8},{7,9},{8,10},{9,11},{10,... | collective-permute-start | bytes 2359304 | tf_op jit(solution)/shard_map/ppermute | solution.py:26
  34.1 24.7 %collective-permute-start.2 = (f32[128,3072]{1,0:T(8,128)S(1)}, f32[128,3072]{1,0:T(8,128)S(1)}, u32[]{:S(2)}, u32[]{:S(2)}) collective-permute-start(f32[128,3072]{1,0:T(8,128)S(1)} %constant_dynamic-update-slice_fusion.refs_0_), channel_id=1, source_target_pairs={{0,2},{1,3},{2,4},{3,5},{4,6},{5,7},{6,8},{7,9},{8,10},{9,11},{10,... | collective-permute-start | bytes 4718600 | tf_op jit(solution)/shard_map/ppermute | solution.py:26
  58.9 30.2 %copy-start = (f32[128,3072]{1,0:T(8,128)}, f32[128,3072]{1,0:T(8,128)S(1)}, u32[]{:S(2)}) copy-start(f32[128,3072]{1,0:T(8,128)S(1)} %collective-permute-done.2.refs_1_) | copy-start | bytes 4718596
  58.9 30.2 %collective-permute-start.5 = (f32[128,3072]{1,0:T(8,128)S(1)}, f32[128,3072]{1,0:T(8,128)}, u32[]{:S(2)}, u32[]{:S(2)}) collective-permute-start(f32[128,3072]{1,0:T(8,128)S(1)} %collective-permute-done.2.refs_1_), channel_id=1, source_target_pairs={{0,2},{1,3},{2,4},{3,5},{4,6},{5,7},{6,8},{7,9},{8,10},{9,11},{10,... | collective-permute-start | bytes 4718600 | tf_op jit(solution)/shard_map/ppermute | solution.py:26
  89.1 32.0 %collective-permute-start.8 = (f32[128,3072]{1,0:T(8,128)}, f32[128,3072]{1,0:T(8,128)}, u32[]{:S(2)}, u32[]{:S(2)}) collective-permute-start(f32[128,3072]{1,0:T(8,128)} %collective-permute-done.5.refs_2_), channel_id=1, source_target_pairs={{0,2},{1,3},{2,4},{3,5},{4,6},{5,7},{14,0},{15,1},{16,30},{17,31},... | collective-permute-start | bytes 4718600 | tf_op jit(solution)/shard_map/ppermute | solution.py:26
  92.9 9.1 %collective-permute-start.3 = (f32[64,512]{1,0:T(8,128)}, f32[64,512]{1,0:T(8,128)S(1)}, u32[]{:S(2)}, u32[]{:S(2)}) collective-permute-start(f32[64,512]{1,0:T(8,128)} %get-tuple-element.22), channel_id=1, source_target_pairs={{0,16},{16,32},{32,48},{48,64},{64,80},{80,96},{96,112},{112,128},... | collective-permute-start | bytes 393224 | tf_op jit(solution)/shard_map/ppermute | solution.py:32
  96.3 7.2 %copy-start.2 = (s32[512]{0:T(512)S(1)}, s32[512]{0:T(512)}, u32[]{:S(2)}) copy-start(s32[512]{0:T(512)} %low_s.1) | copy-start | bytes 6148
  96.3 7.2 %copy-start.3 = (s32[512]{0:T(512)S(1)}, s32[512]{0:T(512)}, u32[]{:S(2)}) copy-start(s32[512]{0:T(512)} %up_s.1) | copy-start | bytes 6148
  96.3 7.2 %copy-start.4 = (f32[6144,128]{1,0:T(8,128)S(1)}, f32[6144,128]{1,0:T(8,128)}, u32[]{:S(2)}) copy-start(f32[6144,128]{1,0:T(8,128)} %get-tuple-element.21.rows_ref) | copy-start | bytes 9437188
  96.3 7.2 %collective-permute-start.4 = (f32[64,512]{1,0:T(8,128)}, f32[64,512]{1,0:T(8,128)S(1)}, u32[]{:S(2)}, u32[]{:S(2)}) collective-permute-start(f32[64,512]{1,0:T(8,128)} %get-tuple-element.23), channel_id=1, source_target_pairs={{16,0},{32,16},{48,32},{64,48},{80,64},{96,80},{112,96},{128,112},... | collective-permute-start | bytes 393224 | tf_op jit(solution)/shard_map/ppermute | solution.py:32
  100.0 21.1 %collective-permute-start.7 = (f32[64,3072]{1,0:T(8,128)S(1)}, f32[64,3072]{1,0:T(8,128)S(1)}, u32[]{:S(2)}, u32[]{:S(2)}) collective-permute-start(f32[64,3072]{1,0:T(8,128)S(1)} %get-tuple-element.33), channel_id=1, source_target_pairs={{0,1},{1,0},{2,3},{3,2},{4,5},{5,4},{6,7},{7,6},{8,9},{9,8},{10,11... | collective-permute-start | bytes 2359304 | tf_op jit(solution)/shard_map/ppermute | solution.py:36
  103.5 17.6 %copy-start.1 = (f32[128,3072]{1,0:T(8,128)S(1)}, f32[128,3072]{1,0:T(8,128)}, u32[]{:S(2)}) copy-start(f32[128,3072]{1,0:T(8,128)} %copy-done) | copy-start | bytes 4718596
  144.3 13.8 %collective-permute-start.9 = (f32[32,128]{1,0:T(8,128)S(1)}, f32[32,128]{1,0:T(8,128)S(1)}, u32[]{:S(2)}, u32[]{:S(2)}) collective-permute-start(f32[32,128]{1,0:T(8,128)S(1)} %reduce_sum.9), channel_id=1, source_target_pairs={{0,0},{16,1},{32,2},{48,3},{64,4},{80,5},{96,6},{112,7},{128,8},{1... | collective-permute-start | bytes 49160 | tf_op jit(solution)/shard_map/ppermute | solution.py:41

commit v3 on v2

--- a/solution.py
+++ b/solution.py
@@ -47,10 +47,10 @@
     a_hbm, b_hbm, c_hbm, m_hbm, x_ref = refs[:5]
     del refs[:5]
     rows_in = None if first else refs.pop(0)
-    low_s, up_s = (refs.pop(0), refs.pop(0)) if last else (None, None)
+    half_s = refs.pop(0) if last else None
     rows_out = refs.pop(0)
-    y_out, low_out, up_out = (refs.pop(0), refs.pop(0), refs.pop(0)) if last else (None, None, None)
-    a_s, b_s, c_s, m_s, sems, *zs = refs
+    y_outs = (refs.pop(0), refs.pop(0)) if last else None
+    a_s, b_s, c_s, m_s, sems, sums, in_sem, out_sems, *zs = refs
     snaps, nodes = x_ref.shape
     tiles = LANES // 8
     width = 1 + parts
@@ -59,6 +59,9 @@
         copy = pltpu.make_async_copy(source.at[pl.ds(start, count)], target, sems.at[j])
         copy.start()
         copies.append(copy)
+    if not first:
+        earlier = pltpu.make_async_copy(rows_in, sums, in_sem)
+        earlier.start()
 
     def tile_of(block, i, part):
         return pl.ds(pl.multiple_of(block * (LANES * width) + (i * width + part) * 8, 8), 8)
@@ -97,7 +100,10 @@
 
     lax.fori_loop(0, count // (arrays * 2 * parts), elements, 0)
 
-    def finish(block, carry):
+    if not first:
+        earlier.wait()
+
+    def finish(block):
         totals = []
         for i in range(tiles):
             total = None
@@ -109,57 +115,77 @@
         total = jnp.concatenate(totals, axis=0)
         at = pl.multiple_of(block * LANES, LANES)
         if not first:
-            total = total + rows_in[pl.ds(at, LANES), :]
+            total = total + sums[pl.ds(at, LANES), :]
         if last:
             total = total * (1.0 / 12.0)
-            columns = total.T
-            y_out[:, pl.ds(at, LANES)] = columns[0:snaps, :] + columns[snaps:2 * snaps, :]
-        rows_out[pl.ds(at, LANES), :] = total
-        return carry
-
-    lax.fori_loop(0, nodes // LANES, finish, 0)
-    if not last:
-        return
+        sums[pl.ds(at, LANES), :] = total
+        return total
+
+    pieces = out_sems.shape[0]
+    size = nodes // pieces
+    writes = []
+    for piece in range(pieces):
+        blocks = size // LANES
+        begin = piece * blocks
+        side = None
+        if last:
+            side = piece // (pieces // 2)
+            begin = lax.rem(half_s[0] + side, 2) * (pieces // 2 * blocks) + piece % (pieces // 2) * blocks
+
+        def inner(i, carry, begin=begin, side=side, piece=piece):
+            total = finish(begin + i)
+            if last:
+                columns = total.T
+                at = pl.multiple_of((piece % (pieces // 2) * blocks + i) * LANES, LANES)
+                y_outs[side][:, pl.ds(at, LANES)] = columns[0:snaps, :] + columns[snaps:2 * snaps, :]
+            return carry
+
+        lax.fori_loop(0, blocks, inner, 0)
+        at = pl.multiple_of(begin * LANES, LANES) if last else begin * LANES
+        write = pltpu.make_async_copy(sums.at[pl.ds(at, size)], rows_out.at[pl.ds(at, size)], out_sems.at[piece])
+        write.start()
+        writes.append(write)
+    for write in writes:
+        write.wait()
+
+
+def gather_kernel(low_s, up_s, rows, low_out, up_out, taken):
+    snaps, shared = low_out.shape
     for list_s, out in ((low_s, low_out), (up_s, up_out)):
         def gather(i, carry, list_s=list_s):
             at = pl.multiple_of(i * 16, 16)
             for k in range(16):
-                zs[0][pl.ds(at + k, 1), :] = rows_out[pl.ds(list_s[at + k], 1), :]
+                taken[pl.ds(at + k, 1), :] = rows[pl.ds(list_s[at + k], 1), :]
             return carry
 
-        shared = out.shape[1]
         lax.fori_loop(0, shared // 16, gather, 0)
         for block in range(shared // LANES):
             at = block * LANES
-            columns = zs[0][at:at + LANES, :].T
+            columns = taken[at:at + LANES, :].T
             out[:, at:at + LANES] = columns[0:snaps, :] + columns[snaps:2 * snaps, :]
 
 
-def assemble_kernel(low_s, up_s, rows_ref, below_ref, above_ref, out_ref, rows, taken):
+def assemble_kernel(low_s, up_s, rows_ref, below_ref, above_ref, out_ref, rows, below, above, sem):
     snaps, shared = below_ref.shape
     nodes = rows_ref.shape[0]
-
-    def copy(i, carry):
-        at = pl.multiple_of(i * LANES, LANES)
-        rows[pl.ds(at, LANES), :] = rows_ref[pl.ds(at, LANES), :]
-        return carry
-
-    lax.fori_loop(0, nodes // LANES, copy, 0)
-    for list_s, received in ((low_s, below_ref), (up_s, above_ref)):
+    copy = pltpu.make_async_copy(rows_ref, rows, sem)
+    copy.start()
+    for received, taken in ((below_ref, below), (above_ref, above)):
         for block in range(shared // LANES):
             at = block * LANES
             value = received[:, at:at + LANES]
             taken[at:at + LANES, :] = jnp.concatenate([value, jnp.zeros_like(value)], axis=0).T
-
-        def add(i, carry, list_s=list_s):
-            at = pl.multiple_of(i * 8, 8)
-            nodes_of = [list_s[at + k] for k in range(8)]
+    copy.wait()
+    for list_s, taken in ((low_s, below), (up_s, above)):
+        def add(i, carry, list_s=list_s, taken=taken):
+            at = pl.multiple_of(i * 16, 16)
+            nodes_of = [list_s[at + k] for k in range(16)]
             new = [rows[pl.ds(n, 1), :] + taken[pl.ds(at + k, 1), :] for k, n in enumerate(nodes_of)]
             for n, value in zip(nodes_of, new):
                 rows[pl.ds(n, 1), :] = value
             return carry
 
-        lax.fori_loop(0, shared // 8, add, 0)
+        lax.fori_loop(0, shared // 16, add, 0)
 
     def write(i, carry):
         at = pl.multiple_of(i * LANES, LANES)
@@ -182,24 +208,23 @@
 ARRAYS, PARTS = 4, 2
 
 
-def apply_call(index, calls, columns, snapshots, rows, lists):
+def apply_call(index, calls, columns, snapshots, rows, half):
     first, last = index == 0, index == calls - 1
     snaps, nodes = snapshots.shape
     count = columns[0].shape[0] // calls
-    shared = lists[0].shape[0]
     row_shape = jax.ShapeDtypeStruct((nodes, LANES), jnp.float32)
-    side = jax.ShapeDtypeStruct((snaps, shared), jnp.float32)
-    whole = jax.ShapeDtypeStruct((snaps, nodes), jnp.float32)
-    operands = columns + (snapshots,) + (() if first else (rows,)) + (lists if last else ())
+    side = jax.ShapeDtypeStruct((snaps, nodes // 2), jnp.float32)
+    operands = columns + (snapshots,) + (() if first else (rows,)) + ((half,) if last else ())
     return pl.pallas_call(
         functools.partial(apply_kernel, first, last, index * count, count, ARRAYS, PARTS),
-        out_shape=[row_shape] + ([whole, side, side] if last else []),
-        in_specs=[ANYWHERE] * 4 + [IN_VMEM] + ([] if first else [IN_VMEM]) + ([IN_SMEM] * 2 if last else []),
-        out_specs=[IN_VMEM] + ([IN_VMEM] * 3 if last else []),
+        out_shape=[row_shape] + ([side, side] if last else []),
+        in_specs=[ANYWHERE] * 4 + [IN_VMEM] + ([] if first else [ANYWHERE]) + ([IN_SMEM] if last else []),
+        out_specs=[ANYWHERE] + ([IN_VMEM] * 2 if last else []),
         scratch_shapes=[pltpu.SMEM((count,), jnp.int32)] * 3
         + [pltpu.SMEM((count,), jnp.float32), pltpu.SemaphoreType.DMA((4,))]
+        + [pltpu.VMEM((nodes, LANES), jnp.float32), pltpu.SemaphoreType.DMA, pltpu.SemaphoreType.DMA((4,))]
         + [pltpu.VMEM((nodes * (1 + PARTS), LANES), jnp.float32)] * ARRAYS,
-        compiler_params=pltpu.CompilerParams(vmem_limit_bytes=56 * MIB),
+        compiler_params=pltpu.CompilerParams(vmem_limit_bytes=52 * MIB),
         cost_estimate=cost(20),
     )(*operands)
 
@@ -284,35 +309,44 @@
 
     spread = (connectivity >> 3) * (8 * (1 + PARTS)) + (connectivity & 7)
     columns = tuple(spread[k] for k in range(3)) + (element_mass,)
-    lists = (lower_shared, upper_shared)
-    (rows,) = apply_call(0, 3, columns, snapshots, None, lists)
+    half_at = jnp.reshape(h, (1,)).astype(jnp.int32)
+    (rows,) = apply_call(0, 3, columns, snapshots, None, half_at)
 
     rows, a1, b1 = tied((rows, a1, b1))
     pair1 = jnp.concatenate([a1, b1], axis=0)
     pair2 = ring_hop(pair1, 1)
-    (rows,) = apply_call(1, 3, columns, snapshots, rows, lists)
+    (rows,) = apply_call(1, 3, columns, snapshots, rows, half_at)
 
     rows, pair2 = tied((rows, pair2))
     pair3 = ring_hop(pair2, 1)
     b0 = partner(given)
-    rows, partial, low, high = apply_call(2, 3, columns, snapshots, rows, lists)
-
-    partial, pair3, b0 = tied((partial, pair3, b0))
-    y_own = lax.dynamic_slice_in_dim(partial, h * half, half, 1)
-    y_theirs = partner(lax.dynamic_slice_in_dim(partial, (1 - h) * half, half, 1))
+    rows, y_own, y_given = apply_call(2, 3, columns, snapshots, rows, half_at)
+
+    y_given, pair3, b0 = tied((y_given, pair3, b0))
+    y_theirs = partner(y_given)
     pair4 = ring_hop(pair3, 1, closing=True)
 
+    shared = lower_shared.shape[0]
+    low, high = pl.pallas_call(
+        gather_kernel,
+        out_shape=[jax.ShapeDtypeStruct((snaps, shared), jnp.float32)] * 2,
+        in_specs=[IN_SMEM] * 2 + [IN_VMEM],
+        out_specs=[IN_VMEM] * 2,
+        scratch_shapes=[pltpu.VMEM((shared, LANES), jnp.float32)],
+        compiler_params=pltpu.CompilerParams(vmem_limit_bytes=12 * MIB),
+        cost_estimate=cost(0.01),
+    )(lower_shared, upper_shared, rows)
     from_below = passed_along(high, "mesh", 1)
     from_above = passed_along(low, "mesh", -1)
-    shared = lower_shared.shape[0]
     weighted = pl.pallas_call(
         assemble_kernel,
         out_shape=jax.ShapeDtypeStruct((snaps, nodes), jnp.float32),
-        in_specs=[IN_SMEM] * 2 + [IN_VMEM] * 3,
+        in_specs=[IN_SMEM] * 2 + [ANYWHERE] + [IN_VMEM] * 2,
         out_specs=IN_VMEM,
-        scratch_shapes=[pltpu.VMEM((nodes, LANES), jnp.float32), pltpu.VMEM((shared, LANES), jnp.float32)],
+        scratch_shapes=[pltpu.VMEM((nodes, LANES), jnp.float32)] + [pltpu.VMEM((shared, LANES), jnp.float32)] * 2
+        + [pltpu.SemaphoreType.DMA],
         compiler_params=pltpu.CompilerParams(vmem_limit_bytes=20 * MIB),
-        cost_estimate=cost(8),
+        cost_estimate=cost(0.01),
     )(lower_shared, upper_shared, rows, from_below, from_above)
     weighted, y_theirs, pair4 = tied((weighted, y_theirs, pair4))
 

time: 159 us -> 158 us (level)
  Pallas kernels: 88 us -> 82.7 us
  waiting for transfers between devices: 17.5 us -> 21 us
  blocking collectives: 17.4 us -> 15.7 us
    ppermute x2, waiting for transfers between devices: 1.48 us -> 10.7 us  [passed_along(): lax.ppermute(value, axis, [(source, source + steps) for source in range(l...]
    ppermute x2, waiting for transfers between devices: 8.69 us -> 0.01 us  [partner(): lax.ppermute(value, 'snap', [(i, i ^ 1) for i in range(lax.axis_size('sna...]
    pallas_call x3, Pallas kernels: 73.4 us -> 65.7 us  [apply_call(): pl.pallas_call(functools.partial(apply_kernel, first, last, index * count...]
    ppermute x2, starting transfers between devices: 1.97 us -> 5.91 us  [partner(): lax.ppermute(value, 'snap', [(i, i ^ 1) for i in range(lax.axis_size('sna...]
    unnamed x13 -> x35, local copies, waits for them, and re-layouts: 0.08 us -> 3.13 us
    pallas_call x0 -> x1, Pallas kernels: none -> 2.63 us  [on_device(): pl.pallas_call(gather_kernel, out_shape=[jax.ShapeDtypeStruct((snaps, sha...]
    ppermute x1, starting transfers between devices: 6.34 us -> 4.27 us  [mirrored(): lax.ppermute(value, ('mesh', 'snap'), [(s * count + m, m * count + s) for...]
    ppermute x1, waiting for transfers between devices: 7.33 us -> 9.33 us  [mirrored(): lax.ppermute(value, ('mesh', 'snap'), [(s * count + m, m * count + s) for...]
  transfers between devices with their start and end apart: 10 -> 10, of which waited for: 3 -> 4; matrix products, arithmetic and copies ran while one was open for 2% -> 0% of each run, Pallas kernels for 52% -> 49%
where the time goes in v3:
time: 158 us; the launch traced here: 157 us
  Pallas kernels  82.7 us (52%)
  starting transfers between devices  31 us (20%)
  waiting for transfers between devices  21 us (13%)
  blocking collectives  15.7 us (10%)
  local copies, waits for them, and re-layouts  5.12 us (3%)
    pallas_call x3, Pallas kernels, apply_call(): pl.pallas_call(functools.partial(apply_kernel, first, last, index * count...  65.7 us
    all_to_all x1, blocking collectives, on_device(): lax.all_to_all(tiles, ('mesh', 'snap'), 0, 0, axis_index_groups=planes, t...  15.7 us
    ppermute x5, starting transfers between devices, ring_hop(): return lax.ppermute(value, ('mesh', 'snap'), pairs)  14.9 us
    ppermute x2, waiting for transfers between devices, passed_along(): lax.ppermute(value, axis, [(source, source + steps) for source in range(l...  10.7 us
    ppermute x1, waiting for transfers between devices, mirrored(): lax.ppermute(value, ('mesh', 'snap'), [(s * count + m, m * count + s) for...  9.33 us
    pallas_call x1, Pallas kernels, on_device(): pl.pallas_call(assemble_kernel, out_shape=jax.ShapeDtypeStruct((snaps, no...  8.66 us
    ppermute x2, starting transfers between devices, passed_along(): lax.ppermute(value, axis, [(source, source + steps) for source in range(l...  5.94 us
    ppermute x2, starting transfers between devices, partner(): lax.ppermute(value, 'snap', [(i, i ^ 1) for i in range(lax.axis_size('sna...  5.91 us
  transfers between devices with their start and end apart: 10, of which 4 were waited for; matrix products, arithmetic and copies ran while one was open for 0% of the time, Pallas kernels for 49%

profile of v3, /device:TPU:5, one launch (start us, length us, event | category | flops | bytes accessed | tf_op | source)
XLA Modules:
  0.0 157.3 jit_solution(274860116138950229)
XLA Ops:
  0.7 1.6 %constant_dynamic-slice_fusion = (f32[64,3072]{1,0:T(8,128)S(1)}, f32[64,3072]{1,0:T(8,128)S(1)}) fusion(f32[64,6144]{1,0:T(8,128)} %refs_4_.5, s32[]{:T(128)S(6)} %select_n.27, s32[]{:T(128)S(6)} %select_n.26), kind=kLoop, calls=%fused_computation.7 | loop fusion | bytes 3145736 | tf_op jit(solution)/shard_map/dynamic_slice | solution.py:306
  2.3 3.0 %collective-permute-start.6 = (f32[64,3072]{1,0:T(8,128)S(1)}, f32[64,3072]{1,0:T(8,128)S(1)}, u32[]{:S(2)}, u32[]{:S(2)}) collective-permute-start(f32[64,3072]{1,0:T(8,128)S(1)} %get-tuple-element.34), channel_id=1, source_target_pairs={{0,1},{1,0},{2,3},{3,2},{4,5},{5,4},{6,7},{7,6},{8,9},{9,8},{10,11... | collective-permute-start | bytes 2359304 | tf_op jit(solution)/shard_map/ppermute | solution.py:36
  5.3 5.4 %collective-permute-start.1 = (f32[64,3072]{1,0:T(8,128)S(1)}, f32[64,3072]{1,0:T(8,128)S(1)}, u32[]{:S(2)}, u32[]{:S(2)}) collective-permute-start(f32[64,3072]{1,0:T(8,128)S(1)} %get-tuple-element.34), channel_id=1, source_target_pairs={{0,3},{1,2},{2,5},{3,4},{4,7},{5,6},{6,9},{7,8},{8,11},{9,10},{10,... | collective-permute-start | bytes 2359304 | tf_op jit(solution)/shard_map/ppermute | solution.py:26
  10.7 0.7 collective-permute-start
  11.4 0.1 and_add_fusion
  11.5 0.1 fusion.1
  11.6 19.7 %shard_map.68.refs_5_ = f32[6144,128]{1,0:T(8,128)} custom-call(s32[12288]{0:T(1024)S(1)} %bitcast.14, s32[12288]{0:T(1024)S(1)} %bitcast.11, s32[12288]{0:T(1024)S(1)} %bitcast.8, f32[12288]{0:T(1024)S(1)} %copy-done.13, f32[64,6144]{1,0:T(8,128)S(1)} %copy-done.2), custom_call_target="tpu_custom_call" | custom-call | flops 20000000000 | bytes 60000000 | tf_op jit(solution)/shard_map/pallas_call | solution.py:218
  31.4 0.9 collective-permute-done
  32.4 0.1 constant_dynamic-update-slice_fusion.refs_0_
  32.5 3.5 %collective-permute-start.2 = (f32[128,3072]{1,0:T(8,128)S(1)}, f32[128,3072]{1,0:T(8,128)S(1)}, u32[]{:S(2)}, u32[]{:S(2)}) collective-permute-start(f32[128,3072]{1,0:T(8,128)S(1)} %constant_dynamic-update-slice_fusion.refs_0_), channel_id=1, source_target_pairs={{0,2},{1,3},{2,4},{3,5},{4,6},{5,7},{6,8},{7,9},{8,10},{9,11},{10,... | collective-permute-start | bytes 4718600 | tf_op jit(solution)/shard_map/ppermute | solution.py:26
  36.0 20.1 %shard_map.69.refs_5_ = f32[6144,128]{1,0:T(8,128)} custom-call(s32[12288]{0:T(1024)S(1)} %bitcast.15, s32[12288]{0:T(1024)S(1)} %bitcast.12, s32[12288]{0:T(1024)S(1)} %bitcast.9, f32[12288]{0:T(1024)S(1)} %copy-done.13, f32[64,6144]{1,0:T(8,128)S(1)} %copy-done.2, f32[6144,128]{1,0:T(8,128)} %shard_map.68.refs_5_), custom_call_target="tpu_custom_call" | custom-call | flops 20000000000 | bytes 60000000 | tf_op jit(solution)/shard_map/pallas_call | solution.py:218
  56.0 1.5 collective-permute-start.5
  57.5 25.9 %shard_map.70 = (f32[6144,128]{1,0:T(8,128)}, f32[64,3072]{1,0:T(8,128)S(1)}, f32[64,3072]{1,0:T(8,128)}) custom-call(s32[12288]{0:T(1024)S(1)} %bitcast.16, s32[12288]{0:T(1024)S(1)} %bitcast.13, s32[12288]{0:T(1024)S(1)} %bitcast.10, f32[12288]{0:T(1024)S(1)} %copy-done.13, f32[64,6144]{1,0:T(8,128)} %refs_4_.5, f32[6144,128]{1,0:T(8,128)} %shard_map.69.refs_5_, ...), custom_call_target="tpu_custom_call" | custom-call | flops 20000000000 | bytes 60000000 | tf_op jit(solution)/shard_map/pallas_call | solution.py:218
  83.5 3.8 %collective-permute-start.8 = (f32[128,3072]{1,0:T(8,128)}, f32[128,3072]{1,0:T(8,128)}, u32[]{:S(2)}, u32[]{:S(2)}) collective-permute-start(f32[128,3072]{1,0:T(8,128)} %collective-permute-done.5.refs_2_), channel_id=1, source_target_pairs={{0,2},{1,3},{2,4},{3,5},{4,6},{5,7},{14,0},{15,1},{16,30},{17,31},... | collective-permute-start | bytes 4718600 | tf_op jit(solution)/shard_map/ppermute | solution.py:26
  87.3 2.9 %collective-permute-start.7 = (f32[64,3072]{1,0:T(8,128)}, f32[64,3072]{1,0:T(8,128)}, u32[]{:S(2)}, u32[]{:S(2)}) collective-permute-start(f32[64,3072]{1,0:T(8,128)} %get-tuple-element.27), channel_id=1, source_target_pairs={{0,1},{1,0},{2,3},{3,2},{4,5},{5,4},{6,7},{7,6},{8,9},{9,8},{10,11... | collective-permute-start | bytes 2359304 | tf_op jit(solution)/shard_map/ppermute | solution.py:36
  90.3 1.9 %copy-done = f32[6144,128]{1,0:T(8,128)S(1)} copy-done((f32[6144,128]{1,0:T(8,128)S(1)}, f32[6144,128]{1,0:T(8,128)}, u32[]{:S(2)}) %copy-start) | copy-done | bytes 3145752
  92.1 2.6 %shard_map.71 = (f32[64,512]{1,0:T(8,128)S(1)}, f32[64,512]{1,0:T(8,128)}) custom-call(s32[512]{0:T(512)S(1)} %copy-done.7, s32[512]{0:T(512)S(1)} %copy-done.8, f32[6144,128]{1,0:T(8,128)S(1)} %copy-done), custom_call_target="tpu_custom_call" | custom-call | flops 10000000 | bytes 30000 | tf_op jit(solution)/shard_map/pallas_call | solution.py:330
  94.8 4.0 %collective-permute-start.3 = (f32[64,512]{1,0:T(8,128)}, f32[64,512]{1,0:T(8,128)S(1)}, u32[]{:S(2)}, u32[]{:S(2)}) collective-permute-start(f32[64,512]{1,0:T(8,128)} %get-tuple-element.23), channel_id=1, source_target_pairs={{0,16},{16,32},{32,48},{48,64},{64,80},{80,96},{96,112},{112,128},... | collective-permute-start | bytes 393224 | tf_op jit(solution)/shard_map/ppermute | solution.py:32
  98.8 1.9 %collective-permute-start.4 = (f32[64,512]{1,0:T(8,128)S(1)}, f32[64,512]{1,0:T(8,128)S(1)}, u32[]{:S(2)}, u32[]{:S(2)}) collective-permute-start(f32[64,512]{1,0:T(8,128)S(1)} %get-tuple-element.24), channel_id=1, source_target_pairs={{16,0},{32,16},{48,32},{64,48},{80,64},{96,80},{112,96},{128,112},... | collective-permute-start | bytes 393224 | tf_op jit(solution)/shard_map/ppermute | solution.py:32
  100.8 0.1 pad_add_fusion.place
  100.9 9.2 %collective-permute-done.3.below_ref = f32[64,512]{1,0:T(8,128)S(1)} collective-permute-done((f32[64,512]{1,0:T(8,128)}, f32[64,512]{1,0:T(8,128)S(1)}, u32[]{:S(2)}, u32[]{:S(2)}) %collective-permute-start.3) | collective-permute-done | bytes 131104 | tf_op jit(solution)/shard_map/ppermute | solution.py:32
  110.0 1.5 collective-permute-done.4.above_ref
  111.5 8.7 %shard_map.72 = f32[64,6144]{1,0:T(8,128)} custom-call(s32[512]{0:T(512)S(1)} %copy-done.7, s32[512]{0:T(512)S(1)} %copy-done.8, f32[6144,128]{1,0:T(8,128)S(1)} %copy-done.1, f32[64,512]{1,0:T(8,128)S(1)} %collective-permute-done.3.below_ref, f32[64,512]{1,0:T(8,128)S(1)} %collective-permute-done.4.above_ref), custom_call_target="tpu_custom_call" | custom-call | flops 10000000 | bytes 30000 | tf_op jit(solution)/shard_map/pallas_call | solution.py:341
  120.3 1.1 copy-done.15
  121.4 5.7 %shard_map.73 = f32[32,32,128]{2,1,0:T(8,128)S(1)} custom-call(s32[3]{0:T(128)S(1)} %pad_add_fusion.place, f32[64,3072]{1,0:T(8,128)S(1)} %copy-done.15, f32[64,3072]{1,0:T(8,128)} %collective-permute-done.7.yb_ref, f32[64,3072]{1,0:T(8,128)S(1)} %copy-done.4, f32[64,3072]{1,0:T(8,128)S(1)} %copy-done.12, f32[128,3072]{1,0:T(8,128)S(1)} %copy-done.6, ...), custom_call_target="tpu_custom_call" | custom-call | flops 8000000000 | bytes 24000000 | tf_op jit(solution)/shard_map/pallas_call | solution.py:282
  127.1 15.7 %all_to_all.5 = f32[32,32,128]{2,1,0:T(8,128)S(1)} all-to-all(f32[32,32,128]{2,1,0:T(8,128)S(1)} %shard_map.73), channel_id=1, replica_groups={{0,1,16,17,32,33,48,49,64,65,80,81,96,97,112,113,128,129,144,145,160,16..., dimensions={0} | all-to-all | bytes 1048576 | tf_op jit(solution)/shard_map/all_to_all | solution.py:356
  142.8 4.3 %collective-permute-start.9 = (f32[32,128]{1,0:T(8,128)S(1)}, f32[32,128]{1,0:T(8,128)S(1)}, u32[]{:S(2)}, u32[]{:S(2)}) collective-permute-start(f32[32,128]{1,0:T(8,128)S(1)} %reduce_sum.9), channel_id=1, source_target_pairs={{0,0},{16,1},{32,2},{48,3},{64,4},{80,5},{96,6},{112,7},{128,8},{1... | collective-permute-start | bytes 49160 | tf_op jit(solution)/shard_map/ppermute | solution.py:41
  147.1 0.1 fusion.3
  147.2 0.1 copy.7
  147.2 9.3 %collective-permute-done.9 = f32[32,128]{1,0:T(8,128)S(1)} collective-permute-done((f32[32,128]{1,0:T(8,128)S(1)}, f32[32,128]{1,0:T(8,128)S(1)}, u32[]{:S(2)}, u32[]{:S(2)}) %collective-permute-start.9) | collective-permute-done | bytes 16416 | tf_op jit(solution)/shard_map/ppermute | solution.py:41
  156.6 0.1 fusion.2
  156.7 0.6 fusion
  (41 shorter events, 0.2 us)
Async XLA Ops:
  0.7 10.8 %copy-start.16 = (s32[3,12288]{1,0:T(4,128)S(1)}, s32[3,12288]{1,0:T(4,128)}, u32[]{:S(2)}) copy-start(s32[3,12288]{1,0:T(4,128)} %param.6) | copy-start | bytes 442372
  0.7 10.9 %copy-start.2 = (f32[64,6144]{1,0:T(8,128)S(1)}, f32[64,6144]{1,0:T(8,128)}, u32[]{:S(2)}) copy-start(f32[64,6144]{1,0:T(8,128)} %refs_4_.5) | copy-start | bytes 4718596
  0.7 10.9 %copy-start.13 = (f32[12288]{0:T(1024)S(1)}, f32[12288]{0:T(1024)}, u32[]{:S(2)}) copy-start(f32[12288]{0:T(1024)} %refs_3_.5) | copy-start | bytes 147460
  2.3 29.1 %copy-start.3 = (f32[64,3072]{1,0:T(8,128)}, f32[64,3072]{1,0:T(8,128)S(1)}, u32[]{:S(2)}) copy-start(f32[64,3072]{1,0:T(8,128)S(1)} %get-tuple-element.35.a0_ref) | copy-start | bytes 2359300
  2.3 81.2 %collective-permute-start.6 = (f32[64,3072]{1,0:T(8,128)S(1)}, f32[64,3072]{1,0:T(8,128)S(1)}, u32[]{:S(2)}, u32[]{:S(2)}) collective-permute-start(f32[64,3072]{1,0:T(8,128)S(1)} %get-tuple-element.34), channel_id=1, source_target_pairs={{0,1},{1,0},{2,3},{3,2},{4,5},{5,4},{6,7},{7,6},{8,9},{9,8},{10,11... | collective-permute-start | bytes 2359304 | tf_op jit(solution)/shard_map/ppermute | solution.py:36
  5.3 26.1 %collective-permute-start.1 = (f32[64,3072]{1,0:T(8,128)S(1)}, f32[64,3072]{1,0:T(8,128)S(1)}, u32[]{:S(2)}, u32[]{:S(2)}) collective-permute-start(f32[64,3072]{1,0:T(8,128)S(1)} %get-tuple-element.34), channel_id=1, source_target_pairs={{0,3},{1,2},{2,5},{3,4},{4,7},{5,6},{6,9},{7,8},{8,11},{9,10},{10,... | collective-permute-start | bytes 2359304 | tf_op jit(solution)/shard_map/ppermute | solution.py:26
  10.7 21.6 %collective-permute-start = (f32[64,3072]{1,0:T(8,128)S(1)}, f32[64,3072]{1,0:T(8,128)S(1)}, u32[]{:S(2)}, u32[]{:S(2)}) collective-permute-start(f32[64,3072]{1,0:T(8,128)S(1)} %get-tuple-element.35.a0_ref), channel_id=1, source_target_pairs={{0,2},{1,3},{2,4},{3,5},{4,6},{5,7},{6,8},{7,9},{8,10},{9,11},{10,... | collective-permute-start | bytes 2359304 | tf_op jit(solution)/shard_map/ppermute | solution.py:26
  32.5 23.6 %copy-start.5 = (f32[128,3072]{1,0:T(8,128)}, f32[128,3072]{1,0:T(8,128)S(1)}, u32[]{:S(2)}) copy-start(f32[128,3072]{1,0:T(8,128)S(1)} %constant_dynamic-update-slice_fusion.refs_0_) | copy-start | bytes 4718596
  32.5 23.6 %collective-permute-start.2 = (f32[128,3072]{1,0:T(8,128)S(1)}, f32[128,3072]{1,0:T(8,128)S(1)}, u32[]{:S(2)}, u32[]{:S(2)}) collective-permute-start(f32[128,3072]{1,0:T(8,128)S(1)} %constant_dynamic-update-slice_fusion.refs_0_), channel_id=1, source_target_pairs={{0,2},{1,3},{2,4},{3,5},{4,6},{5,7},{6,8},{7,9},{8,10},{9,11},{10,... | collective-permute-start | bytes 4718600 | tf_op jit(solution)/shard_map/ppermute | solution.py:26
  56.0 27.4 %copy-start.9 = (f32[128,3072]{1,0:T(8,128)}, f32[128,3072]{1,0:T(8,128)S(1)}, u32[]{:S(2)}) copy-start(f32[128,3072]{1,0:T(8,128)S(1)} %collective-permute-done.2.refs_1_) | copy-start | bytes 4718596
  56.0 27.5 %collective-permute-start.5 = (f32[128,3072]{1,0:T(8,128)S(1)}, f32[128,3072]{1,0:T(8,128)}, u32[]{:S(2)}, u32[]{:S(2)}) collective-permute-start(f32[128,3072]{1,0:T(8,128)S(1)} %collective-permute-done.2.refs_1_), channel_id=1, source_target_pairs={{0,2},{1,3},{2,4},{3,5},{4,6},{5,7},{6,8},{7,9},{8,10},{9,11},{10,... | collective-permute-start | bytes 4718600 | tf_op jit(solution)/shard_map/ppermute | solution.py:26
  57.5 32.7 %copy-start.7 = (s32[512]{0:T(512)S(1)}, s32[512]{0:T(512)}, u32[]{:S(2)}) copy-start(s32[512]{0:T(512)} %low_s.3) | copy-start | bytes 6148
  57.5 32.7 %copy-start.8 = (s32[512]{0:T(512)S(1)}, s32[512]{0:T(512)}, u32[]{:S(2)}) copy-start(s32[512]{0:T(512)} %up_s.3) | copy-start | bytes 6148
  83.5 11.3 %copy-start.14 = (f32[64,3072]{1,0:T(8,128)}, f32[64,3072]{1,0:T(8,128)S(1)}, u32[]{:S(2)}) copy-start(f32[64,3072]{1,0:T(8,128)S(1)} %get-tuple-element.30.ya_ref) | copy-start | bytes 2359300
  83.5 11.3 %copy-start.11 = (f32[64,3072]{1,0:T(8,128)}, f32[64,3072]{1,0:T(8,128)S(1)}, u32[]{:S(2)}) copy-start(f32[64,3072]{1,0:T(8,128)S(1)} %collective-permute-done.6.b0_ref) | copy-start | bytes 2359300
  83.5 36.7 %collective-permute-start.8 = (f32[128,3072]{1,0:T(8,128)}, f32[128,3072]{1,0:T(8,128)}, u32[]{:S(2)}, u32[]{:S(2)}) collective-permute-start(f32[128,3072]{1,0:T(8,128)} %collective-permute-done.5.refs_2_), channel_id=1, source_target_pairs={{0,2},{1,3},{2,4},{3,5},{4,6},{5,7},{14,0},{15,1},{16,30},{17,31},... | collective-permute-start | bytes 4718600 | tf_op jit(solution)/shard_map/ppermute | solution.py:26
  87.3 32.9 %collective-permute-start.7 = (f32[64,3072]{1,0:T(8,128)}, f32[64,3072]{1,0:T(8,128)}, u32[]{:S(2)}, u32[]{:S(2)}) collective-permute-start(f32[64,3072]{1,0:T(8,128)} %get-tuple-element.27), channel_id=1, source_target_pairs={{0,1},{1,0},{2,3},{3,2},{4,5},{5,4},{6,7},{7,6},{8,9},{9,8},{10,11... | collective-permute-start | bytes 2359304 | tf_op jit(solution)/shard_map/ppermute | solution.py:36
  90.2 1.9 %copy-start = (f32[6144,128]{1,0:T(8,128)S(1)}, f32[6144,128]{1,0:T(8,128)}, u32[]{:S(2)}) copy-start(f32[6144,128]{1,0:T(8,128)} %get-tuple-element.22.rows.rows_ref) | copy-start | bytes 9437188
  92.1 19.4 %copy-start.1 = (f32[6144,128]{1,0:T(8,128)S(1)}, f32[6144,128]{1,0:T(8,128)}, u32[]{:S(2)}) copy-start(f32[6144,128]{1,0:T(8,128)} %get-tuple-element.22.rows.rows_ref) | copy-start | bytes 9437188
  94.8 15.3 %collective-permute-start.3 = (f32[64,512]{1,0:T(8,128)}, f32[64,512]{1,0:T(8,128)S(1)}, u32[]{:S(2)}, u32[]{:S(2)}) collective-permute-start(f32[64,512]{1,0:T(8,128)} %get-tuple-element.23), channel_id=1, source_target_pairs={{0,16},{16,32},{32,48},{48,64},{64,80},{80,96},{96,112},{112,128},... | collective-permute-start | bytes 393224 | tf_op jit(solution)/shard_map/ppermute | solution.py:32
  98.8 12.7 %collective-permute-start.4 = (f32[64,512]{1,0:T(8,128)S(1)}, f32[64,512]{1,0:T(8,128)S(1)}, u32[]{:S(2)}, u32[]{:S(2)}) collective-permute-start(f32[64,512]{1,0:T(8,128)S(1)} %get-tuple-element.24), channel_id=1, source_target_pairs={{16,0},{32,16},{48,32},{64,48},{80,64},{96,80},{112,96},{128,112},... | collective-permute-start | bytes 393224 | tf_op jit(solution)/shard_map/ppermute | solution.py:32
  100.8 19.4 %copy-start.4 = (f32[64,3072]{1,0:T(8,128)S(1)}, f32[64,3072]{1,0:T(8,128)}, u32[]{:S(2)}) copy-start(f32[64,3072]{1,0:T(8,128)} %copy-done.3) | copy-start | bytes 2359300
  100.8 19.4 %copy-start.6 = (f32[128,3072]{1,0:T(8,128)S(1)}, f32[128,3072]{1,0:T(8,128)}, u32[]{:S(2)}) copy-start(f32[128,3072]{1,0:T(8,128)} %copy-done.5) | copy-start | bytes 4718596
  100.8 19.4 %copy-start.10 = (f32[128,3072]{1,0:T(8,128)S(1)}, f32[128,3072]{1,0:T(8,128)}, u32[]{:S(2)}) copy-start(f32[128,3072]{1,0:T(8,128)} %copy-done.9) | copy-start | bytes 4718596
  100.8 19.4 %copy-start.12 = (f32[64,3072]{1,0:T(8,128)S(1)}, f32[64,3072]{1,0:T(8,128)}, u32[]{:S(2)}) copy-start(f32[64,3072]{1,0:T(8,128)} %copy-done.11) | copy-start | bytes 2359300
  120.3 1.1 copy-start.15
  142.8 13.8 %collective-permute-start.9 = (f32[32,128]{1,0:T(8,128)S(1)}, f32[32,128]{1,0:T(8,128)S(1)}, u32[]{:S(2)}, u32[]{:S(2)}) collective-permute-start(f32[32,128]{1,0:T(8,128)S(1)} %reduce_sum.9), channel_id=1, source_target_pairs={{0,0},{16,1},{32,2},{48,3},{64,4},{80,5},{96,6},{112,7},{128,8},{1... | collective-permute-start | bytes 49160 | tf_op jit(solution)/shard_map/ppermute | solution.py:41

commit v4 on v3

--- a/solution.py
+++ b/solution.py
@@ -77,7 +77,7 @@
                     z[tile_of(block, i, 1 + part), :] = blank
         return carry
 
-    lax.fori_loop(0, nodes // LANES, prepare, 0)
+    lax.fori_loop(0, nodes // LANES, prepare, 0, unroll=2)
     for copy in copies:
         copy.wait()
 
@@ -140,7 +140,7 @@
                 y_outs[side][:, pl.ds(at, LANES)] = columns[0:snaps, :] + columns[snaps:2 * snaps, :]
             return carry
 
-        lax.fori_loop(0, blocks, inner, 0)
+        lax.fori_loop(0, blocks, inner, 0, unroll=2)
         at = pl.multiple_of(begin * LANES, LANES) if last else begin * LANES
         write = pltpu.make_async_copy(sums.at[pl.ds(at, size)], rows_out.at[pl.ds(at, size)], out_sems.at[piece])
         write.start()
@@ -193,7 +193,7 @@
         out_ref[:, pl.ds(at, LANES)] = columns[0:snaps, :] + columns[snaps:2 * snaps, :]
         return carry
 
-    lax.fori_loop(0, nodes // LANES, write, 0)
+    lax.fori_loop(0, nodes // LANES, write, 0, unroll=4)
 
 
 ANYWHERE = pl.BlockSpec(memory_space=pl.ANY)
@@ -229,13 +229,6 @@
     )(*operands)
 
 
-def split3(left, right):
-    dims = (((1,), (1,)), ((), ()))
-    dot = functools.partial(lax.dot_general, dimension_numbers=dims, preferred_element_type=jnp.float32)
-    (l_hi, l_lo), (r_hi, r_lo) = left, right
-    return dot(l_hi, r_hi) + (dot(l_hi, r_lo) + dot(l_lo, r_hi))
-
-
 def halves_of(value):
     high = value.astype(jnp.bfloat16)
     return high, (value - high.astype(jnp.float32)).astype(jnp.bfloat16)
@@ -253,16 +246,18 @@
     def _():
         sums[...] = jnp.zeros_like(sums)
 
-    y = halves_of(jnp.concatenate([ya_ref[...], yb_ref[...]], axis=0))
-    sums[0] += split3(halves_of(jnp.concatenate([a0_ref[...], b0_ref[...]], axis=0)), y)
-    for distance, stream in enumerate(streams, 1):
-        sums[distance] += split3(halves_of(stream[...]), y)
+    y_high, y_low = halves_of(jnp.concatenate([ya_ref[...], yb_ref[...]], axis=0))
+    high, low_part = halves_of(jnp.concatenate([a0_ref[...], b0_ref[...]] + [stream[...] for stream in streams], axis=0))
+    dot = functools.partial(lax.dot_general, dimension_numbers=(((1,), (1,)), ((), ())),
+                            preferred_element_type=jnp.float32)
+    both = dot(high, jnp.concatenate([y_high, y_low], axis=0))
+    sums[...] += both[:, :2 * snaps] + (both[:, 2 * snaps:] + dot(low_part, y_high))
 
     @pl.when(step == pl.num_programs(0) - 1)
     def _():
         out_ref[...] = jnp.zeros_like(out_ref)
         for distance in range(1 + len(streams)):
-            value = sums[distance]
+            value = sums[2 * snaps * distance:2 * snaps * (distance + 1)]
             if distance == 0:
                 value = 0.5 * value
             at = lax.rem(z - way * distance + rings, rings)
@@ -275,7 +270,7 @@
 
 def gram_call(place, ya, yb, a0, b0, streams, rings):
     snaps, nodes = ya.shape
-    chunk = nodes // 4
+    chunk = nodes // 6
     single = pl.BlockSpec((snaps, chunk), lambda i: (0, i))
     double = pl.BlockSpec((2 * snaps, chunk), lambda i: (0, i))
     tiles = (4 * rings, snaps // 2, 2 * snaps)
@@ -285,7 +280,7 @@
         out_shape=jax.ShapeDtypeStruct(tiles, jnp.float32),
         in_specs=[IN_SMEM] + [single] * 4 + [double] * len(streams),
         out_specs=pl.BlockSpec(tiles, lambda i: (0, 0, 0)),
-        scratch_shapes=[pltpu.VMEM((1 + len(streams), 2 * snaps, 2 * snaps), jnp.float32)],
+        scratch_shapes=[pltpu.VMEM(((1 + len(streams)) * 2 * snaps, 2 * snaps), jnp.float32)],
         compiler_params=pltpu.CompilerParams(vmem_limit_bytes=40 * MIB),
         cost_estimate=cost(8),
     )(place, ya, yb, a0, b0, *streams)
@@ -312,7 +307,7 @@
     half_at = jnp.reshape(h, (1,)).astype(jnp.int32)
     (rows,) = apply_call(0, 3, columns, snapshots, None, half_at)
 
-    rows, a1, b1 = tied((rows, a1, b1))
+    rows, a1, b1, given = tied((rows, a1, b1, given))
     pair1 = jnp.concatenate([a1, b1], axis=0)
     pair2 = ring_hop(pair1, 1)
     (rows,) = apply_call(1, 3, columns, snapshots, rows, half_at)

time: 158 us -> 149 us (0.943)
  Pallas kernels: 82.7 us -> 70 us
  starting transfers between devices: 31 us -> 33.5 us
    pallas_call x3, Pallas kernels: 65.7 us -> 55.9 us  [apply_call(): pl.pallas_call(functools.partial(apply_kernel, first, last, index * count...]
    ppermute x5, starting transfers between devices: 14.9 us -> 19.1 us  [ring_hop(): return lax.ppermute(value, ('mesh', 'snap'), pairs)]
    pallas_call x1, Pallas kernels: 8.66 us -> 5.46 us  [on_device(): pl.pallas_call(assemble_kernel, out_shape=jax.ShapeDtypeStruct((snaps, no...]
    ppermute x2, starting transfers between devices: 5.91 us -> 3.03 us  [partner(): lax.ppermute(value, 'snap', [(i, i ^ 1) for i in range(lax.axis_size('sna...]
    ppermute x5, waiting for transfers between devices: 0.95 us -> 3.56 us  [ring_hop(): return lax.ppermute(value, ('mesh', 'snap'), pairs)]
  transfers between devices with their start and end apart: 10 -> 10, of which waited for: 4 -> 4; matrix products, arithmetic and copies ran while one was open for 0% -> 0% of each run, Pallas kernels for 49% -> 43%
where the time goes in v4:
time: 149 us
  Pallas kernels  70 us (47%)
  starting transfers between devices  33.5 us (22%)
  waiting for transfers between devices  22.4 us (15%)
  blocking collectives  15.7 us (11%)
  local copies, waits for them, and re-layouts  5.12 us (3%)
    pallas_call x3, Pallas kernels, apply_call(): pl.pallas_call(functools.partial(apply_kernel, first, last, index * count...  55.9 us
    ppermute x5, starting transfers between devices, ring_hop(): return lax.ppermute(value, ('mesh', 'snap'), pairs)  19.1 us
    all_to_all x1, blocking collectives, on_device(): lax.all_to_all(tiles, ('mesh', 'snap'), 0, 0, axis_index_groups=planes, t...  15.7 us
    ppermute x2, waiting for transfers between devices, passed_along(): lax.ppermute(value, axis, [(source, source + steps) for source in range(l...  10.4 us
    ppermute x1, waiting for transfers between devices, mirrored(): lax.ppermute(value, ('mesh', 'snap'), [(s * count + m, m * count + s) for...  8.4 us
    ppermute x2, starting transfers between devices, passed_along(): lax.ppermute(value, axis, [(source, source + steps) for source in range(l...  6.17 us
    pallas_call x1, Pallas kernels, gram_call(): pl.pallas_call(gram_kernel, grid=(nodes // chunk,), out_shape=jax.ShapeDt...  5.97 us
    pallas_call x1, Pallas kernels, on_device(): pl.pallas_call(assemble_kernel, out_shape=jax.ShapeDtypeStruct((snaps, no...  5.46 us
  transfers between devices with their start and end apart: 10, of which 4 were waited for; matrix products, arithmetic and copies ran while one was open for 0% of the time, Pallas kernels for 43%

profile of v4, /device:TPU:5, one launch (start us, length us, event | category | flops | bytes accessed | tf_op | source)
XLA Modules:
  0.0 148.5 jit_solution(16132968548214416117)
XLA Ops:
  0.7 1.6 %constant_dynamic-slice_fusion = (f32[64,3072]{1,0:T(8,128)S(1)}, f32[64,3072]{1,0:T(8,128)S(1)}) fusion(f32[64,6144]{1,0:T(8,128)} %refs_4_.5, s32[]{:T(128)S(6)} %select_n.27, s32[]{:T(128)S(6)} %select_n.26), kind=kLoop, calls=%fused_computation.7 | loop fusion | bytes 3145736 | tf_op jit(solution)/shard_map/dynamic_slice | solution.py:301
  2.3 8.3 %collective-permute-start.1 = (f32[64,3072]{1,0:T(8,128)S(1)}, f32[64,3072]{1,0:T(8,128)S(1)}, u32[]{:S(2)}, u32[]{:S(2)}) collective-permute-start(f32[64,3072]{1,0:T(8,128)S(1)} %get-tuple-element.28), channel_id=1, source_target_pairs={{0,3},{1,2},{2,5},{3,4},{4,7},{5,6},{6,9},{7,8},{8,11},{9,10},{10,... | collective-permute-start | bytes 2359304 | tf_op jit(solution)/shard_map/ppermute | solution.py:26
  10.6 0.7 collective-permute-start
  11.3 0.1 and_add_fusion
  11.4 0.1 fusion.1
  11.5 17.2 %shard_map.68.refs_5_ = f32[6144,128]{1,0:T(8,128)} custom-call(s32[12288]{0:T(1024)S(1)} %bitcast.14, s32[12288]{0:T(1024)S(1)} %bitcast.11, s32[12288]{0:T(1024)S(1)} %bitcast.8, f32[12288]{0:T(1024)S(1)} %copy-done.13, f32[64,6144]{1,0:T(8,128)S(1)} %copy-done.2), custom_call_target="tpu_custom_call" | custom-call | flops 20000000000 | bytes 60000000 | tf_op jit(solution)/shard_map/pallas_call | solution.py:218
  28.7 3.6 %collective-permute-done = f32[64,3072]{1,0:T(8,128)S(1)} collective-permute-done((f32[64,3072]{1,0:T(8,128)S(1)}, f32[64,3072]{1,0:T(8,128)S(1)}, u32[]{:S(2)}, u32[]{:S(2)}) %collective-permute-start) | collective-permute-done | bytes 786464 | tf_op jit(solution)/shard_map/ppermute | solution.py:26
  32.3 0.1 collective-permute-start.6
  32.4 0.1 constant_dynamic-update-slice_fusion.refs_0_
  32.5 3.2 %collective-permute-start.2 = (f32[128,3072]{1,0:T(8,128)S(1)}, f32[128,3072]{1,0:T(8,128)S(1)}, u32[]{:S(2)}, u32[]{:S(2)}) collective-permute-start(f32[128,3072]{1,0:T(8,128)S(1)} %constant_dynamic-update-slice_fusion.refs_0_), channel_id=1, source_target_pairs={{0,2},{1,3},{2,4},{3,5},{4,6},{5,7},{6,8},{7,9},{8,10},{9,11},{10,... | collective-permute-start | bytes 4718600 | tf_op jit(solution)/shard_map/ppermute | solution.py:26
  35.7 17.5 %shard_map.69.refs_5_ = f32[6144,128]{1,0:T(8,128)} custom-call(s32[12288]{0:T(1024)S(1)} %bitcast.15, s32[12288]{0:T(1024)S(1)} %bitcast.12, s32[12288]{0:T(1024)S(1)} %bitcast.9, f32[12288]{0:T(1024)S(1)} %copy-done.13, f32[64,6144]{1,0:T(8,128)S(1)} %copy-done.2, f32[6144,128]{1,0:T(8,128)} %shard_map.68.refs_5_), custom_call_target="tpu_custom_call" | custom-call | flops 20000000000 | bytes 60000000 | tf_op jit(solution)/shard_map/pallas_call | solution.py:218
  53.2 3.3 %collective-permute-start.5 = (f32[128,3072]{1,0:T(8,128)S(1)}, f32[128,3072]{1,0:T(8,128)}, u32[]{:S(2)}, u32[]{:S(2)}) collective-permute-start(f32[128,3072]{1,0:T(8,128)S(1)} %collective-permute-done.2.refs_1_), channel_id=1, source_target_pairs={{0,2},{1,3},{2,4},{3,5},{4,6},{5,7},{6,8},{7,9},{8,10},{9,11},{10,... | collective-permute-start | bytes 4718600 | tf_op jit(solution)/shard_map/ppermute | solution.py:26
  56.4 21.3 %shard_map.70 = (f32[6144,128]{1,0:T(8,128)}, f32[64,3072]{1,0:T(8,128)S(1)}, f32[64,3072]{1,0:T(8,128)}) custom-call(s32[12288]{0:T(1024)S(1)} %bitcast.16, s32[12288]{0:T(1024)S(1)} %bitcast.13, s32[12288]{0:T(1024)S(1)} %bitcast.10, f32[12288]{0:T(1024)S(1)} %copy-done.13, f32[64,6144]{1,0:T(8,128)} %refs_4_.5, f32[6144,128]{1,0:T(8,128)} %shard_map.69.refs_5_, ...), custom_call_target="tpu_custom_call" | custom-call | flops 20000000000 | bytes 60000000 | tf_op jit(solution)/shard_map/pallas_call | solution.py:218
  77.8 3.6 %collective-permute-start.8 = (f32[128,3072]{1,0:T(8,128)}, f32[128,3072]{1,0:T(8,128)}, u32[]{:S(2)}, u32[]{:S(2)}) collective-permute-start(f32[128,3072]{1,0:T(8,128)} %collective-permute-done.5.refs_2_), channel_id=1, source_target_pairs={{0,2},{1,3},{2,4},{3,5},{4,6},{5,7},{14,0},{15,1},{16,30},{17,31},... | collective-permute-start | bytes 4718600 | tf_op jit(solution)/shard_map/ppermute | solution.py:26
  81.4 3.0 %collective-permute-start.7 = (f32[64,3072]{1,0:T(8,128)}, f32[64,3072]{1,0:T(8,128)}, u32[]{:S(2)}, u32[]{:S(2)}) collective-permute-start(f32[64,3072]{1,0:T(8,128)} %get-tuple-element.29), channel_id=1, source_target_pairs={{0,1},{1,0},{2,3},{3,2},{4,5},{5,4},{6,7},{7,6},{8,9},{9,8},{10,11... | collective-permute-start | bytes 2359304 | tf_op jit(solution)/shard_map/ppermute | solution.py:36
  84.4 1.9 %copy-done = f32[6144,128]{1,0:T(8,128)S(1)} copy-done((f32[6144,128]{1,0:T(8,128)S(1)}, f32[6144,128]{1,0:T(8,128)}, u32[]{:S(2)}) %copy-start) | copy-done | bytes 3145752
  86.3 2.6 %shard_map.71 = (f32[64,512]{1,0:T(8,128)S(1)}, f32[64,512]{1,0:T(8,128)}) custom-call(s32[512]{0:T(512)S(1)} %copy-done.7, s32[512]{0:T(512)S(1)} %copy-done.8, f32[6144,128]{1,0:T(8,128)S(1)} %copy-done), custom_call_target="tpu_custom_call" | custom-call | flops 10000000 | bytes 30000 | tf_op jit(solution)/shard_map/pallas_call | solution.py:325
  88.9 4.3 %collective-permute-start.3 = (f32[64,512]{1,0:T(8,128)}, f32[64,512]{1,0:T(8,128)S(1)}, u32[]{:S(2)}, u32[]{:S(2)}) collective-permute-start(f32[64,512]{1,0:T(8,128)} %get-tuple-element.24), channel_id=1, source_target_pairs={{0,16},{16,32},{32,48},{48,64},{64,80},{80,96},{96,112},{112,128},... | collective-permute-start | bytes 393224 | tf_op jit(solution)/shard_map/ppermute | solution.py:32
  93.2 1.9 %collective-permute-start.4 = (f32[64,512]{1,0:T(8,128)S(1)}, f32[64,512]{1,0:T(8,128)S(1)}, u32[]{:S(2)}, u32[]{:S(2)}) collective-permute-start(f32[64,512]{1,0:T(8,128)S(1)} %get-tuple-element.25), channel_id=1, source_target_pairs={{16,0},{32,16},{48,32},{64,48},{80,64},{96,80},{112,96},{128,112},... | collective-permute-start | bytes 393224 | tf_op jit(solution)/shard_map/ppermute | solution.py:32
  95.2 0.1 pad_add_fusion.place
  95.2 8.7 %collective-permute-done.3.below_ref = f32[64,512]{1,0:T(8,128)S(1)} collective-permute-done((f32[64,512]{1,0:T(8,128)}, f32[64,512]{1,0:T(8,128)S(1)}, u32[]{:S(2)}, u32[]{:S(2)}) %collective-permute-start.3) | collective-permute-done | bytes 131104 | tf_op jit(solution)/shard_map/ppermute | solution.py:32
  104.0 1.7 %collective-permute-done.4.above_ref = f32[64,512]{1,0:T(8,128)S(1)} collective-permute-done((f32[64,512]{1,0:T(8,128)S(1)}, f32[64,512]{1,0:T(8,128)S(1)}, u32[]{:S(2)}, u32[]{:S(2)}) %collective-permute-start.4) | collective-permute-done | bytes 131104 | tf_op jit(solution)/shard_map/ppermute | solution.py:32
  105.6 5.5 %shard_map.72 = f32[64,6144]{1,0:T(8,128)} custom-call(s32[512]{0:T(512)S(1)} %copy-done.7, s32[512]{0:T(512)S(1)} %copy-done.8, f32[6144,128]{1,0:T(8,128)S(1)} %copy-done.1, f32[64,512]{1,0:T(8,128)S(1)} %collective-permute-done.3.below_ref, f32[64,512]{1,0:T(8,128)S(1)} %collective-permute-done.4.above_ref), custom_call_target="tpu_custom_call" | custom-call | flops 10000000 | bytes 30000 | tf_op jit(solution)/shard_map/pallas_call | solution.py:336
  111.2 1.1 copy-done.15
  112.3 6.0 %shard_map.73 = f32[32,32,128]{2,1,0:T(8,128)S(1)} custom-call(s32[3]{0:T(128)S(1)} %pad_add_fusion.place, f32[64,3072]{1,0:T(8,128)S(1)} %copy-done.15, f32[64,3072]{1,0:T(8,128)} %collective-permute-done.7.yb_ref, f32[64,3072]{1,0:T(8,128)S(1)} %copy-done.4, f32[64,3072]{1,0:T(8,128)S(1)} %copy-done.12, f32[128,3072]{1,0:T(8,128)S(1)} %copy-done.6, ...), custom_call_target="tpu_custom_call" | custom-call | flops 8000000000 | bytes 24000000 | tf_op jit(solution)/shard_map/pallas_call | solution.py:277
  118.3 15.7 %all_to_all.5 = f32[32,32,128]{2,1,0:T(8,128)S(1)} all-to-all(f32[32,32,128]{2,1,0:T(8,128)S(1)} %shard_map.73), channel_id=1, replica_groups={{0,1,16,17,32,33,48,49,64,65,80,81,96,97,112,113,128,129,144,145,160,16..., dimensions={0} | all-to-all | bytes 1048576 | tf_op jit(solution)/shard_map/all_to_all | solution.py:351
  134.1 5.2 %collective-permute-start.9 = (f32[32,128]{1,0:T(8,128)S(1)}, f32[32,128]{1,0:T(8,128)S(1)}, u32[]{:S(2)}, u32[]{:S(2)}) collective-permute-start(f32[32,128]{1,0:T(8,128)S(1)} %reduce_sum.9), channel_id=1, source_target_pairs={{0,0},{16,1},{32,2},{48,3},{64,4},{80,5},{96,6},{112,7},{128,8},{1... | collective-permute-start | bytes 49160 | tf_op jit(solution)/shard_map/ppermute | solution.py:41
  139.3 0.1 fusion.3
  139.3 0.1 copy.7
  139.4 8.4 %collective-permute-done.9 = f32[32,128]{1,0:T(8,128)S(1)} collective-permute-done((f32[32,128]{1,0:T(8,128)S(1)}, f32[32,128]{1,0:T(8,128)S(1)}, u32[]{:S(2)}, u32[]{:S(2)}) %collective-permute-start.9) | collective-permute-done | bytes 16416 | tf_op jit(solution)/shard_map/ppermute | solution.py:41
  147.8 0.1 fusion.2
  147.9 0.6 fusion
  (41 shorter events, 0.2 us)
Async XLA Ops:
  0.7 10.7 %copy-start.16 = (s32[3,12288]{1,0:T(4,128)S(1)}, s32[3,12288]{1,0:T(4,128)}, u32[]{:S(2)}) copy-start(s32[3,12288]{1,0:T(4,128)} %param.6) | copy-start | bytes 442372
  0.7 10.8 %copy-start.2 = (f32[64,6144]{1,0:T(8,128)S(1)}, f32[64,6144]{1,0:T(8,128)}, u32[]{:S(2)}) copy-start(f32[64,6144]{1,0:T(8,128)} %refs_4_.5) | copy-start | bytes 4718596
  0.7 10.8 %copy-start.13 = (f32[12288]{0:T(1024)S(1)}, f32[12288]{0:T(1024)}, u32[]{:S(2)}) copy-start(f32[12288]{0:T(1024)} %refs_3_.5) | copy-start | bytes 147460
  2.3 26.4 %copy-start.3 = (f32[64,3072]{1,0:T(8,128)}, f32[64,3072]{1,0:T(8,128)S(1)}, u32[]{:S(2)}) copy-start(f32[64,3072]{1,0:T(8,128)S(1)} %get-tuple-element.37.a0_ref) | copy-start | bytes 2359300
  2.3 26.4 %collective-permute-start.1 = (f32[64,3072]{1,0:T(8,128)S(1)}, f32[64,3072]{1,0:T(8,128)S(1)}, u32[]{:S(2)}, u32[]{:S(2)}) collective-permute-start(f32[64,3072]{1,0:T(8,128)S(1)} %get-tuple-element.28), channel_id=1, source_target_pairs={{0,3},{1,2},{2,5},{3,4},{4,7},{5,6},{6,9},{7,8},{8,11},{9,10},{10,... | collective-permute-start | bytes 2359304 | tf_op jit(solution)/shard_map/ppermute | solution.py:26
  10.6 21.7 %collective-permute-start = (f32[64,3072]{1,0:T(8,128)S(1)}, f32[64,3072]{1,0:T(8,128)S(1)}, u32[]{:S(2)}, u32[]{:S(2)}) collective-permute-start(f32[64,3072]{1,0:T(8,128)S(1)} %get-tuple-element.37.a0_ref), channel_id=1, source_target_pairs={{0,2},{1,3},{2,4},{3,5},{4,6},{5,7},{6,8},{7,9},{8,10},{9,11},{10,... | collective-permute-start | bytes 2359304 | tf_op jit(solution)/shard_map/ppermute | solution.py:26
  32.3 45.5 %collective-permute-start.6 = (f32[64,3072]{1,0:T(8,128)S(1)}, f32[64,3072]{1,0:T(8,128)S(1)}, u32[]{:S(2)}, u32[]{:S(2)}) collective-permute-start(f32[64,3072]{1,0:T(8,128)S(1)} %get-tuple-element.28), channel_id=1, source_target_pairs={{0,1},{1,0},{2,3},{3,2},{4,5},{5,4},{6,7},{7,6},{8,9},{9,8},{10,11... | collective-permute-start | bytes 2359304 | tf_op jit(solution)/shard_map/ppermute | solution.py:36
  32.5 20.7 %copy-start.5 = (f32[128,3072]{1,0:T(8,128)}, f32[128,3072]{1,0:T(8,128)S(1)}, u32[]{:S(2)}) copy-start(f32[128,3072]{1,0:T(8,128)S(1)} %constant_dynamic-update-slice_fusion.refs_0_) | copy-start | bytes 4718596
  32.5 20.7 %collective-permute-start.2 = (f32[128,3072]{1,0:T(8,128)S(1)}, f32[128,3072]{1,0:T(8,128)S(1)}, u32[]{:S(2)}, u32[]{:S(2)}) collective-permute-start(f32[128,3072]{1,0:T(8,128)S(1)} %constant_dynamic-update-slice_fusion.refs_0_), channel_id=1, source_target_pairs={{0,2},{1,3},{2,4},{3,5},{4,6},{5,7},{6,8},{7,9},{8,10},{9,11},{10,... | collective-permute-start | bytes 4718600 | tf_op jit(solution)/shard_map/ppermute | solution.py:26
  53.2 24.6 %copy-start.9 = (f32[128,3072]{1,0:T(8,128)}, f32[128,3072]{1,0:T(8,128)S(1)}, u32[]{:S(2)}) copy-start(f32[128,3072]{1,0:T(8,128)S(1)} %collective-permute-done.2.refs_1_) | copy-start | bytes 4718596
  53.2 24.6 %collective-permute-start.5 = (f32[128,3072]{1,0:T(8,128)S(1)}, f32[128,3072]{1,0:T(8,128)}, u32[]{:S(2)}, u32[]{:S(2)}) collective-permute-start(f32[128,3072]{1,0:T(8,128)S(1)} %collective-permute-done.2.refs_1_), channel_id=1, source_target_pairs={{0,2},{1,3},{2,4},{3,5},{4,6},{5,7},{6,8},{7,9},{8,10},{9,11},{10,... | collective-permute-start | bytes 4718600 | tf_op jit(solution)/shard_map/ppermute | solution.py:26
  56.4 28.0 %copy-start.7 = (s32[512]{0:T(512)S(1)}, s32[512]{0:T(512)}, u32[]{:S(2)}) copy-start(s32[512]{0:T(512)} %low_s.3) | copy-start | bytes 6148
  56.4 28.0 %copy-start.8 = (s32[512]{0:T(512)S(1)}, s32[512]{0:T(512)}, u32[]{:S(2)}) copy-start(s32[512]{0:T(512)} %up_s.3) | copy-start | bytes 6148
  77.8 11.2 %copy-start.14 = (f32[64,3072]{1,0:T(8,128)}, f32[64,3072]{1,0:T(8,128)S(1)}, u32[]{:S(2)}) copy-start(f32[64,3072]{1,0:T(8,128)S(1)} %get-tuple-element.32.ya_ref) | copy-start | bytes 2359300
  77.8 11.2 %copy-start.11 = (f32[64,3072]{1,0:T(8,128)}, f32[64,3072]{1,0:T(8,128)S(1)}, u32[]{:S(2)}) copy-start(f32[64,3072]{1,0:T(8,128)S(1)} %collective-permute-done.6.b0_ref) | copy-start | bytes 2359300
  77.8 33.3 %collective-permute-start.8 = (f32[128,3072]{1,0:T(8,128)}, f32[128,3072]{1,0:T(8,128)}, u32[]{:S(2)}, u32[]{:S(2)}) collective-permute-start(f32[128,3072]{1,0:T(8,128)} %collective-permute-done.5.refs_2_), channel_id=1, source_target_pairs={{0,2},{1,3},{2,4},{3,5},{4,6},{5,7},{14,0},{15,1},{16,30},{17,31},... | collective-permute-start | bytes 4718600 | tf_op jit(solution)/shard_map/ppermute | solution.py:26
  81.4 29.7 %collective-permute-start.7 = (f32[64,3072]{1,0:T(8,128)}, f32[64,3072]{1,0:T(8,128)}, u32[]{:S(2)}, u32[]{:S(2)}) collective-permute-start(f32[64,3072]{1,0:T(8,128)} %get-tuple-element.29), channel_id=1, source_target_pairs={{0,1},{1,0},{2,3},{3,2},{4,5},{5,4},{6,7},{7,6},{8,9},{9,8},{10,11... | collective-permute-start | bytes 2359304 | tf_op jit(solution)/shard_map/ppermute | solution.py:36
  84.4 1.9 %copy-start = (f32[6144,128]{1,0:T(8,128)S(1)}, f32[6144,128]{1,0:T(8,128)}, u32[]{:S(2)}) copy-start(f32[6144,128]{1,0:T(8,128)} %get-tuple-element.23.rows.rows_ref) | copy-start | bytes 9437188
  86.3 19.3 %copy-start.1 = (f32[6144,128]{1,0:T(8,128)S(1)}, f32[6144,128]{1,0:T(8,128)}, u32[]{:S(2)}) copy-start(f32[6144,128]{1,0:T(8,128)} %get-tuple-element.23.rows.rows_ref) | copy-start | bytes 9437188
  88.9 15.0 %collective-permute-start.3 = (f32[64,512]{1,0:T(8,128)}, f32[64,512]{1,0:T(8,128)S(1)}, u32[]{:S(2)}, u32[]{:S(2)}) collective-permute-start(f32[64,512]{1,0:T(8,128)} %get-tuple-element.24), channel_id=1, source_target_pairs={{0,16},{16,32},{32,48},{48,64},{64,80},{80,96},{96,112},{112,128},... | collective-permute-start | bytes 393224 | tf_op jit(solution)/shard_map/ppermute | solution.py:32
  93.2 12.4 %collective-permute-start.4 = (f32[64,512]{1,0:T(8,128)S(1)}, f32[64,512]{1,0:T(8,128)S(1)}, u32[]{:S(2)}, u32[]{:S(2)}) collective-permute-start(f32[64,512]{1,0:T(8,128)S(1)} %get-tuple-element.25), channel_id=1, source_target_pairs={{16,0},{32,16},{48,32},{64,48},{80,64},{96,80},{112,96},{128,112},... | collective-permute-start | bytes 393224 | tf_op jit(solution)/shard_map/ppermute | solution.py:32
  95.2 15.9 %copy-start.4 = (f32[64,3072]{1,0:T(8,128)S(1)}, f32[64,3072]{1,0:T(8,128)}, u32[]{:S(2)}) copy-start(f32[64,3072]{1,0:T(8,128)} %copy-done.3) | copy-start | bytes 2359300
  95.2 15.9 %copy-start.6 = (f32[128,3072]{1,0:T(8,128)S(1)}, f32[128,3072]{1,0:T(8,128)}, u32[]{:S(2)}) copy-start(f32[128,3072]{1,0:T(8,128)} %copy-done.5) | copy-start | bytes 4718596
  95.2 15.9 %copy-start.10 = (f32[128,3072]{1,0:T(8,128)S(1)}, f32[128,3072]{1,0:T(8,128)}, u32[]{:S(2)}) copy-start(f32[128,3072]{1,0:T(8,128)} %copy-done.9) | copy-start | bytes 4718596
  95.2 15.9 %copy-start.12 = (f32[64,3072]{1,0:T(8,128)S(1)}, f32[64,3072]{1,0:T(8,128)}, u32[]{:S(2)}) copy-start(f32[64,3072]{1,0:T(8,128)} %copy-done.11) | copy-start | bytes 2359300
  111.2 1.1 copy-start.15
  134.1 13.8 %collective-permute-start.9 = (f32[32,128]{1,0:T(8,128)S(1)}, f32[32,128]{1,0:T(8,128)S(1)}, u32[]{:S(2)}, u32[]{:S(2)}) collective-permute-start(f32[32,128]{1,0:T(8,128)S(1)} %reduce_sum.9), channel_id=1, source_target_pairs={{0,0},{16,1},{32,2},{48,3},{64,4},{80,5},{96,6},{112,7},{128,8},{1... | collective-permute-start | bytes 49160 | tf_op jit(solution)/shard_map/ppermute | solution.py:41

commit v5 on v4

--- a/solution.py
+++ b/solution.py
@@ -11,7 +11,7 @@
 MIB = 2 ** 20
 
 
-def ring_hop(value, steps, cross=False, closing=False):
+def ring_hop(value, steps, cross=False):
     parts, blocks = lax.axis_size("mesh"), lax.axis_size("snap")
     rings = blocks // 2
     pairs = []
@@ -20,8 +20,6 @@
         for block in range(blocks):
             z, h = block // 2, block % 2
             target = (z + way * steps) % rings
-            if closing and (target < rings // 2) != (part % 2 == 0):
-                continue
             pairs.append((part * blocks + block, part * blocks + 2 * target + (h ^ 1 if cross else h)))
     return lax.ppermute(value, ("mesh", "snap"), pairs)
 
@@ -34,12 +32,6 @@
 
 def partner(value):
     return lax.ppermute(value, "snap", [(i, i ^ 1) for i in range(lax.axis_size("snap"))])
-
-
-def mirrored(value):
-    count = lax.axis_size("snap")
-    return lax.ppermute(value, ("mesh", "snap"),
-                        [(s * count + m, m * count + s) for m in range(count) for s in range(count)])
 
 
 def apply_kernel(first, last, start, count, arrays, parts, *refs):
@@ -208,15 +200,20 @@
 ARRAYS, PARTS = 4, 2
 
 
-def apply_call(index, calls, columns, snapshots, rows, half):
+SHARES = (1, 1)
+
+
+def apply_call(index, columns, snapshots, rows, half):
+    calls = len(SHARES)
     first, last = index == 0, index == calls - 1
     snaps, nodes = snapshots.shape
-    count = columns[0].shape[0] // calls
+    share = columns[0].shape[0] // sum(SHARES)
+    start, count = share * sum(SHARES[:index]), share * SHARES[index]
     row_shape = jax.ShapeDtypeStruct((nodes, LANES), jnp.float32)
     side = jax.ShapeDtypeStruct((snaps, nodes // 2), jnp.float32)
     operands = columns + (snapshots,) + (() if first else (rows,)) + ((half,) if last else ())
     return pl.pallas_call(
-        functools.partial(apply_kernel, first, last, index * count, count, ARRAYS, PARTS),
+        functools.partial(apply_kernel, first, last, start, count, ARRAYS, PARTS),
         out_shape=[row_shape] + ([side, side] if last else []),
         in_specs=[ANYWHERE] * 4 + [IN_VMEM] + ([] if first else [ANYWHERE]) + ([IN_SMEM] if last else []),
         out_specs=[ANYWHERE] + ([IN_VMEM] * 2 if last else []),
@@ -234,56 +231,84 @@
     return high, (value - high.astype(jnp.float32)).astype(jnp.bfloat16)
 
 
-def gram_kernel(place, ya_ref, yb_ref, a0_ref, b0_ref, *refs):
-    *streams, out_ref, sums = refs
+def product(x_of, ya_ref, yb_ref, row_sets):
+    snaps, nodes = ya_ref.shape
+    dot = functools.partial(lax.dot_general, dimension_numbers=(((1,), (1,)), ((), ())),
+                            preferred_element_type=jnp.float32)
+    chunk = nodes // 6
+    totals = [None] * row_sets
+    for i in range(6):
+        at = slice(i * chunk, (i + 1) * chunk)
+        y_high, y_low = halves_of(jnp.concatenate([ya_ref[:, at], yb_ref[:, at]], axis=0))
+        both_y = jnp.concatenate([y_high, y_low], axis=0)
+        for row_set in range(row_sets):
+            high, low = halves_of(x_of(row_set, at))
+            both = dot(high, both_y)
+            value = both[:, :2 * snaps] + (both[:, 2 * snaps:] + dot(low, y_high))
+            totals[row_set] = value if totals[row_set] is None else totals[row_set] + value
+    return totals
+
+
+def near_kernel(ya_ref, yb_ref, a0_ref, b0_ref, *refs):
+    streams, out_ref, back = refs[:3], refs[3], refs[4:]
+
+    def rows(distance, at):
+        if distance == 0:
+            return jnp.concatenate([a0_ref[:, at], b0_ref[:, at]], axis=0)
+        return streams[distance - 1][:, at]
+
+    for distance, value in enumerate(product(rows, ya_ref, yb_ref, 1 + len(streams))):
+        out_ref[distance] = value
+        if distance > 0:
+            back[distance - 1][...] = value.T
+
+
+def far_kernel(place, ya_ref, yb_ref, far_ref, near_ref, *refs):
+    *back, out_ref = refs
     snaps = ya_ref.shape[0]
     rings = out_ref.shape[0] // 4
     low = snaps // 2
     z, h, way = place[0], place[1], place[2]
-    step = pl.program_id(0)
-
-    @pl.when(step == 0)
-    def _():
-        sums[...] = jnp.zeros_like(sums)
-
-    y_high, y_low = halves_of(jnp.concatenate([ya_ref[...], yb_ref[...]], axis=0))
-    high, low_part = halves_of(jnp.concatenate([a0_ref[...], b0_ref[...]] + [stream[...] for stream in streams], axis=0))
-    dot = functools.partial(lax.dot_general, dimension_numbers=(((1,), (1,)), ((), ())),
-                            preferred_element_type=jnp.float32)
-    both = dot(high, jnp.concatenate([y_high, y_low], axis=0))
-    sums[...] += both[:, :2 * snaps] + (both[:, 2 * snaps:] + dot(low_part, y_high))
-
-    @pl.when(step == pl.num_programs(0) - 1)
-    def _():
-        out_ref[...] = jnp.zeros_like(out_ref)
-        for distance in range(1 + len(streams)):
-            value = sums[2 * snaps * distance:2 * snaps * (distance + 1)]
-            if distance == 0:
-                value = 0.5 * value
-            at = lax.rem(z - way * distance + rings, rings)
-            for side in range(2):
-                row = 2 * at + (h if side == 0 else 1 - h)
-                upper, lower = value[side * snaps:side * snaps + low], value[side * snaps + low:(side + 1) * snaps]
-                out_ref[2 * row + h] = jnp.concatenate([upper[:, :snaps], lower[:, :snaps]], axis=1)
-                out_ref[2 * row + (1 - h)] = jnp.concatenate([upper[:, snaps:], lower[:, snaps:]], axis=1)
-
-
-def gram_call(place, ya, yb, a0, b0, streams, rings):
-    snaps, nodes = ya.shape
-    chunk = nodes // 6
-    single = pl.BlockSpec((snaps, chunk), lambda i: (0, i))
-    double = pl.BlockSpec((2 * snaps, chunk), lambda i: (0, i))
-    tiles = (4 * rings, snaps // 2, 2 * snaps)
+
+    def put(distance, value):
+        at = lax.rem(z - way * distance + rings, rings)
+        for side in range(2):
+            row = 2 * at + (h if side == 0 else 1 - h)
+            upper, lower = value[side * snaps:side * snaps + low], value[side * snaps + low:(side + 1) * snaps]
+            out_ref[2 * row + h] = jnp.concatenate([upper[:, :snaps], lower[:, :snaps]], axis=1)
+            out_ref[2 * row + (1 - h)] = jnp.concatenate([upper[:, snaps:], lower[:, snaps:]], axis=1)
+
+    put(0, near_ref[0])
+    for distance, received in enumerate(back, 1):
+        put(distance, near_ref[distance])
+        put(-distance, received[...])
+    (value,) = product(lambda _, at: far_ref[:, at], ya_ref, yb_ref, 1)
+    put(rings // 2, value)
+
+
+def near_call(ya, yb, a0, b0, streams):
+    snaps = ya.shape[0]
+    square = jax.ShapeDtypeStruct((2 * snaps, 2 * snaps), jnp.float32)
     return pl.pallas_call(
-        gram_kernel,
-        grid=(nodes // chunk,),
-        out_shape=jax.ShapeDtypeStruct(tiles, jnp.float32),
-        in_specs=[IN_SMEM] + [single] * 4 + [double] * len(streams),
-        out_specs=pl.BlockSpec(tiles, lambda i: (0, 0, 0)),
-        scratch_shapes=[pltpu.VMEM(((1 + len(streams)) * 2 * snaps, 2 * snaps), jnp.float32)],
-        compiler_params=pltpu.CompilerParams(vmem_limit_bytes=40 * MIB),
-        cost_estimate=cost(8),
-    )(place, ya, yb, a0, b0, *streams)
+        near_kernel,
+        out_shape=[jax.ShapeDtypeStruct((1 + len(streams), 2 * snaps, 2 * snaps), jnp.float32)] + [square] * len(streams),
+        in_specs=[IN_VMEM] * (4 + len(streams)),
+        out_specs=[IN_VMEM] * (1 + len(streams)),
+        compiler_params=pltpu.CompilerParams(vmem_limit_bytes=16 * MIB),
+        cost_estimate=cost(4),
+    )(ya, yb, a0, b0, *streams)
+
+
+def far_call(place, ya, yb, far, near, back, rings):
+    snaps = ya.shape[0]
+    return pl.pallas_call(
+        far_kernel,
+        out_shape=jax.ShapeDtypeStruct((4 * rings, snaps // 2, 2 * snaps), jnp.float32),
+        in_specs=[IN_SMEM] + [IN_VMEM] * (4 + len(back)),
+        out_specs=IN_VMEM,
+        compiler_params=pltpu.CompilerParams(vmem_limit_bytes=16 * MIB),
+        cost_estimate=cost(2),
+    )(place, ya, yb, far, near, *back)
 
 
 def on_device(snapshots, connectivity, element_mass, lower_shared, upper_shared):
@@ -305,21 +330,17 @@
     spread = (connectivity >> 3) * (8 * (1 + PARTS)) + (connectivity & 7)
     columns = tuple(spread[k] for k in range(3)) + (element_mass,)
     half_at = jnp.reshape(h, (1,)).astype(jnp.int32)
-    (rows,) = apply_call(0, 3, columns, snapshots, None, half_at)
+    (rows,) = apply_call(0, columns, snapshots, None, half_at)
 
     rows, a1, b1, given = tied((rows, a1, b1, given))
     pair1 = jnp.concatenate([a1, b1], axis=0)
     pair2 = ring_hop(pair1, 1)
-    (rows,) = apply_call(1, 3, columns, snapshots, rows, half_at)
-
-    rows, pair2 = tied((rows, pair2))
+    b0 = partner(given)
+    rows, y_own, y_given = apply_call(1, columns, snapshots, rows, half_at)
+
+    y_given, pair2, b0 = tied((y_given, pair2, b0))
     pair3 = ring_hop(pair2, 1)
-    b0 = partner(given)
-    rows, y_own, y_given = apply_call(2, 3, columns, snapshots, rows, half_at)
-
-    y_given, pair3, b0 = tied((y_given, pair3, b0))
     y_theirs = partner(y_given)
-    pair4 = ring_hop(pair3, 1, closing=True)
 
     shared = lower_shared.shape[0]
     low, high = pl.pallas_call(
@@ -333,6 +354,8 @@
     )(lower_shared, upper_shared, rows)
     from_below = passed_along(high, "mesh", 1)
     from_above = passed_along(low, "mesh", -1)
+    from_below, from_above, pair3, y_theirs = tied((from_below, from_above, pair3, y_theirs))
+    pair4 = ring_hop(pair3, 1)
     weighted = pl.pallas_call(
         assemble_kernel,
         out_shape=jax.ShapeDtypeStruct((snaps, nodes), jnp.float32),
@@ -343,18 +366,16 @@
         compiler_params=pltpu.CompilerParams(vmem_limit_bytes=20 * MIB),
         cost_estimate=cost(0.01),
     )(lower_shared, upper_shared, rows, from_below, from_above)
-    weighted, y_theirs, pair4 = tied((weighted, y_theirs, pair4))
-
+    weighted, y_theirs = tied((weighted, y_theirs))
+
+    near, *back = near_call(y_own, y_theirs, own, b0, [pair1, pair2, pair3])
+    back = [ring_hop(value, -distance) for distance, value in enumerate(back, 1)]
     place = jnp.stack([z, h, jnp.where(position % 2 == 0, 1, -1)]).astype(jnp.int32)
-    tiles = gram_call(place, y_own, y_theirs, own, b0, [pair1, pair2, pair3, pair4], rings)
+    tiles = far_call(place, y_own, y_theirs, pair4, near, back, rings)
     planes = [[m * blocks + 2 * r + c for m in range(parts) for c in range(2)] for r in range(rings)]
     tile = jnp.sum(lax.all_to_all(tiles, ("mesh", "snap"), 0, 0, axis_index_groups=planes, tiled=True), axis=0)
-    other = mirrored(tile)
-
-    def unfolded(value):
-        return jnp.concatenate([value[:, :snaps], value[:, snaps:]], axis=0)
-
-    return weighted, (unfolded(tile).T + unfolded(other)) * (1.0 / float(parts * nodes))
+    column = jnp.concatenate([tile[:, :snaps], tile[:, snaps:]], axis=0)
+    return weighted, column.T * (1.0 / float(parts * nodes))
 
 
 def solution(mesh):

time: 149 us -> 140 us (0.940)
  the two profiles are of different devices: /device:TPU:5 before, /device:TPU:1 now
where the time goes in v5:
time: 140 us
  Pallas kernels  64 us (46%)
  starting transfers between devices  25.8 us (18%)
  blocking collectives  22.8 us (16%)
  waiting for transfers between devices  16.5 us (12%)
  local copies, waits for them, and re-layouts  9.47 us (7%)
    pallas_call x2, Pallas kernels, apply_call(): pl.pallas_call(functools.partial(apply_kernel, first, last, start, count,...  49.9 us
    all_to_all x1, blocking collectives, on_device(): lax.all_to_all(tiles, ('mesh', 'snap'), 0, 0, axis_index_groups=planes, t...  22.8 us
    ppermute x8, starting transfers between devices, ring_hop(): return lax.ppermute(value, ('mesh', 'snap'), pairs)  16.9 us
    ppermute x2, waiting for transfers between devices, passed_along(): lax.ppermute(value, axis, [(source, source + steps) for source in range(l...  10.2 us
    unnamed x40, local copies, waits for them, and re-layouts  7.63 us
    ppermute x8, waiting for transfers between devices, ring_hop(): return lax.ppermute(value, ('mesh', 'snap'), pairs)  6.26 us
    ppermute x2, starting transfers between devices, passed_along(): lax.ppermute(value, axis, [(source, source + steps) for source in range(l...  5.81 us
    pallas_call x1, Pallas kernels, on_device(): pl.pallas_call(assemble_kernel, out_shape=jax.ShapeDtypeStruct((snaps, no...  5.46 us
  transfers between devices with their start and end apart: 12, of which 5 were waited for; matrix products, arithmetic and copies ran while one was open for 0% of the time, Pallas kernels for 44%

profile of v5, /device:TPU:1, one launch (start us, length us, event | category | flops | bytes accessed | tf_op | source)
XLA Modules:
  0.0 139.7 jit_solution(8411785835265769161)
XLA Ops:
  0.7 1.6 %constant_dynamic-slice_fusion = (f32[64,3072]{1,0:T(8,128)S(1)}, f32[64,3072]{1,0:T(8,128)S(1)}) fusion(f32[64,6144]{1,0:T(8,128)} %refs_4_.3, s32[]{:T(128)S(6)} %select_n.27, s32[]{:T(128)S(6)} %select_n.26), kind=kLoop, calls=%fused_computation.6 | loop fusion | bytes 3145736 | tf_op jit(solution)/shard_map/dynamic_slice | solution.py:326
  2.3 9.1 %collective-permute-start.1 = (f32[64,3072]{1,0:T(8,128)S(1)}, f32[64,3072]{1,0:T(8,128)S(1)}, u32[]{:S(2)}, u32[]{:S(2)}) collective-permute-start(f32[64,3072]{1,0:T(8,128)S(1)} %get-tuple-element.31), channel_id=1, source_target_pairs={{0,3},{1,2},{2,5},{3,4},{4,7},{5,6},{6,9},{7,8},{8,11},{9,10},{10,... | collective-permute-start | bytes 2359304 | tf_op jit(solution)/shard_map/ppermute | solution.py:24
  11.4 0.7 collective-permute-start
  12.4 23.4 %shard_map.68.refs_5_ = f32[6144,128]{1,0:T(8,128)} custom-call(s32[12288]{0:T(1024)S(1)} %bitcast.12, s32[12288]{0:T(1024)S(1)} %bitcast.10, s32[12288]{0:T(1024)S(1)} %bitcast.8, f32[12288]{0:T(1024)S(1)} %copy-done.15, f32[64,6144]{1,0:T(8,128)S(1)} %copy-done.2), custom_call_target="tpu_custom_call" | custom-call | flops 20000000000 | bytes 60000000 | tf_op jit(solution)/shard_map/pallas_call | solution.py:215
  35.8 0.1 collective-permute-start.5
  36.1 0.8 collective-permute-start.4
  36.9 26.5 %shard_map.69 = (f32[6144,128]{1,0:T(8,128)}, f32[64,3072]{1,0:T(8,128)S(1)}, f32[64,3072]{1,0:T(8,128)S(1)}) custom-call(s32[12288]{0:T(1024)S(1)} %bitcast.13, s32[12288]{0:T(1024)S(1)} %bitcast.11, s32[12288]{0:T(1024)S(1)} %bitcast.9, f32[12288]{0:T(1024)S(1)} %copy-done.15, f32[64,6144]{1,0:T(8,128)} %refs_4_.3, f32[6144,128]{1,0:T(8,128)} %shard_map.68.refs_5_, ...), custom_call_target="tpu_custom_call" | custom-call | flops 20000000000 | bytes 60000000 | tf_op jit(solution)/shard_map/pallas_call | solution.py:215
  63.4 0.9 copy-done.16
  64.3 0.9 copy-done.13
  65.2 1.4 collective-permute-start.6
  66.6 3.0 %collective-permute-start.7 = (f32[64,3072]{1,0:T(8,128)S(1)}, f32[64,3072]{1,0:T(8,128)S(1)}, u32[]{:S(2)}, u32[]{:S(2)}) collective-permute-start(f32[64,3072]{1,0:T(8,128)S(1)} %get-tuple-element.33), channel_id=1, source_target_pairs={{0,1},{1,0},{2,3},{3,2},{4,5},{5,4},{6,7},{7,6},{8,9},{9,8},{10,11... | collective-permute-start | bytes 2359304 | tf_op jit(solution)/shard_map/ppermute | solution.py:34
  69.6 1.9 %copy-done = f32[6144,128]{1,0:T(8,128)S(1)} copy-done((f32[6144,128]{1,0:T(8,128)S(1)}, f32[6144,128]{1,0:T(8,128)}, u32[]{:S(2)}) %copy-start) | copy-done | bytes 3145752
  71.5 1.9 %shard_map.70 = (f32[64,512]{1,0:T(8,128)S(1)}, f32[64,512]{1,0:T(8,128)S(1)}) custom-call(s32[512]{0:T(512)S(1)} %copy-done.7, s32[512]{0:T(512)S(1)} %copy-done.8, f32[6144,128]{1,0:T(8,128)S(1)} %copy-done), custom_call_target="tpu_custom_call" | custom-call | flops 10000000 | bytes 30000 | tf_op jit(solution)/shard_map/pallas_call | solution.py:346
  73.4 3.9 %collective-permute-start.2 = (f32[64,512]{1,0:T(8,128)S(1)}, f32[64,512]{1,0:T(8,128)S(1)}, u32[]{:S(2)}, u32[]{:S(2)}) collective-permute-start(f32[64,512]{1,0:T(8,128)S(1)} %get-tuple-element.26), channel_id=1, source_target_pairs={{0,16},{16,32},{32,48},{48,64},{64,80},{80,96},{96,112},{112,128},... | collective-permute-start | bytes 393224 | tf_op jit(solution)/shard_map/ppermute | solution.py:30
  77.3 1.9 %collective-permute-start.3 = (f32[64,512]{1,0:T(8,128)S(1)}, f32[64,512]{1,0:T(8,128)S(1)}, u32[]{:S(2)}, u32[]{:S(2)}) collective-permute-start(f32[64,512]{1,0:T(8,128)S(1)} %get-tuple-element.27), channel_id=1, source_target_pairs={{16,0},{32,16},{48,32},{64,48},{80,64},{96,80},{112,96},{128,112},... | collective-permute-start | bytes 393224 | tf_op jit(solution)/shard_map/ppermute | solution.py:30
  79.3 9.9 %collective-permute-done.2.below_ref = f32[64,512]{1,0:T(8,128)S(1)} collective-permute-done((f32[64,512]{1,0:T(8,128)S(1)}, f32[64,512]{1,0:T(8,128)S(1)}, u32[]{:S(2)}, u32[]{:S(2)}) %collective-permute-start.2) | collective-permute-done | bytes 131104 | tf_op jit(solution)/shard_map/ppermute | solution.py:30
  89.2 0.3 collective-permute-done.3.above_ref
  89.5 0.9 copy-done.11
  90.4 0.8 collective-permute-start.8
  91.2 5.5 %shard_map.71 = f32[64,6144]{1,0:T(8,128)} custom-call(s32[512]{0:T(512)S(1)} %copy-done.7, s32[512]{0:T(512)S(1)} %copy-done.8, f32[6144,128]{1,0:T(8,128)S(1)} %copy-done.1, f32[64,512]{1,0:T(8,128)S(1)} %collective-permute-done.2.below_ref, f32[64,512]{1,0:T(8,128)S(1)} %collective-permute-done.3.above_ref), custom_call_target="tpu_custom_call" | custom-call | flops 10000000 | bytes 30000 | tf_op jit(solution)/shard_map/pallas_call | solution.py:359
  96.7 1.1 copy-done.14
  97.9 1.1 copy-done.17
  99.0 4.4 %shard_map.72 = (f32[4,128,128]{2,1,0:T(8,128)S(1)}, f32[128,128]{1,0:T(8,128)S(1)}, f32[128,128]{1,0:T(8,128)S(1)}, f32[128,128]{1,0:T(8,128)S(1)}) custom-call(f32[64,3072]{1,0:T(8,128)S(1)} %copy-done.17, f32[64,3072]{1,0:T(8,128)S(1)} %copy-done.12, f32[64,3072]{1,0:T(8,128)S(1)} %copy-done.4, f32[64,3072]{1,0:T(8,128)S(1)} %copy-done.14, ...), custom_call_target="tpu_custom_call" | custom-call | flops 4000000000 | bytes 12000000 | tf_op jit(solution)/shard_map/pallas_call | solution.py:292
  103.4 0.7 collective-permute-start.9
  104.1 0.5 collective-permute-start.10
  104.6 2.8 %collective-permute-start.11 = (f32[128,128]{1,0:T(8,128)S(1)}, f32[128,128]{1,0:T(8,128)S(1)}, u32[]{:S(2)}, u32[]{:S(2)}) collective-permute-start(f32[128,128]{1,0:T(8,128)S(1)} %get-tuple-element.45), channel_id=1, source_target_pairs={{0,10},{1,11},{2,12},{3,13},{4,14},{5,15},{6,0},{7,1},{8,2},{9,3},... | collective-permute-start | bytes 196616 | tf_op jit(solution)/shard_map/ppermute | solution.py:24
  107.5 1.5 %collective-permute-done.9.refs_0_ = f32[128,128]{1,0:T(8,128)S(1)} collective-permute-done((f32[128,128]{1,0:T(8,128)S(1)}, f32[128,128]{1,0:T(8,128)S(1)}, u32[]{:S(2)}, u32[]{:S(2)}) %collective-permute-start.9) | collective-permute-done | bytes 65568 | tf_op jit(solution)/shard_map/ppermute | solution.py:24
  108.9 1.4 collective-permute-done.10.refs_1_
  110.3 3.4 %collective-permute-done.11.refs_2_ = f32[128,128]{1,0:T(8,128)S(1)} collective-permute-done((f32[128,128]{1,0:T(8,128)S(1)}, f32[128,128]{1,0:T(8,128)S(1)}, u32[]{:S(2)}, u32[]{:S(2)}) %collective-permute-start.11) | collective-permute-done | bytes 65568 | tf_op jit(solution)/shard_map/ppermute | solution.py:24
  113.7 2.3 %shard_map.73 = f32[32,32,128]{2,1,0:T(8,128)S(1)} custom-call(s32[3]{0:T(128)S(1)} %pad_add_fusion.place, f32[64,3072]{1,0:T(8,128)S(1)} %copy-done.17, f32[64,3072]{1,0:T(8,128)S(1)} %copy-done.12, f32[128,3072]{1,0:T(8,128)} %collective-permute-done.8.far_ref, f32[4,128,128]{2,1,0:T(8,128)S(1)} %get-tuple-element.42.near_ref, ...), custom_call_target="tpu_custom_call" | custom-call | flops 2000000000 | bytes 6000000 | tf_op jit(solution)/shard_map/pallas_call | solution.py:304
  116.1 22.8 %all_to_all.5 = f32[32,32,128]{2,1,0:T(8,128)S(1)} all-to-all(f32[32,32,128]{2,1,0:T(8,128)S(1)} %shard_map.73), channel_id=1, replica_groups={{0,1,16,17,32,33,48,49,64,65,80,81,96,97,112,113,128,129,144,145,160,16..., dimensions={0} | all-to-all | bytes 1048576 | tf_op jit(solution)/shard_map/all_to_all | solution.py:376
  139.0 0.7 copy.7
  (47 shorter events, 0.6 us)
Async XLA Ops:
  0.7 11.5 %copy-start.18 = (s32[3,12288]{1,0:T(4,128)S(1)}, s32[3,12288]{1,0:T(4,128)}, u32[]{:S(2)}) copy-start(s32[3,12288]{1,0:T(4,128)} %param.6) | copy-start | bytes 442372
  0.7 11.7 %copy-start.2 = (f32[64,6144]{1,0:T(8,128)S(1)}, f32[64,6144]{1,0:T(8,128)}, u32[]{:S(2)}) copy-start(f32[64,6144]{1,0:T(8,128)} %refs_4_.3) | copy-start | bytes 4718596
  0.7 11.7 %copy-start.15 = (f32[12288]{0:T(1024)S(1)}, f32[12288]{0:T(1024)}, u32[]{:S(2)}) copy-start(f32[12288]{0:T(1024)} %refs_3_.3) | copy-start | bytes 147460
  2.3 33.5 %copy-start.3 = (f32[64,3072]{1,0:T(8,128)}, f32[64,3072]{1,0:T(8,128)S(1)}, u32[]{:S(2)}) copy-start(f32[64,3072]{1,0:T(8,128)S(1)} %get-tuple-element.49.a0_ref) | copy-start | bytes 2359300
  2.3 33.5 %collective-permute-start.1 = (f32[64,3072]{1,0:T(8,128)S(1)}, f32[64,3072]{1,0:T(8,128)S(1)}, u32[]{:S(2)}, u32[]{:S(2)}) collective-permute-start(f32[64,3072]{1,0:T(8,128)S(1)} %get-tuple-element.31), channel_id=1, source_target_pairs={{0,3},{1,2},{2,5},{3,4},{4,7},{5,6},{6,9},{7,8},{8,11},{9,10},{10,... | collective-permute-start | bytes 2359304 | tf_op jit(solution)/shard_map/ppermute | solution.py:24
  11.4 24.4 %collective-permute-start = (f32[64,3072]{1,0:T(8,128)S(1)}, f32[64,3072]{1,0:T(8,128)S(1)}, u32[]{:S(2)}, u32[]{:S(2)}) collective-permute-start(f32[64,3072]{1,0:T(8,128)S(1)} %get-tuple-element.49.a0_ref), channel_id=1, source_target_pairs={{0,2},{1,3},{2,4},{3,5},{4,6},{5,7},{6,8},{7,9},{8,10},{9,11},{10,... | collective-permute-start | bytes 2359304 | tf_op jit(solution)/shard_map/ppermute | solution.py:24
  35.8 28.5 %collective-permute-start.5 = (f32[64,3072]{1,0:T(8,128)S(1)}, f32[64,3072]{1,0:T(8,128)S(1)}, u32[]{:S(2)}, u32[]{:S(2)}) collective-permute-start(f32[64,3072]{1,0:T(8,128)S(1)} %get-tuple-element.31), channel_id=1, source_target_pairs={{0,1},{1,0},{2,3},{3,2},{4,5},{5,4},{6,7},{7,6},{8,9},{9,8},{10,11... | collective-permute-start | bytes 2359304 | tf_op jit(solution)/shard_map/ppermute | solution.py:34
  36.0 27.4 %copy-start.5 = (f32[128,3072]{1,0:T(8,128)}, f32[128,3072]{1,0:T(8,128)S(1)}, u32[]{:S(2)}) copy-start(f32[128,3072]{1,0:T(8,128)S(1)} %constant_dynamic-update-slice_fusion.refs_0_) | copy-start | bytes 4718596
  36.1 29.2 %collective-permute-start.4 = (f32[128,3072]{1,0:T(8,128)S(1)}, f32[128,3072]{1,0:T(8,128)S(1)}, u32[]{:S(2)}, u32[]{:S(2)}) collective-permute-start(f32[128,3072]{1,0:T(8,128)S(1)} %constant_dynamic-update-slice_fusion.refs_0_), channel_id=1, source_target_pairs={{0,2},{1,3},{2,4},{3,5},{4,6},{5,7},{6,8},{7,9},{8,10},{9,11},{10,... | collective-permute-start | bytes 4718600 | tf_op jit(solution)/shard_map/ppermute | solution.py:24
  36.9 32.7 %copy-start.7 = (s32[512]{0:T(512)S(1)}, s32[512]{0:T(512)}, u32[]{:S(2)}) copy-start(s32[512]{0:T(512)} %low_s.3) | copy-start | bytes 6148
  36.9 32.7 %copy-start.8 = (s32[512]{0:T(512)S(1)}, s32[512]{0:T(512)}, u32[]{:S(2)}) copy-start(s32[512]{0:T(512)} %up_s.3) | copy-start | bytes 6148
  63.4 0.9 copy-start.16
  64.3 0.9 copy-start.13
  65.2 8.2 %copy-start.9 = (f32[128,3072]{1,0:T(8,128)}, f32[128,3072]{1,0:T(8,128)S(1)}, u32[]{:S(2)}) copy-start(f32[128,3072]{1,0:T(8,128)S(1)} %collective-permute-done.4.refs_1_) | copy-start | bytes 4718596
  65.2 25.2 %collective-permute-start.6 = (f32[128,3072]{1,0:T(8,128)S(1)}, f32[128,3072]{1,0:T(8,128)}, u32[]{:S(2)}, u32[]{:S(2)}) collective-permute-start(f32[128,3072]{1,0:T(8,128)S(1)} %collective-permute-done.4.refs_1_), channel_id=1, source_target_pairs={{0,2},{1,3},{2,4},{3,5},{4,6},{5,7},{6,8},{7,9},{8,10},{9,11},{10,... | collective-permute-start | bytes 4718600 | tf_op jit(solution)/shard_map/ppermute | solution.py:24
  66.6 22.9 %collective-permute-start.7 = (f32[64,3072]{1,0:T(8,128)S(1)}, f32[64,3072]{1,0:T(8,128)S(1)}, u32[]{:S(2)}, u32[]{:S(2)}) collective-permute-start(f32[64,3072]{1,0:T(8,128)S(1)} %get-tuple-element.33), channel_id=1, source_target_pairs={{0,1},{1,0},{2,3},{3,2},{4,5},{5,4},{6,7},{7,6},{8,9},{9,8},{10,11... | collective-permute-start | bytes 2359304 | tf_op jit(solution)/shard_map/ppermute | solution.py:34
  69.6 1.9 %copy-start = (f32[6144,128]{1,0:T(8,128)S(1)}, f32[6144,128]{1,0:T(8,128)}, u32[]{:S(2)}) copy-start(f32[6144,128]{1,0:T(8,128)} %get-tuple-element.25.rows.rows_ref) | copy-start | bytes 9437188
  71.5 19.8 %copy-start.1 = (f32[6144,128]{1,0:T(8,128)S(1)}, f32[6144,128]{1,0:T(8,128)}, u32[]{:S(2)}) copy-start(f32[6144,128]{1,0:T(8,128)} %get-tuple-element.25.rows.rows_ref) | copy-start | bytes 9437188
  73.4 15.8 %collective-permute-start.2 = (f32[64,512]{1,0:T(8,128)S(1)}, f32[64,512]{1,0:T(8,128)S(1)}, u32[]{:S(2)}, u32[]{:S(2)}) collective-permute-start(f32[64,512]{1,0:T(8,128)S(1)} %get-tuple-element.26), channel_id=1, source_target_pairs={{0,16},{16,32},{32,48},{48,64},{64,80},{80,96},{96,112},{112,128},... | collective-permute-start | bytes 393224 | tf_op jit(solution)/shard_map/ppermute | solution.py:30
  77.3 12.1 %collective-permute-start.3 = (f32[64,512]{1,0:T(8,128)S(1)}, f32[64,512]{1,0:T(8,128)S(1)}, u32[]{:S(2)}, u32[]{:S(2)}) collective-permute-start(f32[64,512]{1,0:T(8,128)S(1)} %get-tuple-element.27), channel_id=1, source_target_pairs={{16,0},{32,16},{48,32},{64,48},{80,64},{96,80},{112,96},{128,112},... | collective-permute-start | bytes 393224 | tf_op jit(solution)/shard_map/ppermute | solution.py:30
  89.5 0.9 copy-start.11
  90.4 23.3 %collective-permute-start.8 = (f32[128,3072]{1,0:T(8,128)}, f32[128,3072]{1,0:T(8,128)}, u32[]{:S(2)}, u32[]{:S(2)}) collective-permute-start(f32[128,3072]{1,0:T(8,128)} %collective-permute-done.6.refs_2_), channel_id=1, source_target_pairs={{0,2},{1,3},{2,4},{3,5},{4,6},{5,7},{6,8},{7,9},{8,10},{9,11},{10,... | collective-permute-start | bytes 4718600 | tf_op jit(solution)/shard_map/ppermute | solution.py:24
  91.2 5.5 %copy-start.4 = (f32[64,3072]{1,0:T(8,128)S(1)}, f32[64,3072]{1,0:T(8,128)}, u32[]{:S(2)}) copy-start(f32[64,3072]{1,0:T(8,128)} %copy-done.3) | copy-start | bytes 2359300
  91.2 5.5 %copy-start.6 = (f32[128,3072]{1,0:T(8,128)S(1)}, f32[128,3072]{1,0:T(8,128)}, u32[]{:S(2)}) copy-start(f32[128,3072]{1,0:T(8,128)} %copy-done.5) | copy-start | bytes 4718596
  91.2 5.5 %copy-start.10 = (f32[128,3072]{1,0:T(8,128)S(1)}, f32[128,3072]{1,0:T(8,128)}, u32[]{:S(2)}) copy-start(f32[128,3072]{1,0:T(8,128)} %copy-done.9) | copy-start | bytes 4718596
  91.2 5.5 %copy-start.12 = (f32[64,3072]{1,0:T(8,128)S(1)}, f32[64,3072]{1,0:T(8,128)}, u32[]{:S(2)}) copy-start(f32[64,3072]{1,0:T(8,128)} %copy-done.11) | copy-start | bytes 2359300
  96.7 1.1 copy-start.14
  97.9 1.1 copy-start.17
  103.4 5.6 %collective-permute-start.9 = (f32[128,128]{1,0:T(8,128)S(1)}, f32[128,128]{1,0:T(8,128)S(1)}, u32[]{:S(2)}, u32[]{:S(2)}) collective-permute-start(f32[128,128]{1,0:T(8,128)S(1)} %get-tuple-element.43), channel_id=1, source_target_pairs={{0,14},{1,15},{2,0},{3,1},{4,2},{5,3},{6,4},{7,5},{8,6},{9,7},{10,... | collective-permute-start | bytes 196616 | tf_op jit(solution)/shard_map/ppermute | solution.py:24
  104.1 6.3 %collective-permute-start.10 = (f32[128,128]{1,0:T(8,128)S(1)}, f32[128,128]{1,0:T(8,128)S(1)}, u32[]{:S(2)}, u32[]{:S(2)}) collective-permute-start(f32[128,128]{1,0:T(8,128)S(1)} %get-tuple-element.44), channel_id=1, source_target_pairs={{0,12},{1,13},{2,14},{3,15},{4,0},{5,1},{6,2},{7,3},{8,4},{9,5},{1... | collective-permute-start | bytes 196616 | tf_op jit(solution)/shard_map/ppermute | solution.py:24
  104.6 9.1 %collective-permute-start.11 = (f32[128,128]{1,0:T(8,128)S(1)}, f32[128,128]{1,0:T(8,128)S(1)}, u32[]{:S(2)}, u32[]{:S(2)}) collective-permute-start(f32[128,128]{1,0:T(8,128)S(1)} %get-tuple-element.45), channel_id=1, source_target_pairs={{0,10},{1,11},{2,12},{3,13},{4,14},{5,15},{6,0},{7,1},{8,2},{9,3},... | collective-permute-start | bytes 196616 | tf_op jit(solution)/shard_map/ppermute | solution.py:24

commit v6 on v5

--- a/solution.py
+++ b/solution.py
@@ -221,7 +221,7 @@
         + [pltpu.SMEM((count,), jnp.float32), pltpu.SemaphoreType.DMA((4,))]
         + [pltpu.VMEM((nodes, LANES), jnp.float32), pltpu.SemaphoreType.DMA, pltpu.SemaphoreType.DMA((4,))]
         + [pltpu.VMEM((nodes * (1 + PARTS), LANES), jnp.float32)] * ARRAYS,
-        compiler_params=pltpu.CompilerParams(vmem_limit_bytes=52 * MIB),
+        compiler_params=pltpu.CompilerParams(vmem_limit_bytes=44 * MIB),
         cost_estimate=cost(20),
     )(*operands)
 
@@ -249,21 +249,20 @@
     return totals
 
 
-def near_kernel(ya_ref, yb_ref, a0_ref, b0_ref, *refs):
-    streams, out_ref, back = refs[:3], refs[3], refs[4:]
+def near_kernel(ya_ref, yb_ref, a0_ref, b0_ref, pair1_ref, pair2_ref, a3_ref, b3_ref, out_ref, *back):
+    blocks = ((a0_ref, b0_ref), (pair1_ref,), (pair2_ref,), (a3_ref, b3_ref))
 
     def rows(distance, at):
-        if distance == 0:
-            return jnp.concatenate([a0_ref[:, at], b0_ref[:, at]], axis=0)
-        return streams[distance - 1][:, at]
-
-    for distance, value in enumerate(product(rows, ya_ref, yb_ref, 1 + len(streams))):
+        found = [ref[:, at] for ref in blocks[distance]]
+        return found[0] if len(found) == 1 else jnp.concatenate(found, axis=0)
+
+    for distance, value in enumerate(product(rows, ya_ref, yb_ref, len(blocks))):
         out_ref[distance] = value
         if distance > 0:
             back[distance - 1][...] = value.T
 
 
-def far_kernel(place, ya_ref, yb_ref, far_ref, near_ref, *refs):
+def far_kernel(place, ya_ref, yb_ref, a4_ref, b4_ref, near_ref, *refs):
     *back, out_ref = refs
     snaps = ya_ref.shape[0]
     rings = out_ref.shape[0] // 4
@@ -282,33 +281,33 @@
     for distance, received in enumerate(back, 1):
         put(distance, near_ref[distance])
         put(-distance, received[...])
-    (value,) = product(lambda _, at: far_ref[:, at], ya_ref, yb_ref, 1)
+    (value,) = product(lambda _, at: jnp.concatenate([a4_ref[:, at], b4_ref[:, at]], axis=0), ya_ref, yb_ref, 1)
     put(rings // 2, value)
 
 
-def near_call(ya, yb, a0, b0, streams):
+def near_call(ya, yb, *blocks):
     snaps = ya.shape[0]
     square = jax.ShapeDtypeStruct((2 * snaps, 2 * snaps), jnp.float32)
     return pl.pallas_call(
         near_kernel,
-        out_shape=[jax.ShapeDtypeStruct((1 + len(streams), 2 * snaps, 2 * snaps), jnp.float32)] + [square] * len(streams),
-        in_specs=[IN_VMEM] * (4 + len(streams)),
-        out_specs=[IN_VMEM] * (1 + len(streams)),
+        out_shape=[jax.ShapeDtypeStruct((4, 2 * snaps, 2 * snaps), jnp.float32)] + [square] * 3,
+        in_specs=[IN_VMEM] * (2 + len(blocks)),
+        out_specs=[IN_VMEM] * 4,
         compiler_params=pltpu.CompilerParams(vmem_limit_bytes=16 * MIB),
-        cost_estimate=cost(4),
-    )(ya, yb, a0, b0, *streams)
-
-
-def far_call(place, ya, yb, far, near, back, rings):
+        cost_estimate=cost(0.01),
+    )(ya, yb, *blocks)
+
+
+def far_call(place, ya, yb, a4, b4, near, back, rings):
     snaps = ya.shape[0]
     return pl.pallas_call(
         far_kernel,
         out_shape=jax.ShapeDtypeStruct((4 * rings, snaps // 2, 2 * snaps), jnp.float32),
-        in_specs=[IN_SMEM] + [IN_VMEM] * (4 + len(back)),
+        in_specs=[IN_SMEM] + [IN_VMEM] * (5 + len(back)),
         out_specs=IN_VMEM,
         compiler_params=pltpu.CompilerParams(vmem_limit_bytes=16 * MIB),
         cost_estimate=cost(2),
-    )(place, ya, yb, far, near, *back)
+    )(place, ya, yb, a4, b4, near, *back)
 
 
 def on_device(snapshots, connectivity, element_mass, lower_shared, upper_shared):
@@ -335,11 +334,12 @@
     rows, a1, b1, given = tied((rows, a1, b1, given))
     pair1 = jnp.concatenate([a1, b1], axis=0)
     pair2 = ring_hop(pair1, 1)
+    b3 = ring_hop(b1, 2)
     b0 = partner(given)
     rows, y_own, y_given = apply_call(1, columns, snapshots, rows, half_at)
 
     y_given, pair2, b0 = tied((y_given, pair2, b0))
-    pair3 = ring_hop(pair2, 1)
+    a3 = ring_hop(pair2[:snaps], 1)
     y_theirs = partner(y_given)
 
     shared = lower_shared.shape[0]
@@ -354,8 +354,14 @@
     )(lower_shared, upper_shared, rows)
     from_below = passed_along(high, "mesh", 1)
     from_above = passed_along(low, "mesh", -1)
-    from_below, from_above, pair3, y_theirs = tied((from_below, from_above, pair3, y_theirs))
-    pair4 = ring_hop(pair3, 1)
+    from_below, from_above, b3 = tied((from_below, from_above, b3))
+    b4 = ring_hop(b3, 1)
+    from_below, from_above, a3, y_theirs = tied((from_below, from_above, a3, y_theirs))
+    a4 = ring_hop(a3, 1)
+
+    near, *back = near_call(y_own, y_theirs, own, b0, pair1, pair2, a3, b3)
+    rows, near = tied((rows, near))
+    back = [ring_hop(value, -distance) for distance, value in enumerate(back, 1)]
     weighted = pl.pallas_call(
         assemble_kernel,
         out_shape=jax.ShapeDtypeStruct((snaps, nodes), jnp.float32),
@@ -366,12 +372,10 @@
         compiler_params=pltpu.CompilerParams(vmem_limit_bytes=20 * MIB),
         cost_estimate=cost(0.01),
     )(lower_shared, upper_shared, rows, from_below, from_above)
-    weighted, y_theirs = tied((weighted, y_theirs))
-
-    near, *back = near_call(y_own, y_theirs, own, b0, [pair1, pair2, pair3])
-    back = [ring_hop(value, -distance) for distance, value in enumerate(back, 1)]
+    weighted, *back = tied((weighted, *back))
+
     place = jnp.stack([z, h, jnp.where(position % 2 == 0, 1, -1)]).astype(jnp.int32)
-    tiles = far_call(place, y_own, y_theirs, pair4, near, back, rings)
+    tiles = far_call(place, y_own, y_theirs, a4, b4, near, back, rings)
     planes = [[m * blocks + 2 * r + c for m in range(parts) for c in range(2)] for r in range(rings)]
     tile = jnp.sum(lax.all_to_all(tiles, ("mesh", "snap"), 0, 0, axis_index_groups=planes, tiled=True), axis=0)
     column = jnp.concatenate([tile[:, :snaps], tile[:, snaps:]], axis=0)

time: 140 us -> 146 us (1.043)
  waiting for transfers between devices: 16.5 us -> 23.4 us
  Pallas kernels: 64 us -> 61.5 us
  local copies, waits for them, and re-layouts: 9.47 us -> 11 us
    ppermute x8 -> x10, starting transfers between devices: 16.9 us -> 20.1 us  [ring_hop(): return lax.ppermute(value, ('mesh', 'snap'), pairs)]
    ppermute x2, waiting for transfers between devices: 10.2 us -> 13.4 us  [passed_along(): lax.ppermute(value, axis, [(source, source + steps) for source in range(l...]
    ppermute x2, starting transfers between devices: 3.1 us -> 0.11 us  [partner(): lax.ppermute(value, 'snap', [(i, i ^ 1) for i in range(lax.axis_size('sna...]
    ppermute x8 -> x10, waiting for transfers between devices: 6.26 us -> 9.13 us  [ring_hop(): return lax.ppermute(value, ('mesh', 'snap'), pairs)]
    pallas_call x2, Pallas kernels: 49.9 us -> 47.5 us  [apply_call(): pl.pallas_call(functools.partial(apply_kernel, first, last, start, count,...]
  transfers between devices with their start and end apart: 12 -> 14, of which waited for: 5 -> 4; matrix products, arithmetic and copies ran while one was open for 0% -> 0% of each run, Pallas kernels for 44% -> 41%
where the time goes in v6:
time: 146 us; the launch traced here: 145 us
  Pallas kernels  61.5 us (42%)
  starting transfers between devices  25.7 us (18%)
  waiting for transfers between devices  23.4 us (16%)
  blocking collectives  22.6 us (15%)
  local copies, waits for them, and re-layouts  11 us (8%)
    pallas_call x2, Pallas kernels, apply_call(): pl.pallas_call(functools.partial(apply_kernel, first, last, start, count,...  47.5 us
    all_to_all x1, blocking collectives, on_device(): lax.all_to_all(tiles, ('mesh', 'snap'), 0, 0, axis_index_groups=planes, t...  22.6 us
    ppermute x10, starting transfers between devices, ring_hop(): return lax.ppermute(value, ('mesh', 'snap'), pairs)  20.1 us
    ppermute x2, waiting for transfers between devices, passed_along(): lax.ppermute(value, axis, [(source, source + steps) for source in range(l...  13.4 us
    ppermute x10, waiting for transfers between devices, ring_hop(): return lax.ppermute(value, ('mesh', 'snap'), pairs)  9.13 us
    unnamed x40, local copies, waits for them, and re-layouts  9.08 us
    ppermute x2, starting transfers between devices, passed_along(): lax.ppermute(value, axis, [(source, source + steps) for source in range(l...  5.46 us
    pallas_call x1, Pallas kernels, on_device(): pl.pallas_call(assemble_kernel, out_shape=jax.ShapeDtypeStruct((snaps, no...  5.46 us
  transfers between devices with their start and end apart: 14, of which 4 were waited for; matrix products, arithmetic and copies ran while one was open for 0% of the time, Pallas kernels for 41%

profile of v6, /device:TPU:1, one launch (start us, length us, event | category | flops | bytes accessed | tf_op | source)
XLA Modules:
  0.0 145.4 jit_solution(9942099850912428068)
XLA Ops:
  0.7 1.6 %constant_dynamic-slice_fusion = (f32[64,3072]{1,0:T(8,128)S(1)}, f32[64,3072]{1,0:T(8,128)S(1)}) fusion(f32[64,6144]{1,0:T(8,128)} %refs_4_.3, s32[]{:T(128)S(6)} %select_n.27, s32[]{:T(128)S(6)} %select_n.26), kind=kLoop, calls=%fused_computation.6 | loop fusion | bytes 3145736 | tf_op jit(solution)/shard_map/dynamic_slice | solution.py:325
  2.3 6.5 %collective-permute-start = (f32[64,3072]{1,0:T(8,128)S(1)}, f32[64,3072]{1,0:T(8,128)S(1)}, u32[]{:S(2)}, u32[]{:S(2)}) collective-permute-start(f32[64,3072]{1,0:T(8,128)S(1)} %get-tuple-element.63.a0_ref), channel_id=1, source_target_pairs={{0,2},{1,3},{2,4},{3,5},{4,6},{5,7},{6,8},{7,9},{8,10},{9,11},{10,... | collective-permute-start | bytes 2359304 | tf_op jit(solution)/shard_map/ppermute | solution.py:24
  8.8 3.4 %collective-permute-start.1 = (f32[64,3072]{1,0:T(8,128)S(1)}, f32[64,3072]{1,0:T(8,128)S(1)}, u32[]{:S(2)}, u32[]{:S(2)}) collective-permute-start(f32[64,3072]{1,0:T(8,128)S(1)} %get-tuple-element.41), channel_id=1, source_target_pairs={{0,3},{1,2},{2,5},{3,4},{4,7},{5,6},{6,9},{7,8},{8,11},{9,10},{10,... | collective-permute-start | bytes 2359304 | tf_op jit(solution)/shard_map/ppermute | solution.py:24
  12.2 0.1 fusion.1
  12.4 22.7 %shard_map.68.refs_5_ = f32[6144,128]{1,0:T(8,128)S(1)} custom-call(s32[12288]{0:T(1024)S(1)} %bitcast.12, s32[12288]{0:T(1024)S(1)} %bitcast.10, s32[12288]{0:T(1024)S(1)} %bitcast.8, f32[12288]{0:T(1024)S(1)} %copy-done.17, f32[64,6144]{1,0:T(8,128)S(1)} %copy-done.6), custom_call_target="tpu_custom_call" | custom-call | flops 20000000000 | bytes 60000000 | tf_op jit(solution)/shard_map/pallas_call | solution.py:215
  35.2 3.3 %collective-permute-start.4 = (f32[64,3072]{1,0:T(8,128)S(1)}, f32[64,3072]{1,0:T(8,128)}, u32[]{:S(2)}, u32[]{:S(2)}) collective-permute-start(f32[64,3072]{1,0:T(8,128)S(1)} %collective-permute-done.1), channel_id=1, source_target_pairs={{0,4},{1,5},{2,6},{3,7},{4,8},{5,9},{6,10},{7,11},{8,12},{9,13},{1... | collective-permute-start | bytes 2359304 | tf_op jit(solution)/shard_map/ppermute | solution.py:24
  38.6 0.8 collective-permute-start.5
  39.4 24.7 %shard_map.69 = (f32[6144,128]{1,0:T(8,128)S(1)}, f32[64,3072]{1,0:T(8,128)S(1)}, f32[64,3072]{1,0:T(8,128)S(1)}) custom-call(s32[12288]{0:T(1024)S(1)} %bitcast.13, s32[12288]{0:T(1024)S(1)} %bitcast.11, s32[12288]{0:T(1024)S(1)} %bitcast.9, f32[12288]{0:T(1024)S(1)} %copy-done.17, f32[64,6144]{1,0:T(8,128)S(1)} %copy-done.6, ...), custom_call_target="tpu_custom_call" | custom-call | flops 20000000000 | bytes 60000000 | tf_op jit(solution)/shard_map/pallas_call | solution.py:215
  64.3 9.1 %collective-permute-done.5.pair2_ref = f32[128,3072]{1,0:T(8,128)S(1)} collective-permute-done((f32[128,3072]{1,0:T(8,128)S(1)}, f32[128,3072]{1,0:T(8,128)S(1)}, u32[]{:S(2)}, u32[]{:S(2)}) %collective-permute-start.5) | collective-permute-done | bytes 1572896 | tf_op jit(solution)/shard_map/ppermute | solution.py:24
  73.4 2.5 %collective-permute-start.7 = (f32[64,3072]{1,0:T(8,128)S(1)}, f32[64,3072]{1,0:T(8,128)}, u32[]{:S(2)}, u32[]{:S(2)}) collective-permute-start(f32[64,3072]{1,0:T(8,128)S(1)} %slice.21), channel_id=1, source_target_pairs={{0,2},{1,3},{2,4},{3,5},{4,6},{5,7},{6,8},{7,9},{8,10},{9,11},{10,... | collective-permute-start | bytes 2359304 | tf_op jit(solution)/shard_map/ppermute | solution.py:24
  76.0 2.0 %shard_map.70 = (f32[64,512]{1,0:T(8,128)S(1)}, f32[64,512]{1,0:T(8,128)S(1)}) custom-call(s32[512]{0:T(512)S(1)} %copy-done.15, s32[512]{0:T(512)S(1)} %copy-done.16, f32[6144,128]{1,0:T(8,128)S(1)} %get-tuple-element.49.rows.rows_ref), custom_call_target="tpu_custom_call" | custom-call | flops 10000000 | bytes 30000 | tf_op jit(solution)/shard_map/pallas_call | solution.py:346
  78.0 3.5 %collective-permute-start.2 = (f32[64,512]{1,0:T(8,128)S(1)}, f32[64,512]{1,0:T(8,128)S(1)}, u32[]{:S(2)}, u32[]{:S(2)}) collective-permute-start(f32[64,512]{1,0:T(8,128)S(1)} %get-tuple-element.34), channel_id=1, source_target_pairs={{0,16},{16,32},{32,48},{48,64},{64,80},{80,96},{96,112},{112,128},... | collective-permute-start | bytes 393224 | tf_op jit(solution)/shard_map/ppermute | solution.py:30
  81.5 1.9 %collective-permute-start.3 = (f32[64,512]{1,0:T(8,128)S(1)}, f32[64,512]{1,0:T(8,128)S(1)}, u32[]{:S(2)}, u32[]{:S(2)}) collective-permute-start(f32[64,512]{1,0:T(8,128)S(1)} %get-tuple-element.35), channel_id=1, source_target_pairs={{16,0},{32,16},{48,32},{64,48},{80,64},{96,80},{112,96},{128,112},... | collective-permute-start | bytes 393224 | tf_op jit(solution)/shard_map/ppermute | solution.py:30
  83.4 12.7 %collective-permute-done.2.below_ref = f32[64,512]{1,0:T(8,128)S(1)} collective-permute-done((f32[64,512]{1,0:T(8,128)S(1)}, f32[64,512]{1,0:T(8,128)S(1)}, u32[]{:S(2)}, u32[]{:S(2)}) %collective-permute-start.2) | collective-permute-done | bytes 131104 | tf_op jit(solution)/shard_map/ppermute | solution.py:30
  96.1 0.7 collective-permute-done.3.above_ref
  97.0 0.8 collective-permute-done.8.yb_ref
  97.8 0.9 copy-done.10
  98.7 0.1 collective-permute-start.12
  98.8 1.4 copy-done.1
  100.3 1.4 copy-done.3
  101.7 1.1 copy-done.5
  102.8 1.1 copy-done.8
  103.9 1.1 copy-done.11
  105.1 1.1 copy-done.14
  106.2 4.3 %shard_map.71 = (f32[4,128,128]{2,1,0:T(8,128)S(1)}, f32[128,128]{1,0:T(8,128)S(1)}, f32[128,128]{1,0:T(8,128)S(1)}, f32[128,128]{1,0:T(8,128)S(1)}) custom-call(f32[64,3072]{1,0:T(8,128)S(1)} %copy-done.8, f32[64,3072]{1,0:T(8,128)S(1)} %copy-done.11, f32[64,3072]{1,0:T(8,128)S(1)} %copy-done.5, f32[64,3072]{1,0:T(8,128)S(1)} %copy-done.14, ...), custom_call_target="tpu_custom_call" | custom-call | flops 10000000 | bytes 30000 | tf_op jit(solution)/shard_map/pallas_call | solution.py:291
  110.5 1.4 collective-permute-start.9
  111.9 0.5 collective-permute-start.10
  112.5 1.6 %collective-permute-start.11 = (f32[128,128]{1,0:T(8,128)S(1)}, f32[128,128]{1,0:T(8,128)S(1)}, u32[]{:S(2)}, u32[]{:S(2)}) collective-permute-start(f32[128,128]{1,0:T(8,128)S(1)} %get-tuple-element.54), channel_id=1, source_target_pairs={{0,10},{1,11},{2,12},{3,13},{4,14},{5,15},{6,0},{7,1},{8,2},{9,3},... | collective-permute-start | bytes 196616 | tf_op jit(solution)/shard_map/ppermute | solution.py:24
  114.1 5.5 %shard_map.72 = f32[64,6144]{1,0:T(8,128)} custom-call(s32[512]{0:T(512)S(1)} %copy-done.15, s32[512]{0:T(512)S(1)} %copy-done.16, f32[6144,128]{1,0:T(8,128)S(1)} %get-tuple-element.49.rows.rows_ref, f32[64,512]{1,0:T(8,128)S(1)} %collective-permute-done.2.below_ref, f32[64,512]{1,0:T(8,128)S(1)} %collective-permute-done.3.above_ref), custom_call_target="tpu_custom_call" | custom-call | flops 10000000 | bytes 30000 | tf_op jit(solution)/shard_map/pallas_call | solution.py:365
  119.6 2.3 %shard_map.73 = f32[32,32,128]{2,1,0:T(8,128)S(1)} custom-call(s32[3]{0:T(128)S(1)} %pad_add_fusion.place, f32[64,3072]{1,0:T(8,128)S(1)} %copy-done.9, f32[64,3072]{1,0:T(8,128)S(1)} %copy-done.12, f32[64,3072]{1,0:T(8,128)} %collective-permute-done.12.a4_ref, f32[64,3072]{1,0:T(8,128)} %collective-permute-done.13.b4_ref, ...), custom_call_target="tpu_custom_call" | custom-call | flops 2000000000 | bytes 6000000 | tf_op jit(solution)/shard_map/pallas_call | solution.py:303
  121.9 22.6 %all_to_all.5 = f32[32,32,128]{2,1,0:T(8,128)S(1)} all-to-all(f32[32,32,128]{2,1,0:T(8,128)S(1)} %shard_map.73), channel_id=1, replica_groups={{0,1,16,17,32,33,48,49,64,65,80,81,96,97,112,113,128,129,144,145,160,16..., dimensions={0} | all-to-all | bytes 1048576 | tf_op jit(solution)/shard_map/all_to_all | solution.py:380
  144.7 0.7 copy.7
  (52 shorter events, 0.7 us)
Async XLA Ops:
  0.7 11.5 %copy-start.18 = (s32[3,12288]{1,0:T(4,128)S(1)}, s32[3,12288]{1,0:T(4,128)}, u32[]{:S(2)}) copy-start(s32[3,12288]{1,0:T(4,128)} %param.6) | copy-start | bytes 442372
  0.7 11.7 %copy-start.6 = (f32[64,6144]{1,0:T(8,128)S(1)}, f32[64,6144]{1,0:T(8,128)}, u32[]{:S(2)}) copy-start(f32[64,6144]{1,0:T(8,128)} %refs_4_.3) | copy-start | bytes 4718596
  0.7 11.7 %copy-start.17 = (f32[12288]{0:T(1024)S(1)}, f32[12288]{0:T(1024)}, u32[]{:S(2)}) copy-start(f32[12288]{0:T(1024)} %refs_3_.3) | copy-start | bytes 147460
  2.3 32.8 %copy-start.4 = (f32[64,3072]{1,0:T(8,128)}, f32[64,3072]{1,0:T(8,128)S(1)}, u32[]{:S(2)}) copy-start(f32[64,3072]{1,0:T(8,128)S(1)} %get-tuple-element.63.a0_ref) | copy-start | bytes 2359300
  2.3 32.8 %collective-permute-start = (f32[64,3072]{1,0:T(8,128)S(1)}, f32[64,3072]{1,0:T(8,128)S(1)}, u32[]{:S(2)}, u32[]{:S(2)}) collective-permute-start(f32[64,3072]{1,0:T(8,128)S(1)} %get-tuple-element.63.a0_ref), channel_id=1, source_target_pairs={{0,2},{1,3},{2,4},{3,5},{4,6},{5,7},{6,8},{7,9},{8,10},{9,11},{10,... | collective-permute-start | bytes 2359304 | tf_op jit(solution)/shard_map/ppermute | solution.py:24
  8.8 26.3 %collective-permute-start.1 = (f32[64,3072]{1,0:T(8,128)S(1)}, f32[64,3072]{1,0:T(8,128)S(1)}, u32[]{:S(2)}, u32[]{:S(2)}) collective-permute-start(f32[64,3072]{1,0:T(8,128)S(1)} %get-tuple-element.41), channel_id=1, source_target_pairs={{0,3},{1,2},{2,5},{3,4},{4,7},{5,6},{6,9},{7,8},{8,11},{9,10},{10,... | collective-permute-start | bytes 2359304 | tf_op jit(solution)/shard_map/ppermute | solution.py:24
  35.2 61.7 %collective-permute-start.4 = (f32[64,3072]{1,0:T(8,128)S(1)}, f32[64,3072]{1,0:T(8,128)}, u32[]{:S(2)}, u32[]{:S(2)}) collective-permute-start(f32[64,3072]{1,0:T(8,128)S(1)} %collective-permute-done.1), channel_id=1, source_target_pairs={{0,4},{1,5},{2,6},{3,7},{4,8},{5,9},{6,10},{7,11},{8,12},{9,13},{1... | collective-permute-start | bytes 2359304 | tf_op jit(solution)/shard_map/ppermute | solution.py:24
  38.6 25.6 %copy-start.2 = (f32[128,3072]{1,0:T(8,128)}, f32[128,3072]{1,0:T(8,128)S(1)}, u32[]{:S(2)}) copy-start(f32[128,3072]{1,0:T(8,128)S(1)} %constant_dynamic-update-slice_fusion.pair1_ref) | copy-start | bytes 4718596
  38.6 34.8 %collective-permute-start.5 = (f32[128,3072]{1,0:T(8,128)S(1)}, f32[128,3072]{1,0:T(8,128)S(1)}, u32[]{:S(2)}, u32[]{:S(2)}) collective-permute-start(f32[128,3072]{1,0:T(8,128)S(1)} %constant_dynamic-update-slice_fusion.pair1_ref), channel_id=1, source_target_pairs={{0,2},{1,3},{2,4},{3,5},{4,6},{5,7},{6,8},{7,9},{8,10},{9,11},{10,... | collective-permute-start | bytes 4718600 | tf_op jit(solution)/shard_map/ppermute | solution.py:24
  39.4 24.9 %collective-permute-start.6 = (f32[64,3072]{1,0:T(8,128)S(1)}, f32[64,3072]{1,0:T(8,128)S(1)}, u32[]{:S(2)}, u32[]{:S(2)}) collective-permute-start(f32[64,3072]{1,0:T(8,128)S(1)} %get-tuple-element.41), channel_id=1, source_target_pairs={{0,1},{1,0},{2,3},{3,2},{4,5},{5,4},{6,7},{7,6},{8,9},{9,8},{10,11... | collective-permute-start | bytes 2359304 | tf_op jit(solution)/shard_map/ppermute | solution.py:34
  64.2 13.7 %copy-start.7 = (f32[64,3072]{1,0:T(8,128)}, f32[64,3072]{1,0:T(8,128)S(1)}, u32[]{:S(2)}) copy-start(f32[64,3072]{1,0:T(8,128)S(1)} %get-tuple-element.33.ya_ref) | copy-start | bytes 2359300
  64.2 11.8 %copy-start.15 = (s32[512]{0:T(512)S(1)}, s32[512]{0:T(512)}, u32[]{:S(2)}) copy-start(s32[512]{0:T(512)} %low_s.3) | copy-start | bytes 6148
  64.2 11.7 %copy-start.16 = (s32[512]{0:T(512)S(1)}, s32[512]{0:T(512)}, u32[]{:S(2)}) copy-start(s32[512]{0:T(512)} %up_s.3) | copy-start | bytes 6148
  64.2 13.7 %copy-start.13 = (f32[64,3072]{1,0:T(8,128)}, f32[64,3072]{1,0:T(8,128)S(1)}, u32[]{:S(2)}) copy-start(f32[64,3072]{1,0:T(8,128)S(1)} %collective-permute-done.6.b0_ref) | copy-start | bytes 2359300
  73.4 4.6 %copy-start = (f32[128,3072]{1,0:T(8,128)}, f32[128,3072]{1,0:T(8,128)S(1)}, u32[]{:S(2)}) copy-start(f32[128,3072]{1,0:T(8,128)S(1)} %collective-permute-done.5.pair2_ref) | copy-start | bytes 4718596
  73.4 23.6 %collective-permute-start.7 = (f32[64,3072]{1,0:T(8,128)S(1)}, f32[64,3072]{1,0:T(8,128)}, u32[]{:S(2)}, u32[]{:S(2)}) collective-permute-start(f32[64,3072]{1,0:T(8,128)S(1)} %slice.21), channel_id=1, source_target_pairs={{0,2},{1,3},{2,4},{3,5},{4,6},{5,7},{6,8},{7,9},{8,10},{9,11},{10,... | collective-permute-start | bytes 2359304 | tf_op jit(solution)/shard_map/ppermute | solution.py:24
  75.9 21.9 %collective-permute-start.8 = (f32[64,3072]{1,0:T(8,128)S(1)}, f32[64,3072]{1,0:T(8,128)S(1)}, u32[]{:S(2)}, u32[]{:S(2)}) collective-permute-start(f32[64,3072]{1,0:T(8,128)S(1)} %get-tuple-element.43), channel_id=1, source_target_pairs={{0,1},{1,0},{2,3},{3,2},{4,5},{5,4},{6,7},{7,6},{8,9},{9,8},{10,11... | collective-permute-start | bytes 2359304 | tf_op jit(solution)/shard_map/ppermute | solution.py:34
  78.0 18.2 %collective-permute-start.2 = (f32[64,512]{1,0:T(8,128)S(1)}, f32[64,512]{1,0:T(8,128)S(1)}, u32[]{:S(2)}, u32[]{:S(2)}) collective-permute-start(f32[64,512]{1,0:T(8,128)S(1)} %get-tuple-element.34), channel_id=1, source_target_pairs={{0,16},{16,32},{32,48},{48,64},{64,80},{80,96},{96,112},{112,128},... | collective-permute-start | bytes 393224 | tf_op jit(solution)/shard_map/ppermute | solution.py:30
  81.5 15.4 %collective-permute-start.3 = (f32[64,512]{1,0:T(8,128)S(1)}, f32[64,512]{1,0:T(8,128)S(1)}, u32[]{:S(2)}, u32[]{:S(2)}) collective-permute-start(f32[64,512]{1,0:T(8,128)S(1)} %get-tuple-element.35), channel_id=1, source_target_pairs={{16,0},{32,16},{48,32},{64,48},{80,64},{96,80},{112,96},{128,112},... | collective-permute-start | bytes 393224 | tf_op jit(solution)/shard_map/ppermute | solution.py:30
  96.9 22.7 %collective-permute-start.13 = (f32[64,3072]{1,0:T(8,128)}, f32[64,3072]{1,0:T(8,128)}, u32[]{:S(2)}, u32[]{:S(2)}) collective-permute-start(f32[64,3072]{1,0:T(8,128)} %collective-permute-done.4.b3_ref), channel_id=1, source_target_pairs={{0,2},{1,3},{2,4},{3,5},{4,6},{5,7},{6,8},{7,9},{8,10},{9,11},{10,... | collective-permute-start | bytes 2359304 | tf_op jit(solution)/shard_map/ppermute | solution.py:24
  98.7 20.9 %collective-permute-start.12 = (f32[64,3072]{1,0:T(8,128)}, f32[64,3072]{1,0:T(8,128)}, u32[]{:S(2)}, u32[]{:S(2)}) collective-permute-start(f32[64,3072]{1,0:T(8,128)} %collective-permute-done.7.a3_ref), channel_id=1, source_target_pairs={{0,2},{1,3},{2,4},{3,5},{4,6},{5,7},{6,8},{7,9},{8,10},{9,11},{10,... | collective-permute-start | bytes 2359304 | tf_op jit(solution)/shard_map/ppermute | solution.py:24
  98.8 1.4 copy-start.1
  100.3 1.4 copy-start.3
  101.7 1.1 copy-start.5
  102.8 1.1 copy-start.8
  103.9 1.1 copy-start.11
  105.1 1.1 copy-start.14
  110.5 9.1 %collective-permute-start.9 = (f32[128,128]{1,0:T(8,128)S(1)}, f32[128,128]{1,0:T(8,128)S(1)}, u32[]{:S(2)}, u32[]{:S(2)}) collective-permute-start(f32[128,128]{1,0:T(8,128)S(1)} %get-tuple-element.52), channel_id=1, source_target_pairs={{0,14},{1,15},{2,0},{3,1},{4,2},{5,3},{6,4},{7,5},{8,6},{9,7},{10,... | collective-permute-start | bytes 196616 | tf_op jit(solution)/shard_map/ppermute | solution.py:24
  111.9 7.6 %collective-permute-start.10 = (f32[128,128]{1,0:T(8,128)S(1)}, f32[128,128]{1,0:T(8,128)S(1)}, u32[]{:S(2)}, u32[]{:S(2)}) collective-permute-start(f32[128,128]{1,0:T(8,128)S(1)} %get-tuple-element.53), channel_id=1, source_target_pairs={{0,12},{1,13},{2,14},{3,15},{4,0},{5,1},{6,2},{7,3},{8,4},{9,5},{1... | collective-permute-start | bytes 196616 | tf_op jit(solution)/shard_map/ppermute | solution.py:24
  112.5 7.1 %collective-permute-start.11 = (f32[128,128]{1,0:T(8,128)S(1)}, f32[128,128]{1,0:T(8,128)S(1)}, u32[]{:S(2)}, u32[]{:S(2)}) collective-permute-start(f32[128,128]{1,0:T(8,128)S(1)} %get-tuple-element.54), channel_id=1, source_target_pairs={{0,10},{1,11},{2,12},{3,13},{4,14},{5,15},{6,0},{7,1},{8,2},{9,3},... | collective-permute-start | bytes 196616 | tf_op jit(solution)/shard_map/ppermute | solution.py:24
  114.1 5.5 %copy-start.9 = (f32[64,3072]{1,0:T(8,128)S(1)}, f32[64,3072]{1,0:T(8,128)}, u32[]{:S(2)}) copy-start(f32[64,3072]{1,0:T(8,128)} %copy-done.7) | copy-start | bytes 2359300
  114.1 5.5 %copy-start.12 = (f32[64,3072]{1,0:T(8,128)S(1)}, f32[64,3072]{1,0:T(8,128)}, u32[]{:S(2)}) copy-start(f32[64,3072]{1,0:T(8,128)} %copy-done.10) | copy-start | bytes 2359300
  (1 other events, 0.9 us)

commit v7 on v5

--- a/solution.py
+++ b/solution.py
@@ -221,7 +221,7 @@
         + [pltpu.SMEM((count,), jnp.float32), pltpu.SemaphoreType.DMA((4,))]
         + [pltpu.VMEM((nodes, LANES), jnp.float32), pltpu.SemaphoreType.DMA, pltpu.SemaphoreType.DMA((4,))]
         + [pltpu.VMEM((nodes * (1 + PARTS), LANES), jnp.float32)] * ARRAYS,
-        compiler_params=pltpu.CompilerParams(vmem_limit_bytes=52 * MIB),
+        compiler_params=pltpu.CompilerParams(vmem_limit_bytes=44 * MIB),
         cost_estimate=cost(20),
     )(*operands)
 
@@ -249,15 +249,19 @@
     return totals
 
 
-def near_kernel(ya_ref, yb_ref, a0_ref, b0_ref, *refs):
-    streams, out_ref, back = refs[:3], refs[3], refs[4:]
-
-    def rows(distance, at):
-        if distance == 0:
-            return jnp.concatenate([a0_ref[:, at], b0_ref[:, at]], axis=0)
-        return streams[distance - 1][:, at]
-
-    for distance, value in enumerate(product(rows, ya_ref, yb_ref, 1 + len(streams))):
+def near_kernel(*refs):
+    sources, refs = refs[:7], refs[7:]
+    out_ref, back, held, sems = refs[0], refs[1:4], refs[4:11], refs[11]
+    copies = [pltpu.make_async_copy(source, target, sems.at[i]) for i, (source, target) in enumerate(zip(sources, held))]
+    for copy in copies:
+        copy.start()
+    y_refs, blocks = held[:2], (held[2:4], held[4:5], held[5:6], held[6:7])
+    waits = (copies[:4], copies[4:5], copies[5:6], copies[6:7])
+    for distance, (block, waited) in enumerate(zip(blocks, waits)):
+        for copy in waited:
+            copy.wait()
+        (value,) = product(lambda _, at, block=block: jnp.concatenate([ref[:, at] for ref in block], axis=0),
+                           *y_refs, 1)
         out_ref[distance] = value
         if distance > 0:
             back[distance - 1][...] = value.T
@@ -286,17 +290,19 @@
     put(rings // 2, value)
 
 
-def near_call(ya, yb, a0, b0, streams):
-    snaps = ya.shape[0]
+def near_call(*operands):
+    snaps = operands[0].shape[0]
     square = jax.ShapeDtypeStruct((2 * snaps, 2 * snaps), jnp.float32)
     return pl.pallas_call(
         near_kernel,
-        out_shape=[jax.ShapeDtypeStruct((1 + len(streams), 2 * snaps, 2 * snaps), jnp.float32)] + [square] * len(streams),
-        in_specs=[IN_VMEM] * (4 + len(streams)),
-        out_specs=[IN_VMEM] * (1 + len(streams)),
-        compiler_params=pltpu.CompilerParams(vmem_limit_bytes=16 * MIB),
-        cost_estimate=cost(4),
-    )(ya, yb, a0, b0, *streams)
+        out_shape=[jax.ShapeDtypeStruct((4, 2 * snaps, 2 * snaps), jnp.float32)] + [square] * 3,
+        in_specs=[ANYWHERE] * len(operands),
+        out_specs=[IN_VMEM] * 4,
+        scratch_shapes=[pltpu.VMEM(operand.shape, operand.dtype) for operand in operands]
+        + [pltpu.SemaphoreType.DMA((len(operands),))],
+        compiler_params=pltpu.CompilerParams(vmem_limit_bytes=20 * MIB),
+        cost_estimate=cost(0.01),
+    )(*operands)
 
 
 def far_call(place, ya, yb, far, near, back, rings):
@@ -356,6 +362,9 @@
     from_above = passed_along(low, "mesh", -1)
     from_below, from_above, pair3, y_theirs = tied((from_below, from_above, pair3, y_theirs))
     pair4 = ring_hop(pair3, 1)
+    near, *back = near_call(y_own, y_theirs, own, b0, pair1, pair2, pair3)
+    rows, near = tied((rows, near))
+    back = [ring_hop(value, -distance) for distance, value in enumerate(back, 1)]
     weighted = pl.pallas_call(
         assemble_kernel,
         out_shape=jax.ShapeDtypeStruct((snaps, nodes), jnp.float32),
@@ -366,10 +375,7 @@
         compiler_params=pltpu.CompilerParams(vmem_limit_bytes=20 * MIB),
         cost_estimate=cost(0.01),
     )(lower_shared, upper_shared, rows, from_below, from_above)
-    weighted, y_theirs = tied((weighted, y_theirs))
-
-    near, *back = near_call(y_own, y_theirs, own, b0, [pair1, pair2, pair3])
-    back = [ring_hop(value, -distance) for distance, value in enumerate(back, 1)]
+    weighted, *back = tied((weighted, *back))
     place = jnp.stack([z, h, jnp.where(position % 2 == 0, 1, -1)]).astype(jnp.int32)
     tiles = far_call(place, y_own, y_theirs, pair4, near, back, rings)
     planes = [[m * blocks + 2 * r + c for m in range(parts) for c in range(2)] for r in range(rings)]

time: 140 us -> 137 us (0.979)
  Pallas kernels: 64 us -> 61.3 us
  local copies, waits for them, and re-layouts: 9.47 us -> 10.9 us
    ppermute x8, waiting for transfers between devices: 6.26 us -> 2.93 us  [ring_hop(): return lax.ppermute(value, ('mesh', 'snap'), pairs)]
    ppermute x2, waiting for transfers between devices: 10.2 us -> 12.9 us  [passed_along(): lax.ppermute(value, axis, [(source, source + steps) for source in range(l...]
    pallas_call x2, Pallas kernels: 49.9 us -> 47.5 us  [apply_call(): pl.pallas_call(functools.partial(apply_kernel, first, last, start, count,...]
    unnamed x40 -> x36, local copies, waits for them, and re-layouts: 7.63 us -> 9.04 us
  transfers between devices with their start and end apart: 12 -> 12, of which waited for: 5 -> 3; matrix products, arithmetic and copies ran while one was open for 0% -> 0% of each run, Pallas kernels for 44% -> 43%
where the time goes in v7:
time: 137 us; the launch traced here: 136 us
  Pallas kernels  61.3 us (45%)
  starting transfers between devices  25.3 us (18%)
  blocking collectives  21.8 us (16%)
  waiting for transfers between devices  15.9 us (12%)
  local copies, waits for them, and re-layouts  10.9 us (8%)
    pallas_call x2, Pallas kernels, apply_call(): pl.pallas_call(functools.partial(apply_kernel, first, last, start, count,...  47.5 us
    all_to_all x1, blocking collectives, on_device(): lax.all_to_all(tiles, ('mesh', 'snap'), 0, 0, axis_index_groups=planes, t...  21.8 us
    ppermute x8, starting transfers between devices, ring_hop(): return lax.ppermute(value, ('mesh', 'snap'), pairs)  16.9 us
    ppermute x2, waiting for transfers between devices, passed_along(): lax.ppermute(value, axis, [(source, source + steps) for source in range(l...  12.9 us
    unnamed x36, local copies, waits for them, and re-layouts  9.04 us
    pallas_call x1, Pallas kernels, on_device(): pl.pallas_call(assemble_kernel, out_shape=jax.ShapeDtypeStruct((snaps, no...  5.46 us
    ppermute x2, starting transfers between devices, passed_along(): lax.ppermute(value, axis, [(source, source + steps) for source in range(l...  5.26 us
    pallas_call x1, Pallas kernels, near_call(): pl.pallas_call(near_kernel, out_shape=[jax.ShapeDtypeStruct((4, 2 * snaps...  4.07 us
  transfers between devices with their start and end apart: 12, of which 3 were waited for; matrix products, arithmetic and copies ran while one was open for 0% of the time, Pallas kernels for 43%

profile of v7, /device:TPU:1, one launch (start us, length us, event | category | flops | bytes accessed | tf_op | source)
XLA Modules:
  0.0 136.2 jit_solution(17845237222711480719)
XLA Ops:
  0.7 1.6 %constant_dynamic-slice_fusion = (f32[64,3072]{1,0:T(8,128)S(1)}, f32[64,3072]{1,0:T(8,128)S(1)}) fusion(f32[64,6144]{1,0:T(8,128)} %refs_4_.3, s32[]{:T(128)S(6)} %select_n.27, s32[]{:T(128)S(6)} %select_n.26), kind=kLoop, calls=%fused_computation.6 | loop fusion | bytes 3145736 | tf_op jit(solution)/shard_map/dynamic_slice | solution.py:332
  2.3 9.1 %collective-permute-start.1 = (f32[64,3072]{1,0:T(8,128)S(1)}, f32[64,3072]{1,0:T(8,128)S(1)}, u32[]{:S(2)}, u32[]{:S(2)}) collective-permute-start(f32[64,3072]{1,0:T(8,128)S(1)} %get-tuple-element.36), channel_id=1, source_target_pairs={{0,3},{1,2},{2,5},{3,4},{4,7},{5,6},{6,9},{7,8},{8,11},{9,10},{10,... | collective-permute-start | bytes 2359304 | tf_op jit(solution)/shard_map/ppermute | solution.py:24
  11.4 0.7 collective-permute-start
  12.2 0.1 fusion.1
  12.3 22.7 %shard_map.68.refs_5_ = f32[6144,128]{1,0:T(8,128)S(1)} custom-call(s32[12288]{0:T(1024)S(1)} %bitcast.12, s32[12288]{0:T(1024)S(1)} %bitcast.10, s32[12288]{0:T(1024)S(1)} %bitcast.8, f32[12288]{0:T(1024)S(1)} %copy-done.15, f32[64,6144]{1,0:T(8,128)S(1)} %copy-done.4), custom_call_target="tpu_custom_call" | custom-call | flops 20000000000 | bytes 60000000 | tf_op jit(solution)/shard_map/pallas_call | solution.py:215
  35.1 0.1 collective-permute-start.5
  35.4 1.1 collective-permute-start.4
  36.5 24.7 %shard_map.69 = (f32[6144,128]{1,0:T(8,128)S(1)}, f32[64,3072]{1,0:T(8,128)S(1)}, f32[64,3072]{1,0:T(8,128)S(1)}) custom-call(s32[12288]{0:T(1024)S(1)} %bitcast.13, s32[12288]{0:T(1024)S(1)} %bitcast.11, s32[12288]{0:T(1024)S(1)} %bitcast.9, f32[12288]{0:T(1024)S(1)} %copy-done.15, f32[64,6144]{1,0:T(8,128)S(1)} %copy-done.4, ...), custom_call_target="tpu_custom_call" | custom-call | flops 20000000000 | bytes 60000000 | tf_op jit(solution)/shard_map/pallas_call | solution.py:215
  61.3 1.8 %collective-permute-start.6 = (f32[128,3072]{1,0:T(8,128)S(1)}, f32[128,3072]{1,0:T(8,128)}, u32[]{:S(2)}, u32[]{:S(2)}) collective-permute-start(f32[128,3072]{1,0:T(8,128)S(1)} %collective-permute-done.4.refs_5_), channel_id=1, source_target_pairs={{0,2},{1,3},{2,4},{3,5},{4,6},{5,7},{6,8},{7,9},{8,10},{9,11},{10,... | collective-permute-start | bytes 4718600 | tf_op jit(solution)/shard_map/ppermute | solution.py:24
  63.1 2.9 %collective-permute-start.7 = (f32[64,3072]{1,0:T(8,128)S(1)}, f32[64,3072]{1,0:T(8,128)S(1)}, u32[]{:S(2)}, u32[]{:S(2)}) collective-permute-start(f32[64,3072]{1,0:T(8,128)S(1)} %get-tuple-element.38), channel_id=1, source_target_pairs={{0,1},{1,0},{2,3},{3,2},{4,5},{5,4},{6,7},{7,6},{8,9},{9,8},{10,11... | collective-permute-start | bytes 2359304 | tf_op jit(solution)/shard_map/ppermute | solution.py:34
  66.1 2.0 %shard_map.70 = (f32[64,512]{1,0:T(8,128)S(1)}, f32[64,512]{1,0:T(8,128)S(1)}) custom-call(s32[512]{0:T(512)S(1)} %copy-done.13, s32[512]{0:T(512)S(1)} %copy-done.14, f32[6144,128]{1,0:T(8,128)S(1)} %get-tuple-element.43.rows.rows_ref), custom_call_target="tpu_custom_call" | custom-call | flops 10000000 | bytes 30000 | tf_op jit(solution)/shard_map/pallas_call | solution.py:352
  68.0 3.3 %collective-permute-start.2 = (f32[64,512]{1,0:T(8,128)S(1)}, f32[64,512]{1,0:T(8,128)S(1)}, u32[]{:S(2)}, u32[]{:S(2)}) collective-permute-start(f32[64,512]{1,0:T(8,128)S(1)} %get-tuple-element.31), channel_id=1, source_target_pairs={{0,16},{16,32},{32,48},{48,64},{64,80},{80,96},{96,112},{112,128},... | collective-permute-start | bytes 393224 | tf_op jit(solution)/shard_map/ppermute | solution.py:30
  71.4 1.9 %collective-permute-start.3 = (f32[64,512]{1,0:T(8,128)S(1)}, f32[64,512]{1,0:T(8,128)S(1)}, u32[]{:S(2)}, u32[]{:S(2)}) collective-permute-start(f32[64,512]{1,0:T(8,128)S(1)} %get-tuple-element.32), channel_id=1, source_target_pairs={{16,0},{32,16},{48,32},{64,48},{80,64},{96,80},{112,96},{128,112},... | collective-permute-start | bytes 393224 | tf_op jit(solution)/shard_map/ppermute | solution.py:30
  73.3 12.9 %collective-permute-done.2.below_ref = f32[64,512]{1,0:T(8,128)S(1)} collective-permute-done((f32[64,512]{1,0:T(8,128)S(1)}, f32[64,512]{1,0:T(8,128)S(1)}, u32[]{:S(2)}, u32[]{:S(2)}) %collective-permute-start.2) | collective-permute-done | bytes 131104 | tf_op jit(solution)/shard_map/ppermute | solution.py:30
  86.3 0.9 copy-done.9
  87.2 0.4 collective-permute-start.11
  87.6 1.4 %copy-done.1 = f32[128,3072]{1,0:T(8,128)S(1)} copy-done((f32[128,3072]{1,0:T(8,128)S(1)}, f32[128,3072]{1,0:T(8,128)}, u32[]{:S(2)}) %copy-start.1) | copy-done | bytes 1572888
  89.0 1.1 copy-done.3
  90.1 1.4 %copy-done.6 = f32[128,3072]{1,0:T(8,128)S(1)} copy-done((f32[128,3072]{1,0:T(8,128)S(1)}, f32[128,3072]{1,0:T(8,128)}, u32[]{:S(2)}) %copy-start.6) | copy-done | bytes 1572888
  91.5 1.1 copy-done.8
  92.7 1.1 copy-done.10
  93.8 1.1 copy-done.12
  94.9 4.1 %shard_map.71 = (f32[4,128,128]{2,1,0:T(8,128)S(1)}, f32[128,128]{1,0:T(8,128)S(1)}, f32[128,128]{1,0:T(8,128)S(1)}, f32[128,128]{1,0:T(8,128)S(1)}) custom-call(f32[64,3072]{1,0:T(8,128)S(1)} %copy-done.8, f32[64,3072]{1,0:T(8,128)S(1)} %copy-done.10, f32[64,3072]{1,0:T(8,128)S(1)} %copy-done.3, f32[64,3072]{1,0:T(8,128)S(1)} %copy-done.12, ...), custom_call_target="tpu_custom_call" | custom-call | flops 10000000 | bytes 30000 | tf_op jit(solution)/shard_map/pallas_call | solution.py:296
  99.0 1.1 collective-permute-start.8
  100.1 2.6 %collective-permute-start.10 = (f32[128,128]{1,0:T(8,128)S(1)}, f32[128,128]{1,0:T(8,128)S(1)}, u32[]{:S(2)}, u32[]{:S(2)}) collective-permute-start(f32[128,128]{1,0:T(8,128)S(1)} %get-tuple-element.48), channel_id=1, source_target_pairs={{0,10},{1,11},{2,12},{3,13},{4,14},{5,15},{6,0},{7,1},{8,2},{9,3},... | collective-permute-start | bytes 196616 | tf_op jit(solution)/shard_map/ppermute | solution.py:24
  102.8 0.1 pad_add_fusion.place
  102.8 5.5 %shard_map.72 = f32[64,6144]{1,0:T(8,128)} custom-call(s32[512]{0:T(512)S(1)} %copy-done.13, s32[512]{0:T(512)S(1)} %copy-done.14, f32[6144,128]{1,0:T(8,128)S(1)} %get-tuple-element.43.rows.rows_ref, f32[64,512]{1,0:T(8,128)S(1)} %collective-permute-done.2.below_ref, f32[64,512]{1,0:T(8,128)S(1)} %collective-permute-done.3.above_ref), custom_call_target="tpu_custom_call" | custom-call | flops 10000000 | bytes 30000 | tf_op jit(solution)/shard_map/pallas_call | solution.py:368
  108.3 0.8 collective-permute-done.10.refs_2_
  109.2 2.1 %collective-permute-done.11.far_ref = f32[128,3072]{1,0:T(8,128)} collective-permute-done((f32[128,3072]{1,0:T(8,128)}, f32[128,3072]{1,0:T(8,128)}, u32[]{:S(2)}, u32[]{:S(2)}) %collective-permute-start.11) | collective-permute-done | bytes 1572896 | tf_op jit(solution)/shard_map/ppermute | solution.py:24
  111.3 2.3 %shard_map.73 = f32[32,32,128]{2,1,0:T(8,128)S(1)} custom-call(s32[3]{0:T(128)S(1)} %pad_add_fusion.place, f32[64,3072]{1,0:T(8,128)S(1)} %copy-done.8, f32[64,3072]{1,0:T(8,128)S(1)} %copy-done.10, f32[128,3072]{1,0:T(8,128)} %collective-permute-done.11.far_ref, f32[4,128,128]{2,1,0:T(8,128)S(1)} %get-tuple-element.50.near_ref, ...), custom_call_target="tpu_custom_call" | custom-call | flops 2000000000 | bytes 6000000 | tf_op jit(solution)/shard_map/pallas_call | solution.py:310
  113.6 21.8 %all_to_all.5 = f32[32,32,128]{2,1,0:T(8,128)S(1)} all-to-all(f32[32,32,128]{2,1,0:T(8,128)S(1)} %shard_map.73), channel_id=1, replica_groups={{0,1,16,17,32,33,48,49,64,65,80,81,96,97,112,113,128,129,144,145,160,16..., dimensions={0} | all-to-all | bytes 1048576 | tf_op jit(solution)/shard_map/all_to_all | solution.py:382
  135.5 0.7 copy.7
  (43 shorter events, 0.4 us)
Async XLA Ops:
  0.7 11.5 %copy-start.16 = (s32[3,12288]{1,0:T(4,128)S(1)}, s32[3,12288]{1,0:T(4,128)}, u32[]{:S(2)}) copy-start(s32[3,12288]{1,0:T(4,128)} %param.6) | copy-start | bytes 442372
  0.7 11.7 %copy-start.4 = (f32[64,6144]{1,0:T(8,128)S(1)}, f32[64,6144]{1,0:T(8,128)}, u32[]{:S(2)}) copy-start(f32[64,6144]{1,0:T(8,128)} %refs_4_.3) | copy-start | bytes 4718596
  0.7 11.7 %copy-start.15 = (f32[12288]{0:T(1024)S(1)}, f32[12288]{0:T(1024)}, u32[]{:S(2)}) copy-start(f32[12288]{0:T(1024)} %refs_3_.3) | copy-start | bytes 147460
  2.3 32.8 %copy-start.2 = (f32[64,3072]{1,0:T(8,128)}, f32[64,3072]{1,0:T(8,128)S(1)}, u32[]{:S(2)}) copy-start(f32[64,3072]{1,0:T(8,128)S(1)} %get-tuple-element.57.refs_2_) | copy-start | bytes 2359300
  2.3 32.8 %collective-permute-start.1 = (f32[64,3072]{1,0:T(8,128)S(1)}, f32[64,3072]{1,0:T(8,128)S(1)}, u32[]{:S(2)}, u32[]{:S(2)}) collective-permute-start(f32[64,3072]{1,0:T(8,128)S(1)} %get-tuple-element.36), channel_id=1, source_target_pairs={{0,3},{1,2},{2,5},{3,4},{4,7},{5,6},{6,9},{7,8},{8,11},{9,10},{10,... | collective-permute-start | bytes 2359304 | tf_op jit(solution)/shard_map/ppermute | solution.py:24
  11.4 23.7 %collective-permute-start = (f32[64,3072]{1,0:T(8,128)S(1)}, f32[64,3072]{1,0:T(8,128)S(1)}, u32[]{:S(2)}, u32[]{:S(2)}) collective-permute-start(f32[64,3072]{1,0:T(8,128)S(1)} %get-tuple-element.57.refs_2_), channel_id=1, source_target_pairs={{0,2},{1,3},{2,4},{3,5},{4,6},{5,7},{6,8},{7,9},{8,10},{9,11},{10,... | collective-permute-start | bytes 2359304 | tf_op jit(solution)/shard_map/ppermute | solution.py:24
  35.1 26.1 %collective-permute-start.5 = (f32[64,3072]{1,0:T(8,128)S(1)}, f32[64,3072]{1,0:T(8,128)S(1)}, u32[]{:S(2)}, u32[]{:S(2)}) collective-permute-start(f32[64,3072]{1,0:T(8,128)S(1)} %get-tuple-element.36), channel_id=1, source_target_pairs={{0,1},{1,0},{2,3},{3,2},{4,5},{5,4},{6,7},{7,6},{8,9},{9,8},{10,11... | collective-permute-start | bytes 2359304 | tf_op jit(solution)/shard_map/ppermute | solution.py:34
  35.4 25.8 %copy-start = (f32[128,3072]{1,0:T(8,128)}, f32[128,3072]{1,0:T(8,128)S(1)}, u32[]{:S(2)}) copy-start(f32[128,3072]{1,0:T(8,128)S(1)} %constant_dynamic-update-slice_fusion.refs_4_) | copy-start | bytes 4718596
  35.4 25.9 %collective-permute-start.4 = (f32[128,3072]{1,0:T(8,128)S(1)}, f32[128,3072]{1,0:T(8,128)S(1)}, u32[]{:S(2)}, u32[]{:S(2)}) collective-permute-start(f32[128,3072]{1,0:T(8,128)S(1)} %constant_dynamic-update-slice_fusion.refs_4_), channel_id=1, source_target_pairs={{0,2},{1,3},{2,4},{3,5},{4,6},{5,7},{6,8},{7,9},{8,10},{9,11},{10,... | collective-permute-start | bytes 4718600 | tf_op jit(solution)/shard_map/ppermute | solution.py:24
  36.5 29.6 %copy-start.13 = (s32[512]{0:T(512)S(1)}, s32[512]{0:T(512)}, u32[]{:S(2)}) copy-start(s32[512]{0:T(512)} %low_s.3) | copy-start | bytes 6148
  36.5 29.6 %copy-start.14 = (s32[512]{0:T(512)S(1)}, s32[512]{0:T(512)}, u32[]{:S(2)}) copy-start(s32[512]{0:T(512)} %up_s.3) | copy-start | bytes 6148
  61.3 6.8 %copy-start.7 = (f32[64,3072]{1,0:T(8,128)}, f32[64,3072]{1,0:T(8,128)S(1)}, u32[]{:S(2)}) copy-start(f32[64,3072]{1,0:T(8,128)S(1)} %get-tuple-element.30.refs_0_.ya_ref) | copy-start | bytes 2359300
  61.3 6.8 %copy-start.11 = (f32[64,3072]{1,0:T(8,128)}, f32[64,3072]{1,0:T(8,128)S(1)}, u32[]{:S(2)}) copy-start(f32[64,3072]{1,0:T(8,128)S(1)} %collective-permute-done.5.refs_3_) | copy-start | bytes 2359300
  61.3 6.7 %copy-start.5 = (f32[128,3072]{1,0:T(8,128)}, f32[128,3072]{1,0:T(8,128)S(1)}, u32[]{:S(2)}) copy-start(f32[128,3072]{1,0:T(8,128)S(1)} %collective-permute-done.4.refs_5_) | copy-start | bytes 4718596
  61.3 25.9 %collective-permute-start.6 = (f32[128,3072]{1,0:T(8,128)S(1)}, f32[128,3072]{1,0:T(8,128)}, u32[]{:S(2)}, u32[]{:S(2)}) collective-permute-start(f32[128,3072]{1,0:T(8,128)S(1)} %collective-permute-done.4.refs_5_), channel_id=1, source_target_pairs={{0,2},{1,3},{2,4},{3,5},{4,6},{5,7},{6,8},{7,9},{8,10},{9,11},{10,... | collective-permute-start | bytes 4718600 | tf_op jit(solution)/shard_map/ppermute | solution.py:24
  63.1 23.1 %collective-permute-start.7 = (f32[64,3072]{1,0:T(8,128)S(1)}, f32[64,3072]{1,0:T(8,128)S(1)}, u32[]{:S(2)}, u32[]{:S(2)}) collective-permute-start(f32[64,3072]{1,0:T(8,128)S(1)} %get-tuple-element.38), channel_id=1, source_target_pairs={{0,1},{1,0},{2,3},{3,2},{4,5},{5,4},{6,7},{7,6},{8,9},{9,8},{10,11... | collective-permute-start | bytes 2359304 | tf_op jit(solution)/shard_map/ppermute | solution.py:34
  68.0 18.2 %collective-permute-start.2 = (f32[64,512]{1,0:T(8,128)S(1)}, f32[64,512]{1,0:T(8,128)S(1)}, u32[]{:S(2)}, u32[]{:S(2)}) collective-permute-start(f32[64,512]{1,0:T(8,128)S(1)} %get-tuple-element.31), channel_id=1, source_target_pairs={{0,16},{16,32},{32,48},{48,64},{64,80},{80,96},{96,112},{112,128},... | collective-permute-start | bytes 393224 | tf_op jit(solution)/shard_map/ppermute | solution.py:30
  71.4 14.8 %collective-permute-start.3 = (f32[64,512]{1,0:T(8,128)S(1)}, f32[64,512]{1,0:T(8,128)S(1)}, u32[]{:S(2)}, u32[]{:S(2)}) collective-permute-start(f32[64,512]{1,0:T(8,128)S(1)} %get-tuple-element.32), channel_id=1, source_target_pairs={{16,0},{32,16},{48,32},{64,48},{80,64},{96,80},{112,96},{128,112},... | collective-permute-start | bytes 393224 | tf_op jit(solution)/shard_map/ppermute | solution.py:30
  86.3 0.9 copy-start.9
  87.2 24.1 %collective-permute-start.11 = (f32[128,3072]{1,0:T(8,128)}, f32[128,3072]{1,0:T(8,128)}, u32[]{:S(2)}, u32[]{:S(2)}) collective-permute-start(f32[128,3072]{1,0:T(8,128)} %collective-permute-done.6.refs_6_), channel_id=1, source_target_pairs={{0,2},{1,3},{2,4},{3,5},{4,6},{5,7},{6,8},{7,9},{8,10},{9,11},{10,... | collective-permute-start | bytes 4718600 | tf_op jit(solution)/shard_map/ppermute | solution.py:24
  87.6 1.4 %copy-start.1 = (f32[128,3072]{1,0:T(8,128)S(1)}, f32[128,3072]{1,0:T(8,128)}, u32[]{:S(2)}) copy-start(f32[128,3072]{1,0:T(8,128)} %copy-done) | copy-start | bytes 4718596
  89.0 1.1 copy-start.3
  90.1 1.4 %copy-start.6 = (f32[128,3072]{1,0:T(8,128)S(1)}, f32[128,3072]{1,0:T(8,128)}, u32[]{:S(2)}) copy-start(f32[128,3072]{1,0:T(8,128)} %copy-done.5) | copy-start | bytes 4718596
  91.5 1.1 copy-start.8
  92.7 1.1 copy-start.10
  93.8 1.1 copy-start.12
  99.0 9.3 %collective-permute-start.8 = (f32[128,128]{1,0:T(8,128)S(1)}, f32[128,128]{1,0:T(8,128)S(1)}, u32[]{:S(2)}, u32[]{:S(2)}) collective-permute-start(f32[128,128]{1,0:T(8,128)S(1)} %get-tuple-element.46), channel_id=1, source_target_pairs={{0,14},{1,15},{2,0},{3,1},{4,2},{5,3},{6,4},{7,5},{8,6},{9,7},{10,... | collective-permute-start | bytes 196616 | tf_op jit(solution)/shard_map/ppermute | solution.py:24
  100.1 8.2 %collective-permute-start.9 = (f32[128,128]{1,0:T(8,128)S(1)}, f32[128,128]{1,0:T(8,128)S(1)}, u32[]{:S(2)}, u32[]{:S(2)}) collective-permute-start(f32[128,128]{1,0:T(8,128)S(1)} %get-tuple-element.47), channel_id=1, source_target_pairs={{0,12},{1,13},{2,14},{3,15},{4,0},{5,1},{6,2},{7,3},{8,4},{9,5},{1... | collective-permute-start | bytes 196616 | tf_op jit(solution)/shard_map/ppermute | solution.py:24
  100.1 9.0 %collective-permute-start.10 = (f32[128,128]{1,0:T(8,128)S(1)}, f32[128,128]{1,0:T(8,128)S(1)}, u32[]{:S(2)}, u32[]{:S(2)}) collective-permute-start(f32[128,128]{1,0:T(8,128)S(1)} %get-tuple-element.48), channel_id=1, source_target_pairs={{0,10},{1,11},{2,12},{3,13},{4,14},{5,15},{6,0},{7,1},{8,2},{9,3},... | collective-permute-start | bytes 196616 | tf_op jit(solution)/shard_map/ppermute | solution.py:24

commit v8 on v7

--- a/solution.py
+++ b/solution.py
@@ -90,7 +90,7 @@
                     z[pl.ds(n + 8 * (1 + k // 2), 1), at:at + snaps] = new[:, at:at + snaps]
         return carry
 
-    lax.fori_loop(0, count // (arrays * 2 * parts), elements, 0)
+    lax.fori_loop(0, count // (arrays * 2 * parts), elements, 0, unroll=8)
 
     if not first:
         earlier.wait()
@@ -197,7 +197,7 @@
     return pl.CostEstimate(flops=int(micros * 1e9), bytes_accessed=int(micros * 3e6), transcendentals=0)
 
 
-ARRAYS, PARTS = 4, 2
+ARRAYS, PARTS = 4, 1
 
 
 SHARES = (1, 1)
@@ -221,7 +221,7 @@
         + [pltpu.SMEM((count,), jnp.float32), pltpu.SemaphoreType.DMA((4,))]
         + [pltpu.VMEM((nodes, LANES), jnp.float32), pltpu.SemaphoreType.DMA, pltpu.SemaphoreType.DMA((4,))]
         + [pltpu.VMEM((nodes * (1 + PARTS), LANES), jnp.float32)] * ARRAYS,
-        compiler_params=pltpu.CompilerParams(vmem_limit_bytes=44 * MIB),
+        compiler_params=pltpu.CompilerParams(vmem_limit_bytes=33 * MIB),
         cost_estimate=cost(20),
     )(*operands)
 

time: 137 us -> 134 us (0.978)
  Pallas kernels: 61.3 us -> 55.8 us
  starting transfers between devices: 25.3 us -> 27.3 us
    pallas_call x2, Pallas kernels: 47.5 us -> 42 us  [apply_call(): pl.pallas_call(functools.partial(apply_kernel, first, last, start, count,...]
    ppermute x8, starting transfers between devices: 16.9 us -> 19 us  [ring_hop(): return lax.ppermute(value, ('mesh', 'snap'), pairs)]
  transfers between devices with their start and end apart: 12 -> 12, of which waited for: 3 -> 4; matrix products, arithmetic and copies ran while one was open for 0% -> 0% of each run, Pallas kernels for 43% -> 40%
where the time goes in v8:
time: 134 us
  Pallas kernels  55.8 us (42%)
  starting transfers between devices  27.3 us (20%)
  blocking collectives  21.8 us (16%)
  waiting for transfers between devices  16.7 us (12%)
  local copies, waits for them, and re-layouts  10.9 us (8%)
    pallas_call x2, Pallas kernels, apply_call(): pl.pallas_call(functools.partial(apply_kernel, first, last, start, count,...  42 us
    all_to_all x1, blocking collectives, on_device(): lax.all_to_all(tiles, ('mesh', 'snap'), 0, 0, axis_index_groups=planes, t...  21.8 us
    ppermute x8, starting transfers between devices, ring_hop(): return lax.ppermute(value, ('mesh', 'snap'), pairs)  19 us
    ppermute x2, waiting for transfers between devices, passed_along(): lax.ppermute(value, axis, [(source, source + steps) for source in range(l...  12.9 us
    unnamed x36, local copies, waits for them, and re-layouts  9.04 us
    pallas_call x1, Pallas kernels, on_device(): pl.pallas_call(assemble_kernel, out_shape=jax.ShapeDtypeStruct((snaps, no...  5.46 us
    ppermute x2, starting transfers between devices, passed_along(): lax.ppermute(value, axis, [(source, source + steps) for source in range(l...  5.26 us
    pallas_call x1, Pallas kernels, near_call(): pl.pallas_call(near_kernel, out_shape=[jax.ShapeDtypeStruct((4, 2 * snaps...  4.07 us
  transfers between devices with their start and end apart: 12, of which 4 were waited for; matrix products, arithmetic and copies ran while one was open for 0% of the time, Pallas kernels for 40%

profile of v8, /device:TPU:1, one launch (start us, length us, event | category | flops | bytes accessed | tf_op | source)
XLA Modules:
  0.0 133.6 jit_solution(4455957907076531291)
XLA Ops:
  0.7 1.6 %constant_dynamic-slice_fusion = (f32[64,3072]{1,0:T(8,128)S(1)}, f32[64,3072]{1,0:T(8,128)S(1)}) fusion(f32[64,6144]{1,0:T(8,128)} %refs_4_.3, s32[]{:T(128)S(6)} %select_n.27, s32[]{:T(128)S(6)} %select_n.26), kind=kLoop, calls=%fused_computation.6 | loop fusion | bytes 3145736 | tf_op jit(solution)/shard_map/dynamic_slice | solution.py:332
  2.3 9.1 %collective-permute-start.1 = (f32[64,3072]{1,0:T(8,128)S(1)}, f32[64,3072]{1,0:T(8,128)S(1)}, u32[]{:S(2)}, u32[]{:S(2)}) collective-permute-start(f32[64,3072]{1,0:T(8,128)S(1)} %get-tuple-element.36), channel_id=1, source_target_pairs={{0,3},{1,2},{2,5},{3,4},{4,7},{5,6},{6,9},{7,8},{8,11},{9,10},{10,... | collective-permute-start | bytes 2359304 | tf_op jit(solution)/shard_map/ppermute | solution.py:24
  11.4 0.7 collective-permute-start
  12.2 0.1 fusion.1
  12.3 19.9 %shard_map.68.refs_5_ = f32[6144,128]{1,0:T(8,128)S(1)} custom-call(s32[12288]{0:T(1024)S(1)} %bitcast.12, s32[12288]{0:T(1024)S(1)} %bitcast.10, s32[12288]{0:T(1024)S(1)} %bitcast.8, f32[12288]{0:T(1024)S(1)} %copy-done.15, f32[64,6144]{1,0:T(8,128)S(1)} %copy-done.4), custom_call_target="tpu_custom_call" | custom-call | flops 20000000000 | bytes 60000000 | tf_op jit(solution)/shard_map/pallas_call | solution.py:215
  32.3 0.8 collective-permute-done
  33.3 3.2 %collective-permute-start.4 = (f32[128,3072]{1,0:T(8,128)S(1)}, f32[128,3072]{1,0:T(8,128)S(1)}, u32[]{:S(2)}, u32[]{:S(2)}) collective-permute-start(f32[128,3072]{1,0:T(8,128)S(1)} %constant_dynamic-update-slice_fusion.refs_4_), channel_id=1, source_target_pairs={{0,2},{1,3},{2,4},{3,5},{4,6},{5,7},{6,8},{7,9},{8,10},{9,11},{10,... | collective-permute-start | bytes 4718600 | tf_op jit(solution)/shard_map/ppermute | solution.py:24
  36.5 22.1 %shard_map.69 = (f32[6144,128]{1,0:T(8,128)S(1)}, f32[64,3072]{1,0:T(8,128)S(1)}, f32[64,3072]{1,0:T(8,128)S(1)}) custom-call(s32[12288]{0:T(1024)S(1)} %bitcast.13, s32[12288]{0:T(1024)S(1)} %bitcast.11, s32[12288]{0:T(1024)S(1)} %bitcast.9, f32[12288]{0:T(1024)S(1)} %copy-done.15, f32[64,6144]{1,0:T(8,128)S(1)} %copy-done.4, ...), custom_call_target="tpu_custom_call" | custom-call | flops 20000000000 | bytes 60000000 | tf_op jit(solution)/shard_map/pallas_call | solution.py:215
  58.7 1.8 %collective-permute-start.6 = (f32[128,3072]{1,0:T(8,128)S(1)}, f32[128,3072]{1,0:T(8,128)}, u32[]{:S(2)}, u32[]{:S(2)}) collective-permute-start(f32[128,3072]{1,0:T(8,128)S(1)} %collective-permute-done.4.refs_5_), channel_id=1, source_target_pairs={{0,2},{1,3},{2,4},{3,5},{4,6},{5,7},{6,8},{7,9},{8,10},{9,11},{10,... | collective-permute-start | bytes 4718600 | tf_op jit(solution)/shard_map/ppermute | solution.py:24
  60.5 2.9 %collective-permute-start.7 = (f32[64,3072]{1,0:T(8,128)S(1)}, f32[64,3072]{1,0:T(8,128)S(1)}, u32[]{:S(2)}, u32[]{:S(2)}) collective-permute-start(f32[64,3072]{1,0:T(8,128)S(1)} %get-tuple-element.38), channel_id=1, source_target_pairs={{0,1},{1,0},{2,3},{3,2},{4,5},{5,4},{6,7},{7,6},{8,9},{9,8},{10,11... | collective-permute-start | bytes 2359304 | tf_op jit(solution)/shard_map/ppermute | solution.py:34
  63.5 2.0 %shard_map.70 = (f32[64,512]{1,0:T(8,128)S(1)}, f32[64,512]{1,0:T(8,128)S(1)}) custom-call(s32[512]{0:T(512)S(1)} %copy-done.13, s32[512]{0:T(512)S(1)} %copy-done.14, f32[6144,128]{1,0:T(8,128)S(1)} %get-tuple-element.43.rows.rows_ref), custom_call_target="tpu_custom_call" | custom-call | flops 10000000 | bytes 30000 | tf_op jit(solution)/shard_map/pallas_call | solution.py:352
  65.4 3.3 %collective-permute-start.2 = (f32[64,512]{1,0:T(8,128)S(1)}, f32[64,512]{1,0:T(8,128)S(1)}, u32[]{:S(2)}, u32[]{:S(2)}) collective-permute-start(f32[64,512]{1,0:T(8,128)S(1)} %get-tuple-element.31), channel_id=1, source_target_pairs={{0,16},{16,32},{32,48},{48,64},{64,80},{80,96},{96,112},{112,128},... | collective-permute-start | bytes 393224 | tf_op jit(solution)/shard_map/ppermute | solution.py:30
  68.8 1.9 %collective-permute-start.3 = (f32[64,512]{1,0:T(8,128)S(1)}, f32[64,512]{1,0:T(8,128)S(1)}, u32[]{:S(2)}, u32[]{:S(2)}) collective-permute-start(f32[64,512]{1,0:T(8,128)S(1)} %get-tuple-element.32), channel_id=1, source_target_pairs={{16,0},{32,16},{48,32},{64,48},{80,64},{96,80},{112,96},{128,112},... | collective-permute-start | bytes 393224 | tf_op jit(solution)/shard_map/ppermute | solution.py:30
  70.7 12.9 %collective-permute-done.2.below_ref = f32[64,512]{1,0:T(8,128)S(1)} collective-permute-done((f32[64,512]{1,0:T(8,128)S(1)}, f32[64,512]{1,0:T(8,128)S(1)}, u32[]{:S(2)}, u32[]{:S(2)}) %collective-permute-start.2) | collective-permute-done | bytes 131104 | tf_op jit(solution)/shard_map/ppermute | solution.py:30
  83.7 0.9 copy-done.9
  84.6 0.4 collective-permute-start.11
  85.0 1.4 %copy-done.1 = f32[128,3072]{1,0:T(8,128)S(1)} copy-done((f32[128,3072]{1,0:T(8,128)S(1)}, f32[128,3072]{1,0:T(8,128)}, u32[]{:S(2)}) %copy-start.1) | copy-done | bytes 1572888
  86.4 1.1 copy-done.3
  87.5 1.4 %copy-done.6 = f32[128,3072]{1,0:T(8,128)S(1)} copy-done((f32[128,3072]{1,0:T(8,128)S(1)}, f32[128,3072]{1,0:T(8,128)}, u32[]{:S(2)}) %copy-start.6) | copy-done | bytes 1572888
  88.9 1.1 copy-done.8
  90.1 1.1 copy-done.10
  91.2 1.1 copy-done.12
  92.3 4.1 %shard_map.71 = (f32[4,128,128]{2,1,0:T(8,128)S(1)}, f32[128,128]{1,0:T(8,128)S(1)}, f32[128,128]{1,0:T(8,128)S(1)}, f32[128,128]{1,0:T(8,128)S(1)}) custom-call(f32[64,3072]{1,0:T(8,128)S(1)} %copy-done.8, f32[64,3072]{1,0:T(8,128)S(1)} %copy-done.10, f32[64,3072]{1,0:T(8,128)S(1)} %copy-done.3, f32[64,3072]{1,0:T(8,128)S(1)} %copy-done.12, ...), custom_call_target="tpu_custom_call" | custom-call | flops 10000000 | bytes 30000 | tf_op jit(solution)/shard_map/pallas_call | solution.py:296
  96.4 1.1 collective-permute-start.8
  97.5 2.6 %collective-permute-start.10 = (f32[128,128]{1,0:T(8,128)S(1)}, f32[128,128]{1,0:T(8,128)S(1)}, u32[]{:S(2)}, u32[]{:S(2)}) collective-permute-start(f32[128,128]{1,0:T(8,128)S(1)} %get-tuple-element.48), channel_id=1, source_target_pairs={{0,10},{1,11},{2,12},{3,13},{4,14},{5,15},{6,0},{7,1},{8,2},{9,3},... | collective-permute-start | bytes 196616 | tf_op jit(solution)/shard_map/ppermute | solution.py:24
  100.2 0.1 pad_add_fusion.place
  100.2 5.5 %shard_map.72 = f32[64,6144]{1,0:T(8,128)} custom-call(s32[512]{0:T(512)S(1)} %copy-done.13, s32[512]{0:T(512)S(1)} %copy-done.14, f32[6144,128]{1,0:T(8,128)S(1)} %get-tuple-element.43.rows.rows_ref, f32[64,512]{1,0:T(8,128)S(1)} %collective-permute-done.2.below_ref, f32[64,512]{1,0:T(8,128)S(1)} %collective-permute-done.3.above_ref), custom_call_target="tpu_custom_call" | custom-call | flops 10000000 | bytes 30000 | tf_op jit(solution)/shard_map/pallas_call | solution.py:368
  105.7 0.8 collective-permute-done.10.refs_2_
  106.6 2.1 %collective-permute-done.11.far_ref = f32[128,3072]{1,0:T(8,128)} collective-permute-done((f32[128,3072]{1,0:T(8,128)}, f32[128,3072]{1,0:T(8,128)}, u32[]{:S(2)}, u32[]{:S(2)}) %collective-permute-start.11) | collective-permute-done | bytes 1572896 | tf_op jit(solution)/shard_map/ppermute | solution.py:24
  108.6 2.3 %shard_map.73 = f32[32,32,128]{2,1,0:T(8,128)S(1)} custom-call(s32[3]{0:T(128)S(1)} %pad_add_fusion.place, f32[64,3072]{1,0:T(8,128)S(1)} %copy-done.8, f32[64,3072]{1,0:T(8,128)S(1)} %copy-done.10, f32[128,3072]{1,0:T(8,128)} %collective-permute-done.11.far_ref, f32[4,128,128]{2,1,0:T(8,128)S(1)} %get-tuple-element.50.near_ref, ...), custom_call_target="tpu_custom_call" | custom-call | flops 2000000000 | bytes 6000000 | tf_op jit(solution)/shard_map/pallas_call | solution.py:310
  111.0 21.8 %all_to_all.5 = f32[32,32,128]{2,1,0:T(8,128)S(1)} all-to-all(f32[32,32,128]{2,1,0:T(8,128)S(1)} %shard_map.73), channel_id=1, replica_groups={{0,1,16,17,32,33,48,49,64,65,80,81,96,97,112,113,128,129,144,145,160,16..., dimensions={0} | all-to-all | bytes 1048576 | tf_op jit(solution)/shard_map/all_to_all | solution.py:382
  132.9 0.7 copy.7
  (43 shorter events, 0.4 us)
Async XLA Ops:
  0.7 11.5 %copy-start.16 = (s32[3,12288]{1,0:T(4,128)S(1)}, s32[3,12288]{1,0:T(4,128)}, u32[]{:S(2)}) copy-start(s32[3,12288]{1,0:T(4,128)} %param.6) | copy-start | bytes 442372
  0.7 11.7 %copy-start.4 = (f32[64,6144]{1,0:T(8,128)S(1)}, f32[64,6144]{1,0:T(8,128)}, u32[]{:S(2)}) copy-start(f32[64,6144]{1,0:T(8,128)} %refs_4_.3) | copy-start | bytes 4718596
  0.7 11.7 %copy-start.15 = (f32[12288]{0:T(1024)S(1)}, f32[12288]{0:T(1024)}, u32[]{:S(2)}) copy-start(f32[12288]{0:T(1024)} %refs_3_.3) | copy-start | bytes 147460
  2.3 30.0 %copy-start.2 = (f32[64,3072]{1,0:T(8,128)}, f32[64,3072]{1,0:T(8,128)S(1)}, u32[]{:S(2)}) copy-start(f32[64,3072]{1,0:T(8,128)S(1)} %get-tuple-element.57.refs_2_) | copy-start | bytes 2359300
  2.3 30.0 %collective-permute-start.1 = (f32[64,3072]{1,0:T(8,128)S(1)}, f32[64,3072]{1,0:T(8,128)S(1)}, u32[]{:S(2)}, u32[]{:S(2)}) collective-permute-start(f32[64,3072]{1,0:T(8,128)S(1)} %get-tuple-element.36), channel_id=1, source_target_pairs={{0,3},{1,2},{2,5},{3,4},{4,7},{5,6},{6,9},{7,8},{8,11},{9,10},{10,... | collective-permute-start | bytes 2359304 | tf_op jit(solution)/shard_map/ppermute | solution.py:24
  11.4 21.7 %collective-permute-start = (f32[64,3072]{1,0:T(8,128)S(1)}, f32[64,3072]{1,0:T(8,128)S(1)}, u32[]{:S(2)}, u32[]{:S(2)}) collective-permute-start(f32[64,3072]{1,0:T(8,128)S(1)} %get-tuple-element.57.refs_2_), channel_id=1, source_target_pairs={{0,2},{1,3},{2,4},{3,5},{4,6},{5,7},{6,8},{7,9},{8,10},{9,11},{10,... | collective-permute-start | bytes 2359304 | tf_op jit(solution)/shard_map/ppermute | solution.py:24
  33.1 25.6 %collective-permute-start.5 = (f32[64,3072]{1,0:T(8,128)S(1)}, f32[64,3072]{1,0:T(8,128)S(1)}, u32[]{:S(2)}, u32[]{:S(2)}) collective-permute-start(f32[64,3072]{1,0:T(8,128)S(1)} %get-tuple-element.36), channel_id=1, source_target_pairs={{0,1},{1,0},{2,3},{3,2},{4,5},{5,4},{6,7},{7,6},{8,9},{9,8},{10,11... | collective-permute-start | bytes 2359304 | tf_op jit(solution)/shard_map/ppermute | solution.py:34
  33.3 25.4 %copy-start = (f32[128,3072]{1,0:T(8,128)}, f32[128,3072]{1,0:T(8,128)S(1)}, u32[]{:S(2)}) copy-start(f32[128,3072]{1,0:T(8,128)S(1)} %constant_dynamic-update-slice_fusion.refs_4_) | copy-start | bytes 4718596
  33.3 25.4 %collective-permute-start.4 = (f32[128,3072]{1,0:T(8,128)S(1)}, f32[128,3072]{1,0:T(8,128)S(1)}, u32[]{:S(2)}, u32[]{:S(2)}) collective-permute-start(f32[128,3072]{1,0:T(8,128)S(1)} %constant_dynamic-update-slice_fusion.refs_4_), channel_id=1, source_target_pairs={{0,2},{1,3},{2,4},{3,5},{4,6},{5,7},{6,8},{7,9},{8,10},{9,11},{10,... | collective-permute-start | bytes 4718600 | tf_op jit(solution)/shard_map/ppermute | solution.py:24
  36.5 27.0 %copy-start.13 = (s32[512]{0:T(512)S(1)}, s32[512]{0:T(512)}, u32[]{:S(2)}) copy-start(s32[512]{0:T(512)} %low_s.3) | copy-start | bytes 6148
  36.5 27.0 %copy-start.14 = (s32[512]{0:T(512)S(1)}, s32[512]{0:T(512)}, u32[]{:S(2)}) copy-start(s32[512]{0:T(512)} %up_s.3) | copy-start | bytes 6148
  58.6 6.8 %copy-start.7 = (f32[64,3072]{1,0:T(8,128)}, f32[64,3072]{1,0:T(8,128)S(1)}, u32[]{:S(2)}) copy-start(f32[64,3072]{1,0:T(8,128)S(1)} %get-tuple-element.30.refs_0_.ya_ref) | copy-start | bytes 2359300
  58.7 6.8 %copy-start.11 = (f32[64,3072]{1,0:T(8,128)}, f32[64,3072]{1,0:T(8,128)S(1)}, u32[]{:S(2)}) copy-start(f32[64,3072]{1,0:T(8,128)S(1)} %collective-permute-done.5.refs_3_) | copy-start | bytes 2359300
  58.7 6.7 %copy-start.5 = (f32[128,3072]{1,0:T(8,128)}, f32[128,3072]{1,0:T(8,128)S(1)}, u32[]{:S(2)}) copy-start(f32[128,3072]{1,0:T(8,128)S(1)} %collective-permute-done.4.refs_5_) | copy-start | bytes 4718596
  58.7 25.9 %collective-permute-start.6 = (f32[128,3072]{1,0:T(8,128)S(1)}, f32[128,3072]{1,0:T(8,128)}, u32[]{:S(2)}, u32[]{:S(2)}) collective-permute-start(f32[128,3072]{1,0:T(8,128)S(1)} %collective-permute-done.4.refs_5_), channel_id=1, source_target_pairs={{0,2},{1,3},{2,4},{3,5},{4,6},{5,7},{6,8},{7,9},{8,10},{9,11},{10,... | collective-permute-start | bytes 4718600 | tf_op jit(solution)/shard_map/ppermute | solution.py:24
  60.5 23.1 %collective-permute-start.7 = (f32[64,3072]{1,0:T(8,128)S(1)}, f32[64,3072]{1,0:T(8,128)S(1)}, u32[]{:S(2)}, u32[]{:S(2)}) collective-permute-start(f32[64,3072]{1,0:T(8,128)S(1)} %get-tuple-element.38), channel_id=1, source_target_pairs={{0,1},{1,0},{2,3},{3,2},{4,5},{5,4},{6,7},{7,6},{8,9},{9,8},{10,11... | collective-permute-start | bytes 2359304 | tf_op jit(solution)/shard_map/ppermute | solution.py:34
  65.4 18.2 %collective-permute-start.2 = (f32[64,512]{1,0:T(8,128)S(1)}, f32[64,512]{1,0:T(8,128)S(1)}, u32[]{:S(2)}, u32[]{:S(2)}) collective-permute-start(f32[64,512]{1,0:T(8,128)S(1)} %get-tuple-element.31), channel_id=1, source_target_pairs={{0,16},{16,32},{32,48},{48,64},{64,80},{80,96},{96,112},{112,128},... | collective-permute-start | bytes 393224 | tf_op jit(solution)/shard_map/ppermute | solution.py:30
  68.8 14.8 %collective-permute-start.3 = (f32[64,512]{1,0:T(8,128)S(1)}, f32[64,512]{1,0:T(8,128)S(1)}, u32[]{:S(2)}, u32[]{:S(2)}) collective-permute-start(f32[64,512]{1,0:T(8,128)S(1)} %get-tuple-element.32), channel_id=1, source_target_pairs={{16,0},{32,16},{48,32},{64,48},{80,64},{96,80},{112,96},{128,112},... | collective-permute-start | bytes 393224 | tf_op jit(solution)/shard_map/ppermute | solution.py:30
  83.6 0.9 copy-start.9
  84.6 24.1 %collective-permute-start.11 = (f32[128,3072]{1,0:T(8,128)}, f32[128,3072]{1,0:T(8,128)}, u32[]{:S(2)}, u32[]{:S(2)}) collective-permute-start(f32[128,3072]{1,0:T(8,128)} %collective-permute-done.6.refs_6_), channel_id=1, source_target_pairs={{0,2},{1,3},{2,4},{3,5},{4,6},{5,7},{6,8},{7,9},{8,10},{9,11},{10,... | collective-permute-start | bytes 4718600 | tf_op jit(solution)/shard_map/ppermute | solution.py:24
  85.0 1.4 %copy-start.1 = (f32[128,3072]{1,0:T(8,128)S(1)}, f32[128,3072]{1,0:T(8,128)}, u32[]{:S(2)}) copy-start(f32[128,3072]{1,0:T(8,128)} %copy-done) | copy-start | bytes 4718596
  86.4 1.1 copy-start.3
  87.5 1.4 %copy-start.6 = (f32[128,3072]{1,0:T(8,128)S(1)}, f32[128,3072]{1,0:T(8,128)}, u32[]{:S(2)}) copy-start(f32[128,3072]{1,0:T(8,128)} %copy-done.5) | copy-start | bytes 4718596
  88.9 1.1 copy-start.8
  90.1 1.1 copy-start.10
  91.2 1.1 copy-start.12
  96.4 9.3 %collective-permute-start.8 = (f32[128,128]{1,0:T(8,128)S(1)}, f32[128,128]{1,0:T(8,128)S(1)}, u32[]{:S(2)}, u32[]{:S(2)}) collective-permute-start(f32[128,128]{1,0:T(8,128)S(1)} %get-tuple-element.46), channel_id=1, source_target_pairs={{0,14},{1,15},{2,0},{3,1},{4,2},{5,3},{6,4},{7,5},{8,6},{9,7},{10,... | collective-permute-start | bytes 196616 | tf_op jit(solution)/shard_map/ppermute | solution.py:24
  97.5 8.2 %collective-permute-start.9 = (f32[128,128]{1,0:T(8,128)S(1)}, f32[128,128]{1,0:T(8,128)S(1)}, u32[]{:S(2)}, u32[]{:S(2)}) collective-permute-start(f32[128,128]{1,0:T(8,128)S(1)} %get-tuple-element.47), channel_id=1, source_target_pairs={{0,12},{1,13},{2,14},{3,15},{4,0},{5,1},{6,2},{7,3},{8,4},{9,5},{1... | collective-permute-start | bytes 196616 | tf_op jit(solution)/shard_map/ppermute | solution.py:24
  97.5 9.0 %collective-permute-start.10 = (f32[128,128]{1,0:T(8,128)S(1)}, f32[128,128]{1,0:T(8,128)S(1)}, u32[]{:S(2)}, u32[]{:S(2)}) collective-permute-start(f32[128,128]{1,0:T(8,128)S(1)} %get-tuple-element.48), channel_id=1, source_target_pairs={{0,10},{1,11},{2,12},{3,13},{4,14},{5,15},{6,0},{7,1},{8,2},{9,3},... | collective-permute-start | bytes 196616 | tf_op jit(solution)/shard_map/ppermute | solution.py:24

commit v9 on v8

--- a/solution.py
+++ b/solution.py
@@ -200,7 +200,7 @@
 ARRAYS, PARTS = 4, 1
 
 
-SHARES = (1, 1)
+SHARES = (7, 5)
 
 
 def apply_call(index, columns, snapshots, rows, half):
@@ -267,8 +267,13 @@
             back[distance - 1][...] = value.T
 
 
-def far_kernel(place, ya_ref, yb_ref, far_ref, near_ref, *refs):
-    *back, out_ref = refs
+def far_kernel(place, ya_hbm, yb_hbm, far_hbm, near_ref, *refs):
+    back, out_ref, held, sems = refs[:3], refs[3], refs[4:7], refs[7]
+    copies = [pltpu.make_async_copy(source, target, sems.at[i])
+              for i, (source, target) in enumerate(zip((ya_hbm, yb_hbm, far_hbm), held))]
+    for copy in copies:
+        copy.start()
+    ya_ref, yb_ref, far_ref = held
     snaps = ya_ref.shape[0]
     rings = out_ref.shape[0] // 4
     low = snaps // 2
@@ -286,6 +291,8 @@
     for distance, received in enumerate(back, 1):
         put(distance, near_ref[distance])
         put(-distance, received[...])
+    for copy in copies:
+        copy.wait()
     (value,) = product(lambda _, at: far_ref[:, at], ya_ref, yb_ref, 1)
     put(rings // 2, value)
 
@@ -300,7 +307,7 @@
         out_specs=[IN_VMEM] * 4,
         scratch_shapes=[pltpu.VMEM(operand.shape, operand.dtype) for operand in operands]
         + [pltpu.SemaphoreType.DMA((len(operands),))],
-        compiler_params=pltpu.CompilerParams(vmem_limit_bytes=20 * MIB),
+        compiler_params=pltpu.CompilerParams(vmem_limit_bytes=60 * MIB),
         cost_estimate=cost(0.01),
     )(*operands)
 
@@ -310,9 +317,11 @@
     return pl.pallas_call(
         far_kernel,
         out_shape=jax.ShapeDtypeStruct((4 * rings, snaps // 2, 2 * snaps), jnp.float32),
-        in_specs=[IN_SMEM] + [IN_VMEM] * (4 + len(back)),
+        in_specs=[IN_SMEM] + [ANYWHERE] * 3 + [IN_VMEM] * (1 + len(back)),
         out_specs=IN_VMEM,
-        compiler_params=pltpu.CompilerParams(vmem_limit_bytes=16 * MIB),
+        scratch_shapes=[pltpu.VMEM(operand.shape, operand.dtype) for operand in (ya, yb, far)]
+        + [pltpu.SemaphoreType.DMA((3,))],
+        compiler_params=pltpu.CompilerParams(vmem_limit_bytes=60 * MIB),
         cost_estimate=cost(2),
     )(place, ya, yb, far, near, *back)
 

time: 134 us -> 134 us (level)
  local copies, waits for them, and re-layouts: 10.9 us -> 3.56 us
  Pallas kernels: 55.8 us -> 60.3 us
  waiting for transfers between devices: 16.7 us -> 18.7 us
    unnamed x36 -> x30, local copies, waits for them, and re-layouts: 9.04 us -> 1.7 us
    ppermute x8, waiting for transfers between devices: 3.76 us -> 7.38 us  [ring_hop(): return lax.ppermute(value, ('mesh', 'snap'), pairs)]
    pallas_call x1, Pallas kernels: 2.32 us -> 4.73 us  [far_call(): pl.pallas_call(far_kernel, out_shape=jax.ShapeDtypeStruct((4 * rings, sna...]
    pallas_call x1, Pallas kernels: 4.07 us -> 6.16 us  [near_call(): pl.pallas_call(near_kernel, out_shape=[jax.ShapeDtypeStruct((4, 2 * snaps...]
    ppermute x8, starting transfers between devices: 19 us -> 17.3 us  [ring_hop(): return lax.ppermute(value, ('mesh', 'snap'), pairs)]
    ppermute x2, waiting for transfers between devices: 12.9 us -> 11.4 us  [passed_along(): lax.ppermute(value, axis, [(source, source + steps) for source in range(l...]
    ppermute x2, starting transfers between devices: 5.26 us -> 6.64 us  [passed_along(): lax.ppermute(value, axis, [(source, source + steps) for source in range(l...]
  transfers between devices with their start and end apart: 12 -> 12, of which waited for: 4 -> 4; matrix products, arithmetic and copies ran while one was open for 0% -> 1% of each run, Pallas kernels for 40% -> 42%
where the time goes in v9:
time: 134 us
  Pallas kernels  60.3 us (45%)
  starting transfers between devices  27 us (20%)
  blocking collectives  22.2 us (17%)
  waiting for transfers between devices  18.7 us (14%)
  local copies, waits for them, and re-layouts  3.56 us (3%)
    pallas_call x2, Pallas kernels, apply_call(): pl.pallas_call(functools.partial(apply_kernel, first, last, start, count,...  42 us
    all_to_all x1, blocking collectives, on_device(): lax.all_to_all(tiles, ('mesh', 'snap'), 0, 0, axis_index_groups=planes, t...  22.2 us
    ppermute x8, starting transfers between devices, ring_hop(): return lax.ppermute(value, ('mesh', 'snap'), pairs)  17.3 us
    ppermute x2, waiting for transfers between devices, passed_along(): lax.ppermute(value, axis, [(source, source + steps) for source in range(l...  11.4 us
    ppermute x8, waiting for transfers between devices, ring_hop(): return lax.ppermute(value, ('mesh', 'snap'), pairs)  7.38 us
    ppermute x2, starting transfers between devices, passed_along(): lax.ppermute(value, axis, [(source, source + steps) for source in range(l...  6.64 us
    pallas_call x1, Pallas kernels, near_call(): pl.pallas_call(near_kernel, out_shape=[jax.ShapeDtypeStruct((4, 2 * snaps...  6.16 us
    pallas_call x1, Pallas kernels, on_device(): pl.pallas_call(assemble_kernel, out_shape=jax.ShapeDtypeStruct((snaps, no...  5.46 us
  transfers between devices with their start and end apart: 12, of which 4 were waited for; matrix products, arithmetic and copies ran while one was open for 1% of the time, Pallas kernels for 42%

profile of v9, /device:TPU:1, one launch (start us, length us, event | category | flops | bytes accessed | tf_op | source)
XLA Modules:
  0.0 133.6 jit_solution(6238139294489440172)
XLA Ops:
  0.7 1.6 %constant_dynamic-slice_fusion = (f32[64,3072]{1,0:T(8,128)S(1)}, f32[64,3072]{1,0:T(8,128)S(1)}) fusion(f32[64,6144]{1,0:T(8,128)} %refs_4_.3, s32[]{:T(128)S(6)} %select_n.27, s32[]{:T(128)S(6)} %select_n.26), kind=kLoop, calls=%fused_computation.6 | loop fusion | bytes 3145736 | tf_op jit(solution)/shard_map/dynamic_slice | solution.py:341
  2.3 9.1 %collective-permute-start.1 = (f32[64,3072]{1,0:T(8,128)S(1)}, f32[64,3072]{1,0:T(8,128)S(1)}, u32[]{:S(2)}, u32[]{:S(2)}) collective-permute-start(f32[64,3072]{1,0:T(8,128)S(1)} %get-tuple-element.36), channel_id=1, source_target_pairs={{0,3},{1,2},{2,5},{3,4},{4,7},{5,6},{6,9},{7,8},{8,11},{9,10},{10,... | collective-permute-start | bytes 2359304 | tf_op jit(solution)/shard_map/ppermute | solution.py:24
  11.4 0.7 collective-permute-start
  12.2 0.1 and_add_fusion
  12.2 0.1 fusion.1
  12.4 22.6 %shard_map.68.refs_5_ = f32[6144,128]{1,0:T(8,128)S(1)} custom-call(s32[12288]{0:T(1024)S(1)} %bitcast.12, s32[12288]{0:T(1024)S(1)} %bitcast.10, s32[12288]{0:T(1024)S(1)} %bitcast.8, f32[12288]{0:T(1024)S(1)} %copy-done.4, f32[64,6144]{1,0:T(8,128)S(1)} %copy-done), custom_call_target="tpu_custom_call" | custom-call | flops 20000000000 | bytes 60000000 | tf_op jit(solution)/shard_map/pallas_call | solution.py:215
  35.0 0.1 collective-permute-start.5
  35.1 0.1 constant_dynamic-update-slice_fusion.1
  35.2 0.1 constant_dynamic-update-slice_fusion.refs_4_
  35.2 0.0 copy-start.5
  35.3 1.3 collective-permute-start.4
  36.5 19.5 %shard_map.69 = (f32[6144,128]{1,0:T(8,128)S(1)}, f32[64,3072]{1,0:T(8,128)S(1)}, f32[64,3072]{1,0:T(8,128)S(1)}) custom-call(s32[12288]{0:T(1024)S(1)} %bitcast.13, s32[12288]{0:T(1024)S(1)} %bitcast.11, s32[12288]{0:T(1024)S(1)} %bitcast.9, f32[12288]{0:T(1024)S(1)} %copy-done.4, f32[64,6144]{1,0:T(8,128)S(1)} %copy-done, ...), custom_call_target="tpu_custom_call" | custom-call | flops 20000000000 | bytes 60000000 | tf_op jit(solution)/shard_map/pallas_call | solution.py:215
  56.0 1.8 %collective-permute-start.6 = (f32[128,3072]{1,0:T(8,128)S(1)}, f32[128,3072]{1,0:T(8,128)}, u32[]{:S(2)}, u32[]{:S(2)}) collective-permute-start(f32[128,3072]{1,0:T(8,128)S(1)} %collective-permute-done.4.refs_5_), channel_id=1, source_target_pairs={{0,2},{1,3},{2,4},{3,5},{4,6},{5,7},{6,8},{7,9},{8,10},{9,11},{10,... | collective-permute-start | bytes 4718600 | tf_op jit(solution)/shard_map/ppermute | solution.py:24
  57.9 2.9 %collective-permute-start.7 = (f32[64,3072]{1,0:T(8,128)S(1)}, f32[64,3072]{1,0:T(8,128)S(1)}, u32[]{:S(2)}, u32[]{:S(2)}) collective-permute-start(f32[64,3072]{1,0:T(8,128)S(1)} %get-tuple-element.38), channel_id=1, source_target_pairs={{0,1},{1,0},{2,3},{3,2},{4,5},{5,4},{6,7},{7,6},{8,9},{9,8},{10,11... | collective-permute-start | bytes 2359304 | tf_op jit(solution)/shard_map/ppermute | solution.py:34
  60.8 2.0 %shard_map.70 = (f32[64,512]{1,0:T(8,128)S(1)}, f32[64,512]{1,0:T(8,128)S(1)}) custom-call(s32[512]{0:T(512)S(1)} %copy-done.2, s32[512]{0:T(512)S(1)} %copy-done.3, f32[6144,128]{1,0:T(8,128)S(1)} %get-tuple-element.43.rows.rows_ref), custom_call_target="tpu_custom_call" | custom-call | flops 10000000 | bytes 30000 | tf_op jit(solution)/shard_map/pallas_call | solution.py:361
  62.8 4.7 %collective-permute-start.2 = (f32[64,512]{1,0:T(8,128)S(1)}, f32[64,512]{1,0:T(8,128)S(1)}, u32[]{:S(2)}, u32[]{:S(2)}) collective-permute-start(f32[64,512]{1,0:T(8,128)S(1)} %get-tuple-element.31), channel_id=1, source_target_pairs={{0,16},{16,32},{32,48},{48,64},{64,80},{80,96},{96,112},{112,128},... | collective-permute-start | bytes 393224 | tf_op jit(solution)/shard_map/ppermute | solution.py:30
  67.5 1.9 %collective-permute-start.3 = (f32[64,512]{1,0:T(8,128)S(1)}, f32[64,512]{1,0:T(8,128)S(1)}, u32[]{:S(2)}, u32[]{:S(2)}) collective-permute-start(f32[64,512]{1,0:T(8,128)S(1)} %get-tuple-element.32), channel_id=1, source_target_pairs={{16,0},{32,16},{48,32},{64,48},{80,64},{96,80},{112,96},{128,112},... | collective-permute-start | bytes 393224 | tf_op jit(solution)/shard_map/ppermute | solution.py:30
  69.5 10.1 %collective-permute-done.2.below_ref = f32[64,512]{1,0:T(8,128)S(1)} collective-permute-done((f32[64,512]{1,0:T(8,128)S(1)}, f32[64,512]{1,0:T(8,128)S(1)}, u32[]{:S(2)}, u32[]{:S(2)}) %collective-permute-start.2) | collective-permute-done | bytes 131104 | tf_op jit(solution)/shard_map/ppermute | solution.py:30
  79.6 1.2 collective-permute-done.3.above_ref
  80.8 0.9 copy-done.8
  81.7 0.7 collective-permute-start.11
  82.4 6.2 %shard_map.71 = (f32[4,128,128]{2,1,0:T(8,128)}, f32[128,128]{1,0:T(8,128)}, f32[128,128]{1,0:T(8,128)}, f32[128,128]{1,0:T(8,128)}) custom-call(f32[64,3072]{1,0:T(8,128)} %copy-done.1, f32[64,3072]{1,0:T(8,128)} %copy-done.8, f32[64,3072]{1,0:T(8,128)} %copy-done.6, f32[64,3072]{1,0:T(8,128)} %copy-done.9, f32[128,3072]{1,0:T(8,128)} %copy-done.5, ...), custom_call_target="tpu_custom_call" | custom-call | flops 10000000 | bytes 30000 | tf_op jit(solution)/shard_map/pallas_call | solution.py:303
  88.6 0.8 collective-permute-start.8
  89.4 2.8 %collective-permute-start.10 = (f32[128,128]{1,0:T(8,128)}, f32[128,128]{1,0:T(8,128)S(1)}, u32[]{:S(2)}, u32[]{:S(2)}) collective-permute-start(f32[128,128]{1,0:T(8,128)} %get-tuple-element.48), channel_id=1, source_target_pairs={{0,10},{1,11},{2,12},{3,13},{4,14},{5,15},{6,0},{7,1},{8,2},{9,3},... | collective-permute-start | bytes 196616 | tf_op jit(solution)/shard_map/ppermute | solution.py:24
  92.3 0.7 pad_add_fusion.place
  92.9 5.5 %shard_map.72 = f32[64,6144]{1,0:T(8,128)} custom-call(s32[512]{0:T(512)S(1)} %copy-done.2, s32[512]{0:T(512)S(1)} %copy-done.3, f32[6144,128]{1,0:T(8,128)S(1)} %get-tuple-element.43.rows.rows_ref, f32[64,512]{1,0:T(8,128)S(1)} %collective-permute-done.2.below_ref, f32[64,512]{1,0:T(8,128)S(1)} %collective-permute-done.3.above_ref), custom_call_target="tpu_custom_call" | custom-call | flops 10000000 | bytes 30000 | tf_op jit(solution)/shard_map/pallas_call | solution.py:377
  98.4 0.7 collective-permute-done.10.refs_2_
  99.1 6.7 %collective-permute-done.11.far_hbm = f32[128,3072]{1,0:T(8,128)} collective-permute-done((f32[128,3072]{1,0:T(8,128)}, f32[128,3072]{1,0:T(8,128)}, u32[]{:S(2)}, u32[]{:S(2)}) %collective-permute-start.11) | collective-permute-done | bytes 1572896 | tf_op jit(solution)/shard_map/ppermute | solution.py:24
  105.8 4.7 %shard_map.73 = f32[32,32,128]{2,1,0:T(8,128)} custom-call(s32[3]{0:T(128)} %pad_add_fusion.place, f32[64,3072]{1,0:T(8,128)} %copy-done.1, f32[64,3072]{1,0:T(8,128)} %copy-done.8, f32[128,3072]{1,0:T(8,128)} %collective-permute-done.11.far_hbm, f32[4,128,128]{2,1,0:T(8,128)} %get-tuple-element.50.near_ref, f32[128,128]{1,0:T(8,128)} %copy-done.11, ...), custom_call_target="tpu_custom_call" | custom-call | flops 2000000000 | bytes 6000000 | tf_op jit(solution)/shard_map/pallas_call | solution.py:317
  110.5 22.2 %all_to_all.5 = f32[32,32,128]{2,1,0:T(8,128)S(1)} all-to-all(f32[32,32,128]{2,1,0:T(8,128)} %shard_map.73), channel_id=1, replica_groups={{0,1,16,17,32,33,48,49,64,65,80,81,96,97,112,113,128,129,144,145,160,16..., dimensions={0} | all-to-all | bytes 1048576 | tf_op jit(solution)/shard_map/all_to_all | solution.py:391
  132.8 0.1 fusion.2
  132.9 0.7 copy.7
  (37 shorter events, 0.1 us)
Async XLA Ops:
  0.7 11.5 %copy-start.10 = (s32[3,12288]{1,0:T(4,128)S(1)}, s32[3,12288]{1,0:T(4,128)}, u32[]{:S(2)}) copy-start(s32[3,12288]{1,0:T(4,128)} %param.6) | copy-start | bytes 442372
  0.7 11.7 %copy-start = (f32[64,6144]{1,0:T(8,128)S(1)}, f32[64,6144]{1,0:T(8,128)}, u32[]{:S(2)}) copy-start(f32[64,6144]{1,0:T(8,128)} %refs_4_.3) | copy-start | bytes 4718596
  0.7 11.7 %copy-start.4 = (f32[12288]{0:T(1024)S(1)}, f32[12288]{0:T(1024)}, u32[]{:S(2)}) copy-start(f32[12288]{0:T(1024)} %refs_3_.3) | copy-start | bytes 147460
  2.3 32.6 %copy-start.6 = (f32[64,3072]{1,0:T(8,128)}, f32[64,3072]{1,0:T(8,128)S(1)}, u32[]{:S(2)}) copy-start(f32[64,3072]{1,0:T(8,128)S(1)} %get-tuple-element.57.refs_2_) | copy-start | bytes 2359300
  2.3 32.6 %collective-permute-start.1 = (f32[64,3072]{1,0:T(8,128)S(1)}, f32[64,3072]{1,0:T(8,128)S(1)}, u32[]{:S(2)}, u32[]{:S(2)}) collective-permute-start(f32[64,3072]{1,0:T(8,128)S(1)} %get-tuple-element.36), channel_id=1, source_target_pairs={{0,3},{1,2},{2,5},{3,4},{4,7},{5,6},{6,9},{7,8},{8,11},{9,10},{10,... | collective-permute-start | bytes 2359304 | tf_op jit(solution)/shard_map/ppermute | solution.py:24
  11.4 23.5 %collective-permute-start = (f32[64,3072]{1,0:T(8,128)S(1)}, f32[64,3072]{1,0:T(8,128)S(1)}, u32[]{:S(2)}, u32[]{:S(2)}) collective-permute-start(f32[64,3072]{1,0:T(8,128)S(1)} %get-tuple-element.57.refs_2_), channel_id=1, source_target_pairs={{0,2},{1,3},{2,4},{3,5},{4,6},{5,7},{6,8},{7,9},{8,10},{9,11},{10,... | collective-permute-start | bytes 2359304 | tf_op jit(solution)/shard_map/ppermute | solution.py:24
  35.0 21.0 %collective-permute-start.5 = (f32[64,3072]{1,0:T(8,128)S(1)}, f32[64,3072]{1,0:T(8,128)S(1)}, u32[]{:S(2)}, u32[]{:S(2)}) collective-permute-start(f32[64,3072]{1,0:T(8,128)S(1)} %get-tuple-element.36), channel_id=1, source_target_pairs={{0,1},{1,0},{2,3},{3,2},{4,5},{5,4},{6,7},{7,6},{8,9},{9,8},{10,11... | collective-permute-start | bytes 2359304 | tf_op jit(solution)/shard_map/ppermute | solution.py:34
  35.2 20.8 %copy-start.5 = (f32[128,3072]{1,0:T(8,128)}, f32[128,3072]{1,0:T(8,128)S(1)}, u32[]{:S(2)}) copy-start(f32[128,3072]{1,0:T(8,128)S(1)} %constant_dynamic-update-slice_fusion.refs_4_) | copy-start | bytes 4718596
  35.3 20.8 %collective-permute-start.4 = (f32[128,3072]{1,0:T(8,128)S(1)}, f32[128,3072]{1,0:T(8,128)S(1)}, u32[]{:S(2)}, u32[]{:S(2)}) collective-permute-start(f32[128,3072]{1,0:T(8,128)S(1)} %constant_dynamic-update-slice_fusion.refs_4_), channel_id=1, source_target_pairs={{0,2},{1,3},{2,4},{3,5},{4,6},{5,7},{6,8},{7,9},{8,10},{9,11},{10,... | collective-permute-start | bytes 4718600 | tf_op jit(solution)/shard_map/ppermute | solution.py:24
  36.5 24.3 %copy-start.2 = (s32[512]{0:T(512)S(1)}, s32[512]{0:T(512)}, u32[]{:S(2)}) copy-start(s32[512]{0:T(512)} %low_s.3) | copy-start | bytes 6148
  36.5 24.3 %copy-start.3 = (s32[512]{0:T(512)S(1)}, s32[512]{0:T(512)}, u32[]{:S(2)}) copy-start(s32[512]{0:T(512)} %up_s.3) | copy-start | bytes 6148
  56.0 6.8 %copy-start.1 = (f32[64,3072]{1,0:T(8,128)}, f32[64,3072]{1,0:T(8,128)S(1)}, u32[]{:S(2)}) copy-start(f32[64,3072]{1,0:T(8,128)S(1)} %get-tuple-element.30.refs_0_.ya_hbm) | copy-start | bytes 2359300
  56.0 6.8 %copy-start.9 = (f32[64,3072]{1,0:T(8,128)}, f32[64,3072]{1,0:T(8,128)S(1)}, u32[]{:S(2)}) copy-start(f32[64,3072]{1,0:T(8,128)S(1)} %collective-permute-done.5.refs_3_) | copy-start | bytes 2359300
  56.0 6.7 %copy-start.7 = (f32[128,3072]{1,0:T(8,128)}, f32[128,3072]{1,0:T(8,128)S(1)}, u32[]{:S(2)}) copy-start(f32[128,3072]{1,0:T(8,128)S(1)} %collective-permute-done.4.refs_5_) | copy-start | bytes 4718596
  56.0 24.8 %collective-permute-start.6 = (f32[128,3072]{1,0:T(8,128)S(1)}, f32[128,3072]{1,0:T(8,128)}, u32[]{:S(2)}, u32[]{:S(2)}) collective-permute-start(f32[128,3072]{1,0:T(8,128)S(1)} %collective-permute-done.4.refs_5_), channel_id=1, source_target_pairs={{0,2},{1,3},{2,4},{3,5},{4,6},{5,7},{6,8},{7,9},{8,10},{9,11},{10,... | collective-permute-start | bytes 4718600 | tf_op jit(solution)/shard_map/ppermute | solution.py:24
  57.9 22.9 %collective-permute-start.7 = (f32[64,3072]{1,0:T(8,128)S(1)}, f32[64,3072]{1,0:T(8,128)S(1)}, u32[]{:S(2)}, u32[]{:S(2)}) collective-permute-start(f32[64,3072]{1,0:T(8,128)S(1)} %get-tuple-element.38), channel_id=1, source_target_pairs={{0,1},{1,0},{2,3},{3,2},{4,5},{5,4},{6,7},{7,6},{8,9},{9,8},{10,11... | collective-permute-start | bytes 2359304 | tf_op jit(solution)/shard_map/ppermute | solution.py:34
  62.8 16.8 %collective-permute-start.2 = (f32[64,512]{1,0:T(8,128)S(1)}, f32[64,512]{1,0:T(8,128)S(1)}, u32[]{:S(2)}, u32[]{:S(2)}) collective-permute-start(f32[64,512]{1,0:T(8,128)S(1)} %get-tuple-element.31), channel_id=1, source_target_pairs={{0,16},{16,32},{32,48},{48,64},{64,80},{80,96},{96,112},{112,128},... | collective-permute-start | bytes 393224 | tf_op jit(solution)/shard_map/ppermute | solution.py:30
  67.5 13.3 %collective-permute-start.3 = (f32[64,512]{1,0:T(8,128)S(1)}, f32[64,512]{1,0:T(8,128)S(1)}, u32[]{:S(2)}, u32[]{:S(2)}) collective-permute-start(f32[64,512]{1,0:T(8,128)S(1)} %get-tuple-element.32), channel_id=1, source_target_pairs={{16,0},{32,16},{48,32},{64,48},{80,64},{96,80},{112,96},{128,112},... | collective-permute-start | bytes 393224 | tf_op jit(solution)/shard_map/ppermute | solution.py:30
  80.8 0.9 copy-start.8
  81.7 24.1 %collective-permute-start.11 = (f32[128,3072]{1,0:T(8,128)}, f32[128,3072]{1,0:T(8,128)}, u32[]{:S(2)}, u32[]{:S(2)}) collective-permute-start(f32[128,3072]{1,0:T(8,128)} %collective-permute-done.6.refs_6_), channel_id=1, source_target_pairs={{0,2},{1,3},{2,4},{3,5},{4,6},{5,7},{6,8},{7,9},{8,10},{9,11},{10,... | collective-permute-start | bytes 4718600 | tf_op jit(solution)/shard_map/ppermute | solution.py:24
  88.6 9.8 %collective-permute-start.8 = (f32[128,128]{1,0:T(8,128)}, f32[128,128]{1,0:T(8,128)S(1)}, u32[]{:S(2)}, u32[]{:S(2)}) collective-permute-start(f32[128,128]{1,0:T(8,128)} %get-tuple-element.46), channel_id=1, source_target_pairs={{0,14},{1,15},{2,0},{3,1},{4,2},{5,3},{6,4},{7,5},{8,6},{9,7},{10,... | collective-permute-start | bytes 196616 | tf_op jit(solution)/shard_map/ppermute | solution.py:24
  89.4 9.0 %collective-permute-start.9 = (f32[128,128]{1,0:T(8,128)}, f32[128,128]{1,0:T(8,128)S(1)}, u32[]{:S(2)}, u32[]{:S(2)}) collective-permute-start(f32[128,128]{1,0:T(8,128)} %get-tuple-element.47), channel_id=1, source_target_pairs={{0,12},{1,13},{2,14},{3,15},{4,0},{5,1},{6,2},{7,3},{8,4},{9,5},{1... | collective-permute-start | bytes 196616 | tf_op jit(solution)/shard_map/ppermute | solution.py:24
  89.4 9.7 %collective-permute-start.10 = (f32[128,128]{1,0:T(8,128)}, f32[128,128]{1,0:T(8,128)S(1)}, u32[]{:S(2)}, u32[]{:S(2)}) collective-permute-start(f32[128,128]{1,0:T(8,128)} %get-tuple-element.48), channel_id=1, source_target_pairs={{0,10},{1,11},{2,12},{3,13},{4,14},{5,15},{6,0},{7,1},{8,2},{9,3},... | collective-permute-start | bytes 196616 | tf_op jit(solution)/shard_map/ppermute | solution.py:24
  98.4 7.4 %copy-start.11 = (f32[128,128]{1,0:T(8,128)}, f32[128,128]{1,0:T(8,128)S(1)}, u32[]{:S(2)}) copy-start(f32[128,128]{1,0:T(8,128)S(1)} %collective-permute-done.8.refs_0_) | copy-start | bytes 196612
  98.4 7.4 %copy-start.12 = (f32[128,128]{1,0:T(8,128)}, f32[128,128]{1,0:T(8,128)S(1)}, u32[]{:S(2)}) copy-start(f32[128,128]{1,0:T(8,128)S(1)} %collective-permute-done.9.refs_1_) | copy-start | bytes 196612
  99.1 6.7 %copy-start.13 = (f32[128,128]{1,0:T(8,128)}, f32[128,128]{1,0:T(8,128)S(1)}, u32[]{:S(2)}) copy-start(f32[128,128]{1,0:T(8,128)S(1)} %collective-permute-done.10.refs_2_) | copy-start | bytes 196612

commit v10 on v8

--- a/solution.py
+++ b/solution.py
@@ -200,7 +200,7 @@
 ARRAYS, PARTS = 4, 1
 
 
-SHARES = (1, 1)
+SHARES = (7, 5)
 
 
 def apply_call(index, columns, snapshots, rows, half):
@@ -300,7 +300,7 @@
         out_specs=[IN_VMEM] * 4,
         scratch_shapes=[pltpu.VMEM(operand.shape, operand.dtype) for operand in operands]
         + [pltpu.SemaphoreType.DMA((len(operands),))],
-        compiler_params=pltpu.CompilerParams(vmem_limit_bytes=20 * MIB),
+        compiler_params=pltpu.CompilerParams(vmem_limit_bytes=60 * MIB),
         cost_estimate=cost(0.01),
     )(*operands)
 

time: 134 us -> 131 us (0.978)
  local copies, waits for them, and re-layouts: 10.9 us -> 2.66 us
  waiting for transfers between devices: 16.7 us -> 19.2 us
  Pallas kernels: 55.8 us -> 58.2 us
    unnamed x36 -> x26, local copies, waits for them, and re-layouts: 9.04 us -> 0.8 us
    ppermute x8, waiting for transfers between devices: 3.76 us -> 7.88 us  [ring_hop(): return lax.ppermute(value, ('mesh', 'snap'), pairs)]
    pallas_call x1, Pallas kernels: 4.07 us -> 6.17 us  [near_call(): pl.pallas_call(near_kernel, out_shape=[jax.ShapeDtypeStruct((4, 2 * snaps...]
    ppermute x8, starting transfers between devices: 19 us -> 17.4 us  [ring_hop(): return lax.ppermute(value, ('mesh', 'snap'), pairs)]
    ppermute x2, waiting for transfers between devices: 12.9 us -> 11.3 us  [passed_along(): lax.ppermute(value, axis, [(source, source + steps) for source in range(l...]
    ppermute x2, starting transfers between devices: 5.26 us -> 6.64 us  [passed_along(): lax.ppermute(value, axis, [(source, source + steps) for source in range(l...]
  transfers between devices with their start and end apart: 12 -> 12, of which waited for: 4 -> 4; matrix products, arithmetic and copies ran while one was open for 0% -> 0% of each run, Pallas kernels for 40% -> 43%
where the time goes in v10:
time: 131 us; the launch traced here: 130 us
  Pallas kernels  58.2 us (44%)
  starting transfers between devices  27.1 us (21%)
  blocking collectives  22.1 us (17%)
  waiting for transfers between devices  19.2 us (15%)
  local copies, waits for them, and re-layouts  2.66 us (2%)
    pallas_call x2, Pallas kernels, apply_call(): pl.pallas_call(functools.partial(apply_kernel, first, last, start, count,...  42 us
    all_to_all x1, blocking collectives, on_device(): lax.all_to_all(tiles, ('mesh', 'snap'), 0, 0, axis_index_groups=planes, t...  22.1 us
    ppermute x8, starting transfers between devices, ring_hop(): return lax.ppermute(value, ('mesh', 'snap'), pairs)  17.4 us
    ppermute x2, waiting for transfers between devices, passed_along(): lax.ppermute(value, axis, [(source, source + steps) for source in range(l...  11.3 us
    ppermute x8, waiting for transfers between devices, ring_hop(): return lax.ppermute(value, ('mesh', 'snap'), pairs)  7.88 us
    ppermute x2, starting transfers between devices, passed_along(): lax.ppermute(value, axis, [(source, source + steps) for source in range(l...  6.64 us
    pallas_call x1, Pallas kernels, near_call(): pl.pallas_call(near_kernel, out_shape=[jax.ShapeDtypeStruct((4, 2 * snaps...  6.17 us
    pallas_call x1, Pallas kernels, on_device(): pl.pallas_call(assemble_kernel, out_shape=jax.ShapeDtypeStruct((snaps, no...  5.46 us
  transfers between devices with their start and end apart: 12, of which 4 were waited for; matrix products, arithmetic and copies ran while one was open for 0% of the time, Pallas kernels for 43%

profile of v10, /device:TPU:1, one launch (start us, length us, event | category | flops | bytes accessed | tf_op | source)
XLA Modules:
  0.0 130.4 jit_solution(1885120290444484871)
XLA Ops:
  0.7 1.6 %constant_dynamic-slice_fusion = (f32[64,3072]{1,0:T(8,128)S(1)}, f32[64,3072]{1,0:T(8,128)S(1)}) fusion(f32[64,6144]{1,0:T(8,128)} %refs_4_.3, s32[]{:T(128)S(6)} %select_n.27, s32[]{:T(128)S(6)} %select_n.26), kind=kLoop, calls=%fused_computation.6 | loop fusion | bytes 3145736 | tf_op jit(solution)/shard_map/dynamic_slice | solution.py:332
  2.3 9.1 %collective-permute-start.1 = (f32[64,3072]{1,0:T(8,128)S(1)}, f32[64,3072]{1,0:T(8,128)S(1)}, u32[]{:S(2)}, u32[]{:S(2)}) collective-permute-start(f32[64,3072]{1,0:T(8,128)S(1)} %get-tuple-element.36), channel_id=1, source_target_pairs={{0,3},{1,2},{2,5},{3,4},{4,7},{5,6},{6,9},{7,8},{8,11},{9,10},{10,... | collective-permute-start | bytes 2359304 | tf_op jit(solution)/shard_map/ppermute | solution.py:24
  11.4 0.7 collective-permute-start
  12.2 0.1 and_add_fusion
  12.2 0.1 fusion.1
  12.4 22.6 %shard_map.68.refs_5_ = f32[6144,128]{1,0:T(8,128)S(1)} custom-call(s32[12288]{0:T(1024)S(1)} %bitcast.12, s32[12288]{0:T(1024)S(1)} %bitcast.10, s32[12288]{0:T(1024)S(1)} %bitcast.8, f32[12288]{0:T(1024)S(1)} %copy-done.6, f32[64,6144]{1,0:T(8,128)S(1)} %copy-done), custom_call_target="tpu_custom_call" | custom-call | flops 20000000000 | bytes 60000000 | tf_op jit(solution)/shard_map/pallas_call | solution.py:215
  35.0 0.0 collective-permute-done
  35.0 0.1 collective-permute-start.5
  35.1 0.1 constant_dynamic-update-slice_fusion.1
  35.2 0.1 constant_dynamic-update-slice_fusion.refs_4_
  35.2 0.0 copy-start.7
  35.2 1.3 collective-permute-start.4
  36.5 19.5 %shard_map.69 = (f32[6144,128]{1,0:T(8,128)S(1)}, f32[64,3072]{1,0:T(8,128)S(1)}, f32[64,3072]{1,0:T(8,128)S(1)}) custom-call(s32[12288]{0:T(1024)S(1)} %bitcast.13, s32[12288]{0:T(1024)S(1)} %bitcast.11, s32[12288]{0:T(1024)S(1)} %bitcast.9, f32[12288]{0:T(1024)S(1)} %copy-done.6, f32[64,6144]{1,0:T(8,128)S(1)} %copy-done, ...), custom_call_target="tpu_custom_call" | custom-call | flops 20000000000 | bytes 60000000 | tf_op jit(solution)/shard_map/pallas_call | solution.py:215
  56.0 1.8 %collective-permute-start.6 = (f32[128,3072]{1,0:T(8,128)S(1)}, f32[128,3072]{1,0:T(8,128)}, u32[]{:S(2)}, u32[]{:S(2)}) collective-permute-start(f32[128,3072]{1,0:T(8,128)S(1)} %collective-permute-done.4.refs_5_), channel_id=1, source_target_pairs={{0,2},{1,3},{2,4},{3,5},{4,6},{5,7},{6,8},{7,9},{8,10},{9,11},{10,... | collective-permute-start | bytes 4718600 | tf_op jit(solution)/shard_map/ppermute | solution.py:24
  57.9 2.9 %collective-permute-start.7 = (f32[64,3072]{1,0:T(8,128)S(1)}, f32[64,3072]{1,0:T(8,128)}, u32[]{:S(2)}, u32[]{:S(2)}) collective-permute-start(f32[64,3072]{1,0:T(8,128)S(1)} %get-tuple-element.38), channel_id=1, source_target_pairs={{0,1},{1,0},{2,3},{3,2},{4,5},{5,4},{6,7},{7,6},{8,9},{9,8},{10,11... | collective-permute-start | bytes 2359304 | tf_op jit(solution)/shard_map/ppermute | solution.py:34
  60.8 2.0 %shard_map.70 = (f32[64,512]{1,0:T(8,128)S(1)}, f32[64,512]{1,0:T(8,128)S(1)}) custom-call(s32[512]{0:T(512)S(1)} %copy-done.3, s32[512]{0:T(512)S(1)} %copy-done.4, f32[6144,128]{1,0:T(8,128)S(1)} %get-tuple-element.43.rows.rows_ref), custom_call_target="tpu_custom_call" | custom-call | flops 10000000 | bytes 30000 | tf_op jit(solution)/shard_map/pallas_call | solution.py:352
  62.8 4.7 %collective-permute-start.2 = (f32[64,512]{1,0:T(8,128)S(1)}, f32[64,512]{1,0:T(8,128)S(1)}, u32[]{:S(2)}, u32[]{:S(2)}) collective-permute-start(f32[64,512]{1,0:T(8,128)S(1)} %get-tuple-element.31), channel_id=1, source_target_pairs={{0,16},{16,32},{32,48},{48,64},{64,80},{80,96},{96,112},{112,128},... | collective-permute-start | bytes 393224 | tf_op jit(solution)/shard_map/ppermute | solution.py:30
  67.5 1.9 %collective-permute-start.3 = (f32[64,512]{1,0:T(8,128)S(1)}, f32[64,512]{1,0:T(8,128)S(1)}, u32[]{:S(2)}, u32[]{:S(2)}) collective-permute-start(f32[64,512]{1,0:T(8,128)S(1)} %get-tuple-element.32), channel_id=1, source_target_pairs={{16,0},{32,16},{48,32},{64,48},{80,64},{96,80},{112,96},{128,112},... | collective-permute-start | bytes 393224 | tf_op jit(solution)/shard_map/ppermute | solution.py:30
  69.4 10.1 %collective-permute-done.2.below_ref = f32[64,512]{1,0:T(8,128)S(1)} collective-permute-done((f32[64,512]{1,0:T(8,128)S(1)}, f32[64,512]{1,0:T(8,128)S(1)}, u32[]{:S(2)}, u32[]{:S(2)}) %collective-permute-start.2) | collective-permute-done | bytes 131104 | tf_op jit(solution)/shard_map/ppermute | solution.py:30
  79.6 1.2 collective-permute-done.3.above_ref
  80.8 0.7 collective-permute-start.11
  81.5 6.2 %shard_map.71 = (f32[4,128,128]{2,1,0:T(8,128)}, f32[128,128]{1,0:T(8,128)}, f32[128,128]{1,0:T(8,128)}, f32[128,128]{1,0:T(8,128)}) custom-call(f32[64,3072]{1,0:T(8,128)} %copy-done.1, f32[64,3072]{1,0:T(8,128)} %collective-permute-done.7.refs_1_.yb_ref, f32[64,3072]{1,0:T(8,128)} %copy-done.8, f32[64,3072]{1,0:T(8,128)} %copy-done.10, ...), custom_call_target="tpu_custom_call" | custom-call | flops 10000000 | bytes 30000 | tf_op jit(solution)/shard_map/pallas_call | solution.py:296
  87.7 0.8 collective-permute-start.8
  88.5 2.9 %collective-permute-start.10 = (f32[128,128]{1,0:T(8,128)}, f32[128,128]{1,0:T(8,128)S(1)}, u32[]{:S(2)}, u32[]{:S(2)}) collective-permute-start(f32[128,128]{1,0:T(8,128)} %get-tuple-element.48), channel_id=1, source_target_pairs={{0,10},{1,11},{2,12},{3,13},{4,14},{5,15},{6,0},{7,1},{8,2},{9,3},... | collective-permute-start | bytes 196616 | tf_op jit(solution)/shard_map/ppermute | solution.py:24
  91.5 0.1 pad_add_fusion.place
  91.5 5.5 %shard_map.72 = f32[64,6144]{1,0:T(8,128)} custom-call(s32[512]{0:T(512)S(1)} %copy-done.3, s32[512]{0:T(512)S(1)} %copy-done.4, f32[6144,128]{1,0:T(8,128)S(1)} %get-tuple-element.43.rows.rows_ref, f32[64,512]{1,0:T(8,128)S(1)} %collective-permute-done.2.below_ref, f32[64,512]{1,0:T(8,128)S(1)} %collective-permute-done.3.above_ref), custom_call_target="tpu_custom_call" | custom-call | flops 10000000 | bytes 30000 | tf_op jit(solution)/shard_map/pallas_call | solution.py:368
  97.0 1.2 collective-permute-done.10.refs_2_
  98.3 6.6 %collective-permute-done.11.far_ref = f32[128,3072]{1,0:T(8,128)} collective-permute-done((f32[128,3072]{1,0:T(8,128)}, f32[128,3072]{1,0:T(8,128)}, u32[]{:S(2)}, u32[]{:S(2)}) %collective-permute-start.11) | collective-permute-done | bytes 1572896 | tf_op jit(solution)/shard_map/ppermute | solution.py:24
  104.9 2.6 %shard_map.73 = f32[32,32,128]{2,1,0:T(8,128)S(1)} custom-call(s32[3]{0:T(128)S(1)} %pad_add_fusion.place, f32[64,3072]{1,0:T(8,128)S(1)} %copy-done.2, f32[64,3072]{1,0:T(8,128)} %collective-permute-done.7.refs_1_.yb_ref, f32[128,3072]{1,0:T(8,128)} %collective-permute-done.11.far_ref, f32[4,128,128]{2,1,0:T(8,128)S(1)} %copy-done.5, ...), custom_call_target="tpu_custom_call" | custom-call | flops 2000000000 | bytes 6000000 | tf_op jit(solution)/shard_map/pallas_call | solution.py:310
  107.5 22.1 %all_to_all.5 = f32[32,32,128]{2,1,0:T(8,128)S(1)} all-to-all(f32[32,32,128]{2,1,0:T(8,128)S(1)} %shard_map.73), channel_id=1, replica_groups={{0,1,16,17,32,33,48,49,64,65,80,81,96,97,112,113,128,129,144,145,160,16..., dimensions={0} | all-to-all | bytes 1048576 | tf_op jit(solution)/shard_map/all_to_all | solution.py:382
  129.6 0.1 fusion.2
  129.7 0.7 copy.7
  (33 shorter events, 0.1 us)
Async XLA Ops:
  0.7 11.5 %copy-start.11 = (s32[3,12288]{1,0:T(4,128)S(1)}, s32[3,12288]{1,0:T(4,128)}, u32[]{:S(2)}) copy-start(s32[3,12288]{1,0:T(4,128)} %param.6) | copy-start | bytes 442372
  0.7 11.7 %copy-start = (f32[64,6144]{1,0:T(8,128)S(1)}, f32[64,6144]{1,0:T(8,128)}, u32[]{:S(2)}) copy-start(f32[64,6144]{1,0:T(8,128)} %refs_4_.3) | copy-start | bytes 4718596
  0.7 11.7 %copy-start.6 = (f32[12288]{0:T(1024)S(1)}, f32[12288]{0:T(1024)}, u32[]{:S(2)}) copy-start(f32[12288]{0:T(1024)} %refs_3_.3) | copy-start | bytes 147460
  2.3 32.6 %copy-start.8 = (f32[64,3072]{1,0:T(8,128)}, f32[64,3072]{1,0:T(8,128)S(1)}, u32[]{:S(2)}) copy-start(f32[64,3072]{1,0:T(8,128)S(1)} %get-tuple-element.57.refs_2_) | copy-start | bytes 2359300
  2.3 32.6 %collective-permute-start.1 = (f32[64,3072]{1,0:T(8,128)S(1)}, f32[64,3072]{1,0:T(8,128)S(1)}, u32[]{:S(2)}, u32[]{:S(2)}) collective-permute-start(f32[64,3072]{1,0:T(8,128)S(1)} %get-tuple-element.36), channel_id=1, source_target_pairs={{0,3},{1,2},{2,5},{3,4},{4,7},{5,6},{6,9},{7,8},{8,11},{9,10},{10,... | collective-permute-start | bytes 2359304 | tf_op jit(solution)/shard_map/ppermute | solution.py:24
  11.4 23.5 %collective-permute-start = (f32[64,3072]{1,0:T(8,128)S(1)}, f32[64,3072]{1,0:T(8,128)S(1)}, u32[]{:S(2)}, u32[]{:S(2)}) collective-permute-start(f32[64,3072]{1,0:T(8,128)S(1)} %get-tuple-element.57.refs_2_), channel_id=1, source_target_pairs={{0,2},{1,3},{2,4},{3,5},{4,6},{5,7},{6,8},{7,9},{8,10},{9,11},{10,... | collective-permute-start | bytes 2359304 | tf_op jit(solution)/shard_map/ppermute | solution.py:24
  35.0 21.0 %collective-permute-start.5 = (f32[64,3072]{1,0:T(8,128)S(1)}, f32[64,3072]{1,0:T(8,128)S(1)}, u32[]{:S(2)}, u32[]{:S(2)}) collective-permute-start(f32[64,3072]{1,0:T(8,128)S(1)} %get-tuple-element.36), channel_id=1, source_target_pairs={{0,1},{1,0},{2,3},{3,2},{4,5},{5,4},{6,7},{7,6},{8,9},{9,8},{10,11... | collective-permute-start | bytes 2359304 | tf_op jit(solution)/shard_map/ppermute | solution.py:34
  35.2 20.7 %copy-start.7 = (f32[128,3072]{1,0:T(8,128)}, f32[128,3072]{1,0:T(8,128)S(1)}, u32[]{:S(2)}) copy-start(f32[128,3072]{1,0:T(8,128)S(1)} %constant_dynamic-update-slice_fusion.refs_4_) | copy-start | bytes 4718596
  35.2 20.8 %collective-permute-start.4 = (f32[128,3072]{1,0:T(8,128)S(1)}, f32[128,3072]{1,0:T(8,128)S(1)}, u32[]{:S(2)}, u32[]{:S(2)}) collective-permute-start(f32[128,3072]{1,0:T(8,128)S(1)} %constant_dynamic-update-slice_fusion.refs_4_), channel_id=1, source_target_pairs={{0,2},{1,3},{2,4},{3,5},{4,6},{5,7},{6,8},{7,9},{8,10},{9,11},{10,... | collective-permute-start | bytes 4718600 | tf_op jit(solution)/shard_map/ppermute | solution.py:24
  36.5 24.3 %copy-start.3 = (s32[512]{0:T(512)S(1)}, s32[512]{0:T(512)}, u32[]{:S(2)}) copy-start(s32[512]{0:T(512)} %low_s.3) | copy-start | bytes 6148
  36.5 24.3 %copy-start.4 = (s32[512]{0:T(512)S(1)}, s32[512]{0:T(512)}, u32[]{:S(2)}) copy-start(s32[512]{0:T(512)} %up_s.3) | copy-start | bytes 6148
  56.0 6.8 %copy-start.1 = (f32[64,3072]{1,0:T(8,128)}, f32[64,3072]{1,0:T(8,128)S(1)}, u32[]{:S(2)}) copy-start(f32[64,3072]{1,0:T(8,128)S(1)} %get-tuple-element.30.refs_0_.ya_ref) | copy-start | bytes 2359300
  56.0 6.8 %copy-start.10 = (f32[64,3072]{1,0:T(8,128)}, f32[64,3072]{1,0:T(8,128)S(1)}, u32[]{:S(2)}) copy-start(f32[64,3072]{1,0:T(8,128)S(1)} %collective-permute-done.5.refs_3_) | copy-start | bytes 2359300
  56.0 6.7 %copy-start.9 = (f32[128,3072]{1,0:T(8,128)}, f32[128,3072]{1,0:T(8,128)S(1)}, u32[]{:S(2)}) copy-start(f32[128,3072]{1,0:T(8,128)S(1)} %collective-permute-done.4.refs_5_) | copy-start | bytes 4718596
  56.0 24.8 %collective-permute-start.6 = (f32[128,3072]{1,0:T(8,128)S(1)}, f32[128,3072]{1,0:T(8,128)}, u32[]{:S(2)}, u32[]{:S(2)}) collective-permute-start(f32[128,3072]{1,0:T(8,128)S(1)} %collective-permute-done.4.refs_5_), channel_id=1, source_target_pairs={{0,2},{1,3},{2,4},{3,5},{4,6},{5,7},{6,8},{7,9},{8,10},{9,11},{10,... | collective-permute-start | bytes 4718600 | tf_op jit(solution)/shard_map/ppermute | solution.py:24
  57.9 22.9 %collective-permute-start.7 = (f32[64,3072]{1,0:T(8,128)S(1)}, f32[64,3072]{1,0:T(8,128)}, u32[]{:S(2)}, u32[]{:S(2)}) collective-permute-start(f32[64,3072]{1,0:T(8,128)S(1)} %get-tuple-element.38), channel_id=1, source_target_pairs={{0,1},{1,0},{2,3},{3,2},{4,5},{5,4},{6,7},{7,6},{8,9},{9,8},{10,11... | collective-permute-start | bytes 2359304 | tf_op jit(solution)/shard_map/ppermute | solution.py:34
  62.8 16.8 %collective-permute-start.2 = (f32[64,512]{1,0:T(8,128)S(1)}, f32[64,512]{1,0:T(8,128)S(1)}, u32[]{:S(2)}, u32[]{:S(2)}) collective-permute-start(f32[64,512]{1,0:T(8,128)S(1)} %get-tuple-element.31), channel_id=1, source_target_pairs={{0,16},{16,32},{32,48},{48,64},{64,80},{80,96},{96,112},{112,128},... | collective-permute-start | bytes 393224 | tf_op jit(solution)/shard_map/ppermute | solution.py:30
  67.5 13.3 %collective-permute-start.3 = (f32[64,512]{1,0:T(8,128)S(1)}, f32[64,512]{1,0:T(8,128)S(1)}, u32[]{:S(2)}, u32[]{:S(2)}) collective-permute-start(f32[64,512]{1,0:T(8,128)S(1)} %get-tuple-element.32), channel_id=1, source_target_pairs={{16,0},{32,16},{48,32},{64,48},{80,64},{96,80},{112,96},{128,112},... | collective-permute-start | bytes 393224 | tf_op jit(solution)/shard_map/ppermute | solution.py:30
  80.8 24.1 %collective-permute-start.11 = (f32[128,3072]{1,0:T(8,128)}, f32[128,3072]{1,0:T(8,128)}, u32[]{:S(2)}, u32[]{:S(2)}) collective-permute-start(f32[128,3072]{1,0:T(8,128)} %collective-permute-done.6.refs_6_), channel_id=1, source_target_pairs={{0,2},{1,3},{2,4},{3,5},{4,6},{5,7},{6,8},{7,9},{8,10},{9,11},{10,... | collective-permute-start | bytes 4718600 | tf_op jit(solution)/shard_map/ppermute | solution.py:24
  87.7 9.3 %collective-permute-start.8 = (f32[128,128]{1,0:T(8,128)}, f32[128,128]{1,0:T(8,128)S(1)}, u32[]{:S(2)}, u32[]{:S(2)}) collective-permute-start(f32[128,128]{1,0:T(8,128)} %get-tuple-element.46), channel_id=1, source_target_pairs={{0,14},{1,15},{2,0},{3,1},{4,2},{5,3},{6,4},{7,5},{8,6},{9,7},{10,... | collective-permute-start | bytes 196616 | tf_op jit(solution)/shard_map/ppermute | solution.py:24
  88.5 8.5 %collective-permute-start.9 = (f32[128,128]{1,0:T(8,128)}, f32[128,128]{1,0:T(8,128)S(1)}, u32[]{:S(2)}, u32[]{:S(2)}) collective-permute-start(f32[128,128]{1,0:T(8,128)} %get-tuple-element.47), channel_id=1, source_target_pairs={{0,12},{1,13},{2,14},{3,15},{4,0},{5,1},{6,2},{7,3},{8,4},{9,5},{1... | collective-permute-start | bytes 196616 | tf_op jit(solution)/shard_map/ppermute | solution.py:24
  88.5 9.7 %collective-permute-start.10 = (f32[128,128]{1,0:T(8,128)}, f32[128,128]{1,0:T(8,128)S(1)}, u32[]{:S(2)}, u32[]{:S(2)}) collective-permute-start(f32[128,128]{1,0:T(8,128)} %get-tuple-element.48), channel_id=1, source_target_pairs={{0,10},{1,11},{2,12},{3,13},{4,14},{5,15},{6,0},{7,1},{8,2},{9,3},... | collective-permute-start | bytes 196616 | tf_op jit(solution)/shard_map/ppermute | solution.py:24
  91.5 13.4 %copy-start.2 = (f32[64,3072]{1,0:T(8,128)S(1)}, f32[64,3072]{1,0:T(8,128)}, u32[]{:S(2)}) copy-start(f32[64,3072]{1,0:T(8,128)} %copy-done.1) | copy-start | bytes 2359300
  91.5 13.4 %copy-start.5 = (f32[4,128,128]{2,1,0:T(8,128)S(1)}, f32[4,128,128]{2,1,0:T(8,128)}, u32[]{:S(2)}) copy-start(f32[4,128,128]{2,1,0:T(8,128)} %get-tuple-element.50.near_ref) | copy-start | bytes 786436

commit v11 on v10

--- a/solution.py
+++ b/solution.py
@@ -90,7 +90,7 @@
                     z[pl.ds(n + 8 * (1 + k // 2), 1), at:at + snaps] = new[:, at:at + snaps]
         return carry
 
-    lax.fori_loop(0, count // (arrays * 2 * parts), elements, 0, unroll=8)
+    lax.fori_loop(0, count // (arrays * 2 * parts), elements, 0, unroll=16)
 
     if not first:
         earlier.wait()
@@ -267,27 +267,29 @@
             back[distance - 1][...] = value.T
 
 
-def far_kernel(place, ya_ref, yb_ref, far_ref, near_ref, *refs):
+def put(out_ref, place, distance, value):
+    z, h, way = place[0], place[1], place[2]
+    rings, low, snaps = out_ref.shape[0] // 4, out_ref.shape[1], out_ref.shape[2] // 2
+    at = lax.rem(z - way * distance + rings, rings)
+    for side in range(2):
+        row = 2 * at + (h if side == 0 else 1 - h)
+        upper, lower = value[side * snaps:side * snaps + low], value[side * snaps + low:(side + 1) * snaps]
+        out_ref[2 * row + h] = jnp.concatenate([upper[:, :snaps], lower[:, :snaps]], axis=1)
+        out_ref[2 * row + (1 - h)] = jnp.concatenate([upper[:, snaps:], lower[:, snaps:]], axis=1)
+
+
+def lay_kernel(place, near_ref, *refs):
     *back, out_ref = refs
-    snaps = ya_ref.shape[0]
-    rings = out_ref.shape[0] // 4
-    low = snaps // 2
-    z, h, way = place[0], place[1], place[2]
-
-    def put(distance, value):
-        at = lax.rem(z - way * distance + rings, rings)
-        for side in range(2):
-            row = 2 * at + (h if side == 0 else 1 - h)
-            upper, lower = value[side * snaps:side * snaps + low], value[side * snaps + low:(side + 1) * snaps]
-            out_ref[2 * row + h] = jnp.concatenate([upper[:, :snaps], lower[:, :snaps]], axis=1)
-            out_ref[2 * row + (1 - h)] = jnp.concatenate([upper[:, snaps:], lower[:, snaps:]], axis=1)
-
-    put(0, near_ref[0])
+    put(out_ref, place, 0, near_ref[0])
     for distance, received in enumerate(back, 1):
-        put(distance, near_ref[distance])
-        put(-distance, received[...])
+        put(out_ref, place, distance, near_ref[distance])
+        put(out_ref, place, -distance, received[...])
+    put(out_ref, place, out_ref.shape[0] // 8, jnp.zeros_like(near_ref[0]))
+
+
+def far_kernel(place, ya_ref, yb_ref, far_ref, laid_ref, out_ref):
     (value,) = product(lambda _, at: far_ref[:, at], ya_ref, yb_ref, 1)
-    put(rings // 2, value)
+    put(out_ref, place, out_ref.shape[0] // 8, value)
 
 
 def near_call(*operands):
@@ -305,16 +307,28 @@
     )(*operands)
 
 
-def far_call(place, ya, yb, far, near, back, rings):
-    snaps = ya.shape[0]
+def lay_call(place, near, back, rings):
+    snaps = near.shape[1] // 2
+    return pl.pallas_call(
+        lay_kernel,
+        out_shape=jax.ShapeDtypeStruct((4 * rings, snaps // 2, 2 * snaps), jnp.float32),
+        in_specs=[IN_SMEM] + [IN_VMEM] * (1 + len(back)),
+        out_specs=IN_VMEM,
+        compiler_params=pltpu.CompilerParams(vmem_limit_bytes=16 * MIB),
+        cost_estimate=cost(0.01),
+    )(place, near, *back)
+
+
+def far_call(place, ya, yb, far, laid):
     return pl.pallas_call(
         far_kernel,
-        out_shape=jax.ShapeDtypeStruct((4 * rings, snaps // 2, 2 * snaps), jnp.float32),
-        in_specs=[IN_SMEM] + [IN_VMEM] * (4 + len(back)),
+        out_shape=jax.ShapeDtypeStruct(laid.shape, laid.dtype),
+        in_specs=[IN_SMEM] + [IN_VMEM] * 4,
         out_specs=IN_VMEM,
+        input_output_aliases={4: 0},
         compiler_params=pltpu.CompilerParams(vmem_limit_bytes=16 * MIB),
         cost_estimate=cost(2),
-    )(place, ya, yb, far, near, *back)
+    )(place, ya, yb, far, laid)
 
 
 def on_device(snapshots, connectivity, element_mass, lower_shared, upper_shared):
@@ -377,7 +391,9 @@
     )(lower_shared, upper_shared, rows, from_below, from_above)
     weighted, *back = tied((weighted, *back))
     place = jnp.stack([z, h, jnp.where(position % 2 == 0, 1, -1)]).astype(jnp.int32)
-    tiles = far_call(place, y_own, y_theirs, pair4, near, back, rings)
+    laid = lay_call(place, near, back, rings)
+    laid, pair4 = tied((laid, pair4))
+    tiles = far_call(place, y_own, y_theirs, pair4, laid)
     planes = [[m * blocks + 2 * r + c for m in range(parts) for c in range(2)] for r in range(rings)]
     tile = jnp.sum(lax.all_to_all(tiles, ("mesh", "snap"), 0, 0, axis_index_groups=planes, tiled=True), axis=0)
     column = jnp.concatenate([tile[:, :snaps], tile[:, snaps:]], axis=0)

time: 131 us -> 130 us (level)
    pallas_call x1 -> x2, Pallas kernels: 2.58 us -> 3.29 us  [the longest x1 2.57 us: far_call(): pl.pallas_call(far_kernel, out_shape=jax.ShapeDtypeStruct(laid.shape, lai...]
where the time goes in v11:
time: 130 us
  Pallas kernels  58.2 us (45%)
  starting transfers between devices  28 us (22%)
  blocking collectives  22.1 us (17%)
  waiting for transfers between devices  18 us (14%)
  local copies, waits for them, and re-layouts  2.66 us (2%)
    pallas_call x2, Pallas kernels, apply_call(): pl.pallas_call(functools.partial(apply_kernel, first, last, start, count,...  41.3 us
    all_to_all x1, blocking collectives, on_device(): lax.all_to_all(tiles, ('mesh', 'snap'), 0, 0, axis_index_groups=planes, t...  22.1 us
    ppermute x8, starting transfers between devices, ring_hop(): return lax.ppermute(value, ('mesh', 'snap'), pairs)  18 us
    ppermute x2, waiting for transfers between devices, passed_along(): lax.ppermute(value, axis, [(source, source + steps) for source in range(l...  11 us
    ppermute x8, waiting for transfers between devices, ring_hop(): return lax.ppermute(value, ('mesh', 'snap'), pairs)  6.97 us
    ppermute x2, starting transfers between devices, passed_along(): lax.ppermute(value, axis, [(source, source + steps) for source in range(l...  6.96 us
    pallas_call x1, Pallas kernels, near_call(): pl.pallas_call(near_kernel, out_shape=[jax.ShapeDtypeStruct((4, 2 * snaps...  6.17 us
    pallas_call x1, Pallas kernels, on_device(): pl.pallas_call(assemble_kernel, out_shape=jax.ShapeDtypeStruct((snaps, no...  5.46 us
  transfers between devices with their start and end apart: 12, of which 4 were waited for; matrix products, arithmetic and copies ran while one was open for 0% of the time, Pallas kernels for 43%

profile of v11, /device:TPU:1, one launch (start us, length us, event | category | flops | bytes accessed | tf_op | source)
XLA Modules:
  0.0 130.1 jit_solution(17831381924567684671)
XLA Ops:
  0.7 1.6 %constant_dynamic-slice_fusion = (f32[64,3072]{1,0:T(8,128)S(1)}, f32[64,3072]{1,0:T(8,128)S(1)}) fusion(f32[64,6144]{1,0:T(8,128)} %refs_4_.3, s32[]{:T(128)S(6)} %select_n.27, s32[]{:T(128)S(6)} %select_n.26), kind=kLoop, calls=%fused_computation.6 | loop fusion | bytes 3145736 | tf_op jit(solution)/shard_map/dynamic_slice | solution.py:346
  2.3 9.1 %collective-permute-start.1 = (f32[64,3072]{1,0:T(8,128)S(1)}, f32[64,3072]{1,0:T(8,128)S(1)}, u32[]{:S(2)}, u32[]{:S(2)}) collective-permute-start(f32[64,3072]{1,0:T(8,128)S(1)} %get-tuple-element.38), channel_id=1, source_target_pairs={{0,3},{1,2},{2,5},{3,4},{4,7},{5,6},{6,9},{7,8},{8,11},{9,10},{10,... | collective-permute-start | bytes 2359304 | tf_op jit(solution)/shard_map/ppermute | solution.py:24
  11.4 0.7 collective-permute-start
  12.2 0.1 and_add_fusion
  12.2 0.1 fusion.1
  12.4 22.1 %shard_map.68.refs_5_ = f32[6144,128]{1,0:T(8,128)S(1)} custom-call(s32[12288]{0:T(1024)S(1)} %bitcast.12, s32[12288]{0:T(1024)S(1)} %bitcast.10, s32[12288]{0:T(1024)S(1)} %bitcast.8, f32[12288]{0:T(1024)S(1)} %copy-done.6, f32[64,6144]{1,0:T(8,128)S(1)} %copy-done), custom_call_target="tpu_custom_call" | custom-call | flops 20000000000 | bytes 60000000 | tf_op jit(solution)/shard_map/pallas_call | solution.py:215
  34.6 0.1 collective-permute-start.5
  34.7 0.1 constant_dynamic-update-slice_fusion.1
  34.8 0.1 constant_dynamic-update-slice_fusion.refs_4_
  34.8 0.0 copy-start.7
  34.8 1.7 %collective-permute-start.4 = (f32[128,3072]{1,0:T(8,128)S(1)}, f32[128,3072]{1,0:T(8,128)S(1)}, u32[]{:S(2)}, u32[]{:S(2)}) collective-permute-start(f32[128,3072]{1,0:T(8,128)S(1)} %constant_dynamic-update-slice_fusion.refs_4_), channel_id=1, source_target_pairs={{0,2},{1,3},{2,4},{3,5},{4,6},{5,7},{6,8},{7,9},{8,10},{9,11},{10,... | collective-permute-start | bytes 4718600 | tf_op jit(solution)/shard_map/ppermute | solution.py:24
  36.5 19.1 %shard_map.69 = (f32[6144,128]{1,0:T(8,128)S(1)}, f32[64,3072]{1,0:T(8,128)S(1)}, f32[64,3072]{1,0:T(8,128)S(1)}) custom-call(s32[12288]{0:T(1024)S(1)} %bitcast.13, s32[12288]{0:T(1024)S(1)} %bitcast.11, s32[12288]{0:T(1024)S(1)} %bitcast.9, f32[12288]{0:T(1024)S(1)} %copy-done.6, f32[64,6144]{1,0:T(8,128)S(1)} %copy-done, ...), custom_call_target="tpu_custom_call" | custom-call | flops 20000000000 | bytes 60000000 | tf_op jit(solution)/shard_map/pallas_call | solution.py:215
  55.7 1.8 %collective-permute-start.6 = (f32[128,3072]{1,0:T(8,128)S(1)}, f32[128,3072]{1,0:T(8,128)}, u32[]{:S(2)}, u32[]{:S(2)}) collective-permute-start(f32[128,3072]{1,0:T(8,128)S(1)} %collective-permute-done.4.refs_5_), channel_id=1, source_target_pairs={{0,2},{1,3},{2,4},{3,5},{4,6},{5,7},{6,8},{7,9},{8,10},{9,11},{10,... | collective-permute-start | bytes 4718600 | tf_op jit(solution)/shard_map/ppermute | solution.py:24
  57.6 2.9 %collective-permute-start.7 = (f32[64,3072]{1,0:T(8,128)S(1)}, f32[64,3072]{1,0:T(8,128)}, u32[]{:S(2)}, u32[]{:S(2)}) collective-permute-start(f32[64,3072]{1,0:T(8,128)S(1)} %get-tuple-element.40), channel_id=1, source_target_pairs={{0,1},{1,0},{2,3},{3,2},{4,5},{5,4},{6,7},{7,6},{8,9},{9,8},{10,11... | collective-permute-start | bytes 2359304 | tf_op jit(solution)/shard_map/ppermute | solution.py:34
  60.5 2.0 %shard_map.70 = (f32[64,512]{1,0:T(8,128)S(1)}, f32[64,512]{1,0:T(8,128)S(1)}) custom-call(s32[512]{0:T(512)S(1)} %copy-done.4, s32[512]{0:T(512)S(1)} %copy-done.5, f32[6144,128]{1,0:T(8,128)S(1)} %get-tuple-element.45.rows.rows_ref), custom_call_target="tpu_custom_call" | custom-call | flops 10000000 | bytes 30000 | tf_op jit(solution)/shard_map/pallas_call | solution.py:366
  62.5 5.0 %collective-permute-start.2 = (f32[64,512]{1,0:T(8,128)S(1)}, f32[64,512]{1,0:T(8,128)S(1)}, u32[]{:S(2)}, u32[]{:S(2)}) collective-permute-start(f32[64,512]{1,0:T(8,128)S(1)} %get-tuple-element.33), channel_id=1, source_target_pairs={{0,16},{16,32},{32,48},{48,64},{64,80},{80,96},{96,112},{112,128},... | collective-permute-start | bytes 393224 | tf_op jit(solution)/shard_map/ppermute | solution.py:30
  67.5 1.9 %collective-permute-start.3 = (f32[64,512]{1,0:T(8,128)S(1)}, f32[64,512]{1,0:T(8,128)S(1)}, u32[]{:S(2)}, u32[]{:S(2)}) collective-permute-start(f32[64,512]{1,0:T(8,128)S(1)} %get-tuple-element.34), channel_id=1, source_target_pairs={{16,0},{32,16},{48,32},{64,48},{80,64},{96,80},{112,96},{128,112},... | collective-permute-start | bytes 393224 | tf_op jit(solution)/shard_map/ppermute | solution.py:30
  69.4 9.5 %collective-permute-done.2.below_ref = f32[64,512]{1,0:T(8,128)S(1)} collective-permute-done((f32[64,512]{1,0:T(8,128)S(1)}, f32[64,512]{1,0:T(8,128)S(1)}, u32[]{:S(2)}, u32[]{:S(2)}) %collective-permute-start.2) | collective-permute-done | bytes 131104 | tf_op jit(solution)/shard_map/ppermute | solution.py:30
  78.9 1.5 %collective-permute-done.3.above_ref = f32[64,512]{1,0:T(8,128)S(1)} collective-permute-done((f32[64,512]{1,0:T(8,128)S(1)}, f32[64,512]{1,0:T(8,128)S(1)}, u32[]{:S(2)}, u32[]{:S(2)}) %collective-permute-start.3) | collective-permute-done | bytes 131104 | tf_op jit(solution)/shard_map/ppermute | solution.py:30
  80.5 0.7 collective-permute-start.11
  81.2 6.2 %shard_map.71 = (f32[4,128,128]{2,1,0:T(8,128)}, f32[128,128]{1,0:T(8,128)}, f32[128,128]{1,0:T(8,128)}, f32[128,128]{1,0:T(8,128)}) custom-call(f32[64,3072]{1,0:T(8,128)} %copy-done.1, f32[64,3072]{1,0:T(8,128)} %collective-permute-done.7.refs_1_.yb_ref, f32[64,3072]{1,0:T(8,128)} %copy-done.8, f32[64,3072]{1,0:T(8,128)} %copy-done.10, ...), custom_call_target="tpu_custom_call" | custom-call | flops 10000000 | bytes 30000 | tf_op jit(solution)/shard_map/pallas_call | solution.py:298
  87.4 0.8 collective-permute-start.8
  88.2 3.1 %collective-permute-start.10 = (f32[128,128]{1,0:T(8,128)}, f32[128,128]{1,0:T(8,128)S(1)}, u32[]{:S(2)}, u32[]{:S(2)}) collective-permute-start(f32[128,128]{1,0:T(8,128)} %get-tuple-element.50), channel_id=1, source_target_pairs={{0,10},{1,11},{2,12},{3,13},{4,14},{5,15},{6,0},{7,1},{8,2},{9,3},... | collective-permute-start | bytes 196616 | tf_op jit(solution)/shard_map/ppermute | solution.py:24
  91.3 0.1 pad_add_fusion.place
  91.4 5.5 %shard_map.72 = f32[64,6144]{1,0:T(8,128)} custom-call(s32[512]{0:T(512)S(1)} %copy-done.4, s32[512]{0:T(512)S(1)} %copy-done.5, f32[6144,128]{1,0:T(8,128)S(1)} %get-tuple-element.45.rows.rows_ref, f32[64,512]{1,0:T(8,128)S(1)} %collective-permute-done.2.below_ref, f32[64,512]{1,0:T(8,128)S(1)} %collective-permute-done.3.above_ref), custom_call_target="tpu_custom_call" | custom-call | flops 10000000 | bytes 30000 | tf_op jit(solution)/shard_map/pallas_call | solution.py:382
  96.9 1.0 collective-permute-done.10.refs_2_
  97.9 0.7 shard_map.73.laid_ref
  98.6 6.0 %collective-permute-done.11.far_ref = f32[128,3072]{1,0:T(8,128)} collective-permute-done((f32[128,3072]{1,0:T(8,128)}, f32[128,3072]{1,0:T(8,128)}, u32[]{:S(2)}, u32[]{:S(2)}) %collective-permute-start.11) | collective-permute-done | bytes 1572896 | tf_op jit(solution)/shard_map/ppermute | solution.py:24
  104.6 2.6 %shard_map.74 = f32[32,32,128]{2,1,0:T(8,128)S(1)} custom-call(s32[3]{0:T(128)S(1)} %pad_add_fusion.place, f32[64,3072]{1,0:T(8,128)S(1)} %copy-done.2, f32[64,3072]{1,0:T(8,128)} %collective-permute-done.7.refs_1_.yb_ref, f32[128,3072]{1,0:T(8,128)} %collective-permute-done.11.far_ref, ...), custom_call_target="tpu_custom_call", output_to_operand_aliasing={{}: (4, {})} | custom-call | flops 2000000000 | bytes 6000000 | tf_op jit(solution)/shard_map/pallas_call | solution.py:323
  107.1 22.1 %all_to_all.5 = f32[32,32,128]{2,1,0:T(8,128)S(1)} all-to-all(f32[32,32,128]{2,1,0:T(8,128)S(1)} %shard_map.74), channel_id=1, replica_groups={{0,1,16,17,32,33,48,49,64,65,80,81,96,97,112,113,128,129,144,145,160,16..., dimensions={0} | all-to-all | bytes 1048576 | tf_op jit(solution)/shard_map/all_to_all | solution.py:398
  129.3 0.1 fusion.2
  129.4 0.7 copy.8
  (34 shorter events, 0.1 us)
Async XLA Ops:
  0.7 11.5 %copy-start.11 = (s32[3,12288]{1,0:T(4,128)S(1)}, s32[3,12288]{1,0:T(4,128)}, u32[]{:S(2)}) copy-start(s32[3,12288]{1,0:T(4,128)} %param.6) | copy-start | bytes 442372
  0.7 11.7 %copy-start = (f32[64,6144]{1,0:T(8,128)S(1)}, f32[64,6144]{1,0:T(8,128)}, u32[]{:S(2)}) copy-start(f32[64,6144]{1,0:T(8,128)} %refs_4_.3) | copy-start | bytes 4718596
  0.7 11.7 %copy-start.6 = (f32[12288]{0:T(1024)S(1)}, f32[12288]{0:T(1024)}, u32[]{:S(2)}) copy-start(f32[12288]{0:T(1024)} %refs_3_.3) | copy-start | bytes 147460
  2.3 32.2 %copy-start.8 = (f32[64,3072]{1,0:T(8,128)}, f32[64,3072]{1,0:T(8,128)S(1)}, u32[]{:S(2)}) copy-start(f32[64,3072]{1,0:T(8,128)S(1)} %get-tuple-element.61.refs_2_) | copy-start | bytes 2359300
  2.3 32.2 %collective-permute-start.1 = (f32[64,3072]{1,0:T(8,128)S(1)}, f32[64,3072]{1,0:T(8,128)S(1)}, u32[]{:S(2)}, u32[]{:S(2)}) collective-permute-start(f32[64,3072]{1,0:T(8,128)S(1)} %get-tuple-element.38), channel_id=1, source_target_pairs={{0,3},{1,2},{2,5},{3,4},{4,7},{5,6},{6,9},{7,8},{8,11},{9,10},{10,... | collective-permute-start | bytes 2359304 | tf_op jit(solution)/shard_map/ppermute | solution.py:24
  11.4 23.1 %collective-permute-start = (f32[64,3072]{1,0:T(8,128)S(1)}, f32[64,3072]{1,0:T(8,128)S(1)}, u32[]{:S(2)}, u32[]{:S(2)}) collective-permute-start(f32[64,3072]{1,0:T(8,128)S(1)} %get-tuple-element.61.refs_2_), channel_id=1, source_target_pairs={{0,2},{1,3},{2,4},{3,5},{4,6},{5,7},{6,8},{7,9},{8,10},{9,11},{10,... | collective-permute-start | bytes 2359304 | tf_op jit(solution)/shard_map/ppermute | solution.py:24
  34.6 21.1 %collective-permute-start.5 = (f32[64,3072]{1,0:T(8,128)S(1)}, f32[64,3072]{1,0:T(8,128)S(1)}, u32[]{:S(2)}, u32[]{:S(2)}) collective-permute-start(f32[64,3072]{1,0:T(8,128)S(1)} %get-tuple-element.38), channel_id=1, source_target_pairs={{0,1},{1,0},{2,3},{3,2},{4,5},{5,4},{6,7},{7,6},{8,9},{9,8},{10,11... | collective-permute-start | bytes 2359304 | tf_op jit(solution)/shard_map/ppermute | solution.py:34
  34.8 20.8 %copy-start.7 = (f32[128,3072]{1,0:T(8,128)}, f32[128,3072]{1,0:T(8,128)S(1)}, u32[]{:S(2)}) copy-start(f32[128,3072]{1,0:T(8,128)S(1)} %constant_dynamic-update-slice_fusion.refs_4_) | copy-start | bytes 4718596
  34.8 20.9 %collective-permute-start.4 = (f32[128,3072]{1,0:T(8,128)S(1)}, f32[128,3072]{1,0:T(8,128)S(1)}, u32[]{:S(2)}, u32[]{:S(2)}) collective-permute-start(f32[128,3072]{1,0:T(8,128)S(1)} %constant_dynamic-update-slice_fusion.refs_4_), channel_id=1, source_target_pairs={{0,2},{1,3},{2,4},{3,5},{4,6},{5,7},{6,8},{7,9},{8,10},{9,11},{10,... | collective-permute-start | bytes 4718600 | tf_op jit(solution)/shard_map/ppermute | solution.py:24
  36.5 24.0 %copy-start.4 = (s32[512]{0:T(512)S(1)}, s32[512]{0:T(512)}, u32[]{:S(2)}) copy-start(s32[512]{0:T(512)} %low_s.3) | copy-start | bytes 6148
  36.5 24.0 %copy-start.5 = (s32[512]{0:T(512)S(1)}, s32[512]{0:T(512)}, u32[]{:S(2)}) copy-start(s32[512]{0:T(512)} %up_s.3) | copy-start | bytes 6148
  55.7 6.8 %copy-start.1 = (f32[64,3072]{1,0:T(8,128)}, f32[64,3072]{1,0:T(8,128)S(1)}, u32[]{:S(2)}) copy-start(f32[64,3072]{1,0:T(8,128)S(1)} %get-tuple-element.32.refs_0_.ya_ref) | copy-start | bytes 2359300
  55.7 6.8 %copy-start.10 = (f32[64,3072]{1,0:T(8,128)}, f32[64,3072]{1,0:T(8,128)S(1)}, u32[]{:S(2)}) copy-start(f32[64,3072]{1,0:T(8,128)S(1)} %collective-permute-done.5.refs_3_) | copy-start | bytes 2359300
  55.7 6.7 %copy-start.9 = (f32[128,3072]{1,0:T(8,128)}, f32[128,3072]{1,0:T(8,128)S(1)}, u32[]{:S(2)}) copy-start(f32[128,3072]{1,0:T(8,128)S(1)} %collective-permute-done.4.refs_5_) | copy-start | bytes 4718596
  55.7 24.8 %collective-permute-start.6 = (f32[128,3072]{1,0:T(8,128)S(1)}, f32[128,3072]{1,0:T(8,128)}, u32[]{:S(2)}, u32[]{:S(2)}) collective-permute-start(f32[128,3072]{1,0:T(8,128)S(1)} %collective-permute-done.4.refs_5_), channel_id=1, source_target_pairs={{0,2},{1,3},{2,4},{3,5},{4,6},{5,7},{6,8},{7,9},{8,10},{9,11},{10,... | collective-permute-start | bytes 4718600 | tf_op jit(solution)/shard_map/ppermute | solution.py:24
  57.6 22.9 %collective-permute-start.7 = (f32[64,3072]{1,0:T(8,128)S(1)}, f32[64,3072]{1,0:T(8,128)}, u32[]{:S(2)}, u32[]{:S(2)}) collective-permute-start(f32[64,3072]{1,0:T(8,128)S(1)} %get-tuple-element.40), channel_id=1, source_target_pairs={{0,1},{1,0},{2,3},{3,2},{4,5},{5,4},{6,7},{7,6},{8,9},{9,8},{10,11... | collective-permute-start | bytes 2359304 | tf_op jit(solution)/shard_map/ppermute | solution.py:34
  62.5 16.5 %collective-permute-start.2 = (f32[64,512]{1,0:T(8,128)S(1)}, f32[64,512]{1,0:T(8,128)S(1)}, u32[]{:S(2)}, u32[]{:S(2)}) collective-permute-start(f32[64,512]{1,0:T(8,128)S(1)} %get-tuple-element.33), channel_id=1, source_target_pairs={{0,16},{16,32},{32,48},{48,64},{64,80},{80,96},{96,112},{112,128},... | collective-permute-start | bytes 393224 | tf_op jit(solution)/shard_map/ppermute | solution.py:30
  67.5 13.0 %collective-permute-start.3 = (f32[64,512]{1,0:T(8,128)S(1)}, f32[64,512]{1,0:T(8,128)S(1)}, u32[]{:S(2)}, u32[]{:S(2)}) collective-permute-start(f32[64,512]{1,0:T(8,128)S(1)} %get-tuple-element.34), channel_id=1, source_target_pairs={{16,0},{32,16},{48,32},{64,48},{80,64},{96,80},{112,96},{128,112},... | collective-permute-start | bytes 393224 | tf_op jit(solution)/shard_map/ppermute | solution.py:30
  80.5 24.1 %collective-permute-start.11 = (f32[128,3072]{1,0:T(8,128)}, f32[128,3072]{1,0:T(8,128)}, u32[]{:S(2)}, u32[]{:S(2)}) collective-permute-start(f32[128,3072]{1,0:T(8,128)} %collective-permute-done.6.refs_6_), channel_id=1, source_target_pairs={{0,2},{1,3},{2,4},{3,5},{4,6},{5,7},{6,8},{7,9},{8,10},{9,11},{10,... | collective-permute-start | bytes 4718600 | tf_op jit(solution)/shard_map/ppermute | solution.py:24
  87.4 9.5 %collective-permute-start.8 = (f32[128,128]{1,0:T(8,128)}, f32[128,128]{1,0:T(8,128)S(1)}, u32[]{:S(2)}, u32[]{:S(2)}) collective-permute-start(f32[128,128]{1,0:T(8,128)} %get-tuple-element.48), channel_id=1, source_target_pairs={{0,14},{1,15},{2,0},{3,1},{4,2},{5,3},{6,4},{7,5},{8,6},{9,7},{10,... | collective-permute-start | bytes 196616 | tf_op jit(solution)/shard_map/ppermute | solution.py:24
  88.2 8.7 %collective-permute-start.9 = (f32[128,128]{1,0:T(8,128)}, f32[128,128]{1,0:T(8,128)S(1)}, u32[]{:S(2)}, u32[]{:S(2)}) collective-permute-start(f32[128,128]{1,0:T(8,128)} %get-tuple-element.49), channel_id=1, source_target_pairs={{0,12},{1,13},{2,14},{3,15},{4,0},{5,1},{6,2},{7,3},{8,4},{9,5},{1... | collective-permute-start | bytes 196616 | tf_op jit(solution)/shard_map/ppermute | solution.py:24
  88.2 9.6 %collective-permute-start.10 = (f32[128,128]{1,0:T(8,128)}, f32[128,128]{1,0:T(8,128)S(1)}, u32[]{:S(2)}, u32[]{:S(2)}) collective-permute-start(f32[128,128]{1,0:T(8,128)} %get-tuple-element.50), channel_id=1, source_target_pairs={{0,10},{1,11},{2,12},{3,13},{4,14},{5,15},{6,0},{7,1},{8,2},{9,3},... | collective-permute-start | bytes 196616 | tf_op jit(solution)/shard_map/ppermute | solution.py:24
  91.4 6.5 %copy-start.3 = (f32[4,128,128]{2,1,0:T(8,128)S(1)}, f32[4,128,128]{2,1,0:T(8,128)}, u32[]{:S(2)}) copy-start(f32[4,128,128]{2,1,0:T(8,128)} %get-tuple-element.52.near_ref) | copy-start | bytes 786436
  91.4 13.2 %copy-start.2 = (f32[64,3072]{1,0:T(8,128)S(1)}, f32[64,3072]{1,0:T(8,128)}, u32[]{:S(2)}) copy-start(f32[64,3072]{1,0:T(8,128)} %copy-done.1) | copy-start | bytes 2359300

commit v12 on v11

--- a/solution.py
+++ b/solution.py
@@ -271,11 +271,12 @@
     z, h, way = place[0], place[1], place[2]
     rings, low, snaps = out_ref.shape[0] // 4, out_ref.shape[1], out_ref.shape[2] // 2
     at = lax.rem(z - way * distance + rings, rings)
+    turned = value.T
     for side in range(2):
         row = 2 * at + (h if side == 0 else 1 - h)
-        upper, lower = value[side * snaps:side * snaps + low], value[side * snaps + low:(side + 1) * snaps]
-        out_ref[2 * row + h] = jnp.concatenate([upper[:, :snaps], lower[:, :snaps]], axis=1)
-        out_ref[2 * row + (1 - h)] = jnp.concatenate([upper[:, snaps:], lower[:, snaps:]], axis=1)
+        for part in range(2):
+            block = turned[part * snaps:(part + 1) * snaps, side * snaps:(side + 1) * snaps]
+            out_ref[2 * row + (h if part == 0 else 1 - h)] = jnp.concatenate([block[:low], block[low:]], axis=1)
 
 
 def lay_kernel(place, near_ref, *refs):
@@ -397,7 +398,7 @@
     planes = [[m * blocks + 2 * r + c for m in range(parts) for c in range(2)] for r in range(rings)]
     tile = jnp.sum(lax.all_to_all(tiles, ("mesh", "snap"), 0, 0, axis_index_groups=planes, tiled=True), axis=0)
     column = jnp.concatenate([tile[:, :snaps], tile[:, snaps:]], axis=0)
-    return weighted, column.T * (1.0 / float(parts * nodes))
+    return weighted, column * (1.0 / float(parts * nodes))
 
 
 def solution(mesh):

time: 130 us -> 130 us (level)
  no operation moved by 1% of the time
where the time goes in v12:
time: 130 us
  Pallas kernels  58.4 us (45%)
  starting transfers between devices  28 us (22%)
  blocking collectives  22.1 us (17%)
  waiting for transfers between devices  17.8 us (14%)
  local copies, waits for them, and re-layouts  1.96 us (2%)
    pallas_call x2, Pallas kernels, apply_call(): pl.pallas_call(functools.partial(apply_kernel, first, last, start, count,...  41.3 us
    all_to_all x1, blocking collectives, on_device(): lax.all_to_all(tiles, ('mesh', 'snap'), 0, 0, axis_index_groups=planes, t...  22.1 us
    ppermute x8, starting transfers between devices, ring_hop(): return lax.ppermute(value, ('mesh', 'snap'), pairs)  18 us
    ppermute x2, waiting for transfers between devices, passed_along(): lax.ppermute(value, axis, [(source, source + steps) for source in range(l...  11 us
    ppermute x2, starting transfers between devices, passed_along(): lax.ppermute(value, axis, [(source, source + steps) for source in range(l...  6.96 us
    ppermute x8, waiting for transfers between devices, ring_hop(): return lax.ppermute(value, ('mesh', 'snap'), pairs)  6.79 us
    pallas_call x1, Pallas kernels, near_call(): pl.pallas_call(near_kernel, out_shape=[jax.ShapeDtypeStruct((4, 2 * snaps...  6.17 us
    pallas_call x1, Pallas kernels, on_device(): pl.pallas_call(assemble_kernel, out_shape=jax.ShapeDtypeStruct((snaps, no...  5.46 us
  transfers between devices with their start and end apart: 12, of which 4 were waited for; matrix products, arithmetic and copies ran while one was open for 0% of the time, Pallas kernels for 43%

profile of v12, /device:TPU:1, one launch (start us, length us, event | category | flops | bytes accessed | tf_op | source)
XLA Modules:
  0.0 130.1 jit_solution(3167429246477266940)
XLA Ops:
  0.7 1.6 %constant_dynamic-slice_fusion = (f32[64,3072]{1,0:T(8,128)S(1)}, f32[64,3072]{1,0:T(8,128)S(1)}) fusion(f32[64,6144]{1,0:T(8,128)} %refs_4_.3, s32[]{:T(128)S(6)} %select_n.27, s32[]{:T(128)S(6)} %select_n.26), kind=kLoop, calls=%fused_computation.5 | loop fusion | bytes 3145736 | tf_op jit(solution)/shard_map/dynamic_slice | solution.py:347
  2.3 9.1 %collective-permute-start.1 = (f32[64,3072]{1,0:T(8,128)S(1)}, f32[64,3072]{1,0:T(8,128)S(1)}, u32[]{:S(2)}, u32[]{:S(2)}) collective-permute-start(f32[64,3072]{1,0:T(8,128)S(1)} %get-tuple-element.38), channel_id=1, source_target_pairs={{0,3},{1,2},{2,5},{3,4},{4,7},{5,6},{6,9},{7,8},{8,11},{9,10},{10,... | collective-permute-start | bytes 2359304 | tf_op jit(solution)/shard_map/ppermute | solution.py:24
  11.4 0.7 collective-permute-start
  12.2 0.1 and_add_fusion
  12.2 0.1 fusion
  12.4 22.1 %shard_map.68.refs_5_ = f32[6144,128]{1,0:T(8,128)S(1)} custom-call(s32[12288]{0:T(1024)S(1)} %bitcast.10, s32[12288]{0:T(1024)S(1)} %bitcast.8, s32[12288]{0:T(1024)S(1)} %bitcast.6, f32[12288]{0:T(1024)S(1)} %copy-done.6, f32[64,6144]{1,0:T(8,128)S(1)} %copy-done), custom_call_target="tpu_custom_call" | custom-call | flops 20000000000 | bytes 60000000 | tf_op jit(solution)/shard_map/pallas_call | solution.py:215
  34.6 0.1 collective-permute-start.5
  34.7 0.1 constant_dynamic-update-slice_fusion.1
  34.8 0.1 constant_dynamic-update-slice_fusion.refs_4_
  34.8 0.0 copy-start.7
  34.8 1.7 %collective-permute-start.4 = (f32[128,3072]{1,0:T(8,128)S(1)}, f32[128,3072]{1,0:T(8,128)S(1)}, u32[]{:S(2)}, u32[]{:S(2)}) collective-permute-start(f32[128,3072]{1,0:T(8,128)S(1)} %constant_dynamic-update-slice_fusion.refs_4_), channel_id=1, source_target_pairs={{0,2},{1,3},{2,4},{3,5},{4,6},{5,7},{6,8},{7,9},{8,10},{9,11},{10,... | collective-permute-start | bytes 4718600 | tf_op jit(solution)/shard_map/ppermute | solution.py:24
  36.5 19.1 %shard_map.69 = (f32[6144,128]{1,0:T(8,128)S(1)}, f32[64,3072]{1,0:T(8,128)S(1)}, f32[64,3072]{1,0:T(8,128)S(1)}) custom-call(s32[12288]{0:T(1024)S(1)} %bitcast.11, s32[12288]{0:T(1024)S(1)} %bitcast.9, s32[12288]{0:T(1024)S(1)} %bitcast.7, f32[12288]{0:T(1024)S(1)} %copy-done.6, f32[64,6144]{1,0:T(8,128)S(1)} %copy-done, ...), custom_call_target="tpu_custom_call" | custom-call | flops 20000000000 | bytes 60000000 | tf_op jit(solution)/shard_map/pallas_call | solution.py:215
  55.7 1.8 %collective-permute-start.6 = (f32[128,3072]{1,0:T(8,128)S(1)}, f32[128,3072]{1,0:T(8,128)}, u32[]{:S(2)}, u32[]{:S(2)}) collective-permute-start(f32[128,3072]{1,0:T(8,128)S(1)} %collective-permute-done.4.refs_5_), channel_id=1, source_target_pairs={{0,2},{1,3},{2,4},{3,5},{4,6},{5,7},{6,8},{7,9},{8,10},{9,11},{10,... | collective-permute-start | bytes 4718600 | tf_op jit(solution)/shard_map/ppermute | solution.py:24
  57.6 2.9 %collective-permute-start.7 = (f32[64,3072]{1,0:T(8,128)S(1)}, f32[64,3072]{1,0:T(8,128)}, u32[]{:S(2)}, u32[]{:S(2)}) collective-permute-start(f32[64,3072]{1,0:T(8,128)S(1)} %get-tuple-element.40), channel_id=1, source_target_pairs={{0,1},{1,0},{2,3},{3,2},{4,5},{5,4},{6,7},{7,6},{8,9},{9,8},{10,11... | collective-permute-start | bytes 2359304 | tf_op jit(solution)/shard_map/ppermute | solution.py:34
  60.5 2.0 %shard_map.70 = (f32[64,512]{1,0:T(8,128)S(1)}, f32[64,512]{1,0:T(8,128)S(1)}) custom-call(s32[512]{0:T(512)S(1)} %copy-done.4, s32[512]{0:T(512)S(1)} %copy-done.5, f32[6144,128]{1,0:T(8,128)S(1)} %get-tuple-element.45.rows.rows_ref), custom_call_target="tpu_custom_call" | custom-call | flops 10000000 | bytes 30000 | tf_op jit(solution)/shard_map/pallas_call | solution.py:367
  62.5 5.0 %collective-permute-start.2 = (f32[64,512]{1,0:T(8,128)S(1)}, f32[64,512]{1,0:T(8,128)S(1)}, u32[]{:S(2)}, u32[]{:S(2)}) collective-permute-start(f32[64,512]{1,0:T(8,128)S(1)} %get-tuple-element.33), channel_id=1, source_target_pairs={{0,16},{16,32},{32,48},{48,64},{64,80},{80,96},{96,112},{112,128},... | collective-permute-start | bytes 393224 | tf_op jit(solution)/shard_map/ppermute | solution.py:30
  67.5 1.9 %collective-permute-start.3 = (f32[64,512]{1,0:T(8,128)S(1)}, f32[64,512]{1,0:T(8,128)S(1)}, u32[]{:S(2)}, u32[]{:S(2)}) collective-permute-start(f32[64,512]{1,0:T(8,128)S(1)} %get-tuple-element.34), channel_id=1, source_target_pairs={{16,0},{32,16},{48,32},{64,48},{80,64},{96,80},{112,96},{128,112},... | collective-permute-start | bytes 393224 | tf_op jit(solution)/shard_map/ppermute | solution.py:30
  69.4 9.5 %collective-permute-done.2.below_ref = f32[64,512]{1,0:T(8,128)S(1)} collective-permute-done((f32[64,512]{1,0:T(8,128)S(1)}, f32[64,512]{1,0:T(8,128)S(1)}, u32[]{:S(2)}, u32[]{:S(2)}) %collective-permute-start.2) | collective-permute-done | bytes 131104 | tf_op jit(solution)/shard_map/ppermute | solution.py:30
  78.9 1.5 %collective-permute-done.3.above_ref = f32[64,512]{1,0:T(8,128)S(1)} collective-permute-done((f32[64,512]{1,0:T(8,128)S(1)}, f32[64,512]{1,0:T(8,128)S(1)}, u32[]{:S(2)}, u32[]{:S(2)}) %collective-permute-start.3) | collective-permute-done | bytes 131104 | tf_op jit(solution)/shard_map/ppermute | solution.py:30
  80.5 0.7 collective-permute-start.11
  81.2 6.2 %shard_map.71 = (f32[4,128,128]{2,1,0:T(8,128)}, f32[128,128]{1,0:T(8,128)}, f32[128,128]{1,0:T(8,128)}, f32[128,128]{1,0:T(8,128)}) custom-call(f32[64,3072]{1,0:T(8,128)} %copy-done.1, f32[64,3072]{1,0:T(8,128)} %collective-permute-done.7.refs_1_.yb_ref, f32[64,3072]{1,0:T(8,128)} %copy-done.8, f32[64,3072]{1,0:T(8,128)} %copy-done.10, ...), custom_call_target="tpu_custom_call" | custom-call | flops 10000000 | bytes 30000 | tf_op jit(solution)/shard_map/pallas_call | solution.py:299
  87.4 0.8 collective-permute-start.8
  88.2 3.1 %collective-permute-start.10 = (f32[128,128]{1,0:T(8,128)}, f32[128,128]{1,0:T(8,128)S(1)}, u32[]{:S(2)}, u32[]{:S(2)}) collective-permute-start(f32[128,128]{1,0:T(8,128)} %get-tuple-element.50), channel_id=1, source_target_pairs={{0,10},{1,11},{2,12},{3,13},{4,14},{5,15},{6,0},{7,1},{8,2},{9,3},... | collective-permute-start | bytes 196616 | tf_op jit(solution)/shard_map/ppermute | solution.py:24
  91.3 0.1 pad_add_fusion.place
  91.4 5.5 %shard_map.72 = f32[64,6144]{1,0:T(8,128)} custom-call(s32[512]{0:T(512)S(1)} %copy-done.4, s32[512]{0:T(512)S(1)} %copy-done.5, f32[6144,128]{1,0:T(8,128)S(1)} %get-tuple-element.45.rows.rows_ref, f32[64,512]{1,0:T(8,128)S(1)} %collective-permute-done.2.below_ref, f32[64,512]{1,0:T(8,128)S(1)} %collective-permute-done.3.above_ref), custom_call_target="tpu_custom_call" | custom-call | flops 10000000 | bytes 30000 | tf_op jit(solution)/shard_map/pallas_call | solution.py:383
  96.9 1.0 collective-permute-done.10.refs_2_
  97.9 0.9 shard_map.73.laid_ref
  98.8 5.8 %collective-permute-done.11.far_ref = f32[128,3072]{1,0:T(8,128)} collective-permute-done((f32[128,3072]{1,0:T(8,128)}, f32[128,3072]{1,0:T(8,128)}, u32[]{:S(2)}, u32[]{:S(2)}) %collective-permute-start.11) | collective-permute-done | bytes 1572896 | tf_op jit(solution)/shard_map/ppermute | solution.py:24
  104.6 2.6 %shard_map.74 = f32[32,32,128]{2,1,0:T(8,128)S(1)} custom-call(s32[3]{0:T(128)S(1)} %pad_add_fusion.place, f32[64,3072]{1,0:T(8,128)S(1)} %copy-done.2, f32[64,3072]{1,0:T(8,128)} %collective-permute-done.7.refs_1_.yb_ref, f32[128,3072]{1,0:T(8,128)} %collective-permute-done.11.far_ref, ...), custom_call_target="tpu_custom_call", output_to_operand_aliasing={{}: (4, {})} | custom-call | flops 2000000000 | bytes 6000000 | tf_op jit(solution)/shard_map/pallas_call | solution.py:324
  107.2 22.1 %all_to_all.5 = f32[32,32,128]{2,1,0:T(8,128)S(1)} all-to-all(f32[32,32,128]{2,1,0:T(8,128)S(1)} %shard_map.74), channel_id=1, replica_groups={{0,1,16,17,32,33,48,49,64,65,80,81,96,97,112,113,128,129,144,145,160,16..., dimensions={0} | all-to-all | bytes 1048576 | tf_op jit(solution)/shard_map/all_to_all | solution.py:399
  129.4 0.1 fusion.1
  129.4 0.6 maximum_multiply_fusion
  (33 shorter events, 0.1 us)
Async XLA Ops:
  0.7 11.5 %copy-start.11 = (s32[3,12288]{1,0:T(4,128)S(1)}, s32[3,12288]{1,0:T(4,128)}, u32[]{:S(2)}) copy-start(s32[3,12288]{1,0:T(4,128)} %param.6) | copy-start | bytes 442372
  0.7 11.7 %copy-start = (f32[64,6144]{1,0:T(8,128)S(1)}, f32[64,6144]{1,0:T(8,128)}, u32[]{:S(2)}) copy-start(f32[64,6144]{1,0:T(8,128)} %refs_4_.3) | copy-start | bytes 4718596
  0.7 11.7 %copy-start.6 = (f32[12288]{0:T(1024)S(1)}, f32[12288]{0:T(1024)}, u32[]{:S(2)}) copy-start(f32[12288]{0:T(1024)} %refs_3_.3) | copy-start | bytes 147460
  2.3 32.2 %copy-start.8 = (f32[64,3072]{1,0:T(8,128)}, f32[64,3072]{1,0:T(8,128)S(1)}, u32[]{:S(2)}) copy-start(f32[64,3072]{1,0:T(8,128)S(1)} %get-tuple-element.59.refs_2_) | copy-start | bytes 2359300
  2.3 32.2 %collective-permute-start.1 = (f32[64,3072]{1,0:T(8,128)S(1)}, f32[64,3072]{1,0:T(8,128)S(1)}, u32[]{:S(2)}, u32[]{:S(2)}) collective-permute-start(f32[64,3072]{1,0:T(8,128)S(1)} %get-tuple-element.38), channel_id=1, source_target_pairs={{0,3},{1,2},{2,5},{3,4},{4,7},{5,6},{6,9},{7,8},{8,11},{9,10},{10,... | collective-permute-start | bytes 2359304 | tf_op jit(solution)/shard_map/ppermute | solution.py:24
  11.4 23.1 %collective-permute-start = (f32[64,3072]{1,0:T(8,128)S(1)}, f32[64,3072]{1,0:T(8,128)S(1)}, u32[]{:S(2)}, u32[]{:S(2)}) collective-permute-start(f32[64,3072]{1,0:T(8,128)S(1)} %get-tuple-element.59.refs_2_), channel_id=1, source_target_pairs={{0,2},{1,3},{2,4},{3,5},{4,6},{5,7},{6,8},{7,9},{8,10},{9,11},{10,... | collective-permute-start | bytes 2359304 | tf_op jit(solution)/shard_map/ppermute | solution.py:24
  34.6 21.1 %collective-permute-start.5 = (f32[64,3072]{1,0:T(8,128)S(1)}, f32[64,3072]{1,0:T(8,128)S(1)}, u32[]{:S(2)}, u32[]{:S(2)}) collective-permute-start(f32[64,3072]{1,0:T(8,128)S(1)} %get-tuple-element.38), channel_id=1, source_target_pairs={{0,1},{1,0},{2,3},{3,2},{4,5},{5,4},{6,7},{7,6},{8,9},{9,8},{10,11... | collective-permute-start | bytes 2359304 | tf_op jit(solution)/shard_map/ppermute | solution.py:34
  34.8 20.8 %copy-start.7 = (f32[128,3072]{1,0:T(8,128)}, f32[128,3072]{1,0:T(8,128)S(1)}, u32[]{:S(2)}) copy-start(f32[128,3072]{1,0:T(8,128)S(1)} %constant_dynamic-update-slice_fusion.refs_4_) | copy-start | bytes 4718596
  34.8 20.9 %collective-permute-start.4 = (f32[128,3072]{1,0:T(8,128)S(1)}, f32[128,3072]{1,0:T(8,128)S(1)}, u32[]{:S(2)}, u32[]{:S(2)}) collective-permute-start(f32[128,3072]{1,0:T(8,128)S(1)} %constant_dynamic-update-slice_fusion.refs_4_), channel_id=1, source_target_pairs={{0,2},{1,3},{2,4},{3,5},{4,6},{5,7},{6,8},{7,9},{8,10},{9,11},{10,... | collective-permute-start | bytes 4718600 | tf_op jit(solution)/shard_map/ppermute | solution.py:24
  36.5 24.0 %copy-start.4 = (s32[512]{0:T(512)S(1)}, s32[512]{0:T(512)}, u32[]{:S(2)}) copy-start(s32[512]{0:T(512)} %low_s.3) | copy-start | bytes 6148
  36.5 24.0 %copy-start.5 = (s32[512]{0:T(512)S(1)}, s32[512]{0:T(512)}, u32[]{:S(2)}) copy-start(s32[512]{0:T(512)} %up_s.3) | copy-start | bytes 6148
  55.7 6.8 %copy-start.1 = (f32[64,3072]{1,0:T(8,128)}, f32[64,3072]{1,0:T(8,128)S(1)}, u32[]{:S(2)}) copy-start(f32[64,3072]{1,0:T(8,128)S(1)} %get-tuple-element.32.refs_0_.ya_ref) | copy-start | bytes 2359300
  55.7 6.8 %copy-start.10 = (f32[64,3072]{1,0:T(8,128)}, f32[64,3072]{1,0:T(8,128)S(1)}, u32[]{:S(2)}) copy-start(f32[64,3072]{1,0:T(8,128)S(1)} %collective-permute-done.5.refs_3_) | copy-start | bytes 2359300
  55.7 6.7 %copy-start.9 = (f32[128,3072]{1,0:T(8,128)}, f32[128,3072]{1,0:T(8,128)S(1)}, u32[]{:S(2)}) copy-start(f32[128,3072]{1,0:T(8,128)S(1)} %collective-permute-done.4.refs_5_) | copy-start | bytes 4718596
  55.7 24.8 %collective-permute-start.6 = (f32[128,3072]{1,0:T(8,128)S(1)}, f32[128,3072]{1,0:T(8,128)}, u32[]{:S(2)}, u32[]{:S(2)}) collective-permute-start(f32[128,3072]{1,0:T(8,128)S(1)} %collective-permute-done.4.refs_5_), channel_id=1, source_target_pairs={{0,2},{1,3},{2,4},{3,5},{4,6},{5,7},{6,8},{7,9},{8,10},{9,11},{10,... | collective-permute-start | bytes 4718600 | tf_op jit(solution)/shard_map/ppermute | solution.py:24
  57.6 22.9 %collective-permute-start.7 = (f32[64,3072]{1,0:T(8,128)S(1)}, f32[64,3072]{1,0:T(8,128)}, u32[]{:S(2)}, u32[]{:S(2)}) collective-permute-start(f32[64,3072]{1,0:T(8,128)S(1)} %get-tuple-element.40), channel_id=1, source_target_pairs={{0,1},{1,0},{2,3},{3,2},{4,5},{5,4},{6,7},{7,6},{8,9},{9,8},{10,11... | collective-permute-start | bytes 2359304 | tf_op jit(solution)/shard_map/ppermute | solution.py:34
  62.5 16.5 %collective-permute-start.2 = (f32[64,512]{1,0:T(8,128)S(1)}, f32[64,512]{1,0:T(8,128)S(1)}, u32[]{:S(2)}, u32[]{:S(2)}) collective-permute-start(f32[64,512]{1,0:T(8,128)S(1)} %get-tuple-element.33), channel_id=1, source_target_pairs={{0,16},{16,32},{32,48},{48,64},{64,80},{80,96},{96,112},{112,128},... | collective-permute-start | bytes 393224 | tf_op jit(solution)/shard_map/ppermute | solution.py:30
  67.5 13.0 %collective-permute-start.3 = (f32[64,512]{1,0:T(8,128)S(1)}, f32[64,512]{1,0:T(8,128)S(1)}, u32[]{:S(2)}, u32[]{:S(2)}) collective-permute-start(f32[64,512]{1,0:T(8,128)S(1)} %get-tuple-element.34), channel_id=1, source_target_pairs={{16,0},{32,16},{48,32},{64,48},{80,64},{96,80},{112,96},{128,112},... | collective-permute-start | bytes 393224 | tf_op jit(solution)/shard_map/ppermute | solution.py:30
  80.5 24.1 %collective-permute-start.11 = (f32[128,3072]{1,0:T(8,128)}, f32[128,3072]{1,0:T(8,128)}, u32[]{:S(2)}, u32[]{:S(2)}) collective-permute-start(f32[128,3072]{1,0:T(8,128)} %collective-permute-done.6.refs_6_), channel_id=1, source_target_pairs={{0,2},{1,3},{2,4},{3,5},{4,6},{5,7},{6,8},{7,9},{8,10},{9,11},{10,... | collective-permute-start | bytes 4718600 | tf_op jit(solution)/shard_map/ppermute | solution.py:24
  87.4 9.5 %collective-permute-start.8 = (f32[128,128]{1,0:T(8,128)}, f32[128,128]{1,0:T(8,128)S(1)}, u32[]{:S(2)}, u32[]{:S(2)}) collective-permute-start(f32[128,128]{1,0:T(8,128)} %get-tuple-element.48), channel_id=1, source_target_pairs={{0,14},{1,15},{2,0},{3,1},{4,2},{5,3},{6,4},{7,5},{8,6},{9,7},{10,... | collective-permute-start | bytes 196616 | tf_op jit(solution)/shard_map/ppermute | solution.py:24
  88.2 8.7 %collective-permute-start.9 = (f32[128,128]{1,0:T(8,128)}, f32[128,128]{1,0:T(8,128)S(1)}, u32[]{:S(2)}, u32[]{:S(2)}) collective-permute-start(f32[128,128]{1,0:T(8,128)} %get-tuple-element.49), channel_id=1, source_target_pairs={{0,12},{1,13},{2,14},{3,15},{4,0},{5,1},{6,2},{7,3},{8,4},{9,5},{1... | collective-permute-start | bytes 196616 | tf_op jit(solution)/shard_map/ppermute | solution.py:24
  88.2 9.6 %collective-permute-start.10 = (f32[128,128]{1,0:T(8,128)}, f32[128,128]{1,0:T(8,128)S(1)}, u32[]{:S(2)}, u32[]{:S(2)}) collective-permute-start(f32[128,128]{1,0:T(8,128)} %get-tuple-element.50), channel_id=1, source_target_pairs={{0,10},{1,11},{2,12},{3,13},{4,14},{5,15},{6,0},{7,1},{8,2},{9,3},... | collective-permute-start | bytes 196616 | tf_op jit(solution)/shard_map/ppermute | solution.py:24
  91.4 6.5 %copy-start.3 = (f32[4,128,128]{2,1,0:T(8,128)S(1)}, f32[4,128,128]{2,1,0:T(8,128)}, u32[]{:S(2)}) copy-start(f32[4,128,128]{2,1,0:T(8,128)} %get-tuple-element.52.near_ref) | copy-start | bytes 786436
  91.4 13.2 %copy-start.2 = (f32[64,3072]{1,0:T(8,128)S(1)}, f32[64,3072]{1,0:T(8,128)}, u32[]{:S(2)}) copy-start(f32[64,3072]{1,0:T(8,128)} %copy-done.1) | copy-start | bytes 2359300
